TPU v7x, 32 devices: a whole 2x2x4 slice. The times are simulated.
32 devices in a mesh: seq: 8 (over y, x, core), mp: 4 (over z).
Axes of the slice: x: 2, y: 2, z: 4, core: 2. Of those that a mesh axis runs over, the one named last changes fastest.
Arguments:
- tokens: bfloat16 [2, 4096, 1024], P(None, 'seq'), may hold values from -6 to 6
- cotangent: bfloat16 [2, 4096, 1024], P(None, 'seq'), may hold values from -6 to 6
- w_qkv: float32 [3, 1024, 1024], P(None, 'seq', 'mp'), may hold values from -0.1875 to 0.1875
- w_out: float32 [1024, 1024], P('mp', 'seq'), may hold values from -3 to 3
- w_up: float32 [1024, 4096], P('seq', 'mp'), may hold values from -0.1875 to 0.1875
- w_down: float32 [4096, 1024], P('mp', 'seq'), may hold values from -0.09375 to 0.09375
- norm_gains: float32 [2, 1024], P(None, ('seq', 'mp'))
- ssm_param: float32 [2, 16, 1024], P(None, None, ('seq', 'mp'))
- first_qkv: float32 [3, 1024, 1024], P(None, 'seq', 'mp'), may hold values from -32 to 32
- second_qkv: float32 [3, 1024, 1024], P(None, 'seq', 'mp'), may hold values from 2.048 to 8.192
- first_out: float32 [1024, 1024], P('mp', 'seq'), may hold values from -4 to 4
- second_out: float32 [1024, 1024], P('mp', 'seq'), may hold values from 0.032 to 0.128
- first_up: float32 [1024, 4096], P('seq', 'mp'), may hold values from -16 to 16
- second_up: float32 [1024, 4096], P('seq', 'mp'), may hold values from 0.73728 to 2.94912
- first_down: float32 [4096, 1024], P('mp', 'seq'), may hold values from -32 to 32
- second_down: float32 [4096, 1024], P('mp', 'seq'), may hold values from 2.94912 to 11.79648
- first_gain: float32 [2, 1024], P(None, ('seq', 'mp')), may hold values from -64 to 64
- second_gain: float32 [2, 1024], P(None, ('seq', 'mp')), may hold values from 8.192 to 32.768
- first_ssm: float32 [2, 16, 1024], P(None, None, ('seq', 'mp')), may hold values from -32 to 32
- second_ssm: float32 [2, 16, 1024], P(None, None, ('seq', 'mp')), may hold values from 2.048 to 8.192
Outputs:
- layer_out: bfloat16 [2, 4096, 1024], P(None, 'seq')
- input_grad: float32 [2, 4096, 1024], P(None, 'seq')
- new_qkv: float32 [3, 1024, 1024], P(None, 'seq', 'mp')
- next_first_qkv: float32 [3, 1024, 1024], P(None, 'seq', 'mp')
- next_second_qkv: float32 [3, 1024, 1024], P(None, 'seq', 'mp')
- new_out: float32 [1024, 1024], P('mp', 'seq')
- next_first_out: float32 [1024, 1024], P('mp', 'seq')
- next_second_out: float32 [1024, 1024], P('mp', 'seq')
- new_up: float32 [1024, 4096], P('seq', 'mp')
- next_first_up: float32 [1024, 4096], P('seq', 'mp')
- next_second_up: float32 [1024, 4096], P('seq', 'mp')
- new_down: float32 [4096, 1024], P('mp', 'seq')
- next_first_down: float32 [4096, 1024], P('mp', 'seq')
- next_second_down: float32 [4096, 1024], P('mp', 'seq')
- new_gains: float32 [2, 1024], P(None, ('seq', 'mp'))
- next_first_gain: float32 [2, 1024], P(None, ('seq', 'mp'))
- next_second_gain: float32 [1024], P(('seq', 'mp'))
- next_second_gain_two: float32 [1024], P(('seq', 'mp'))
- new_ssm: float32 [2, 16, 1024], P(None, None, ('seq', 'mp'))
- next_first_ssm: float32 [2, 16, 1024], P(None, None, ('seq', 'mp'))
- next_second_ssm: float32 [2, 16, 1024], P(None, None, ('seq', 'mp'))
- lamb_norms: float32 [2, 10], replicated
All inputs are finite; a program needn't handle non-finite values.
Results may differ from a plain program's by a relative error of at most 0.035.
Values may be sent and summed in bfloat16 or wider, within the bound.
No kernel may reach another device: no remote copies, remote signals or barrier semaphores. Data moves between devices by JAX's collectives and lax.ppermute only.
A program may use at most 128 MiB of HBM per device.

v0:
```python
import functools
import math

import jax
import jax.numpy as jnp
from jax import lax
from jax.experimental import pallas as pl
from jax.experimental.pallas import tpu as pltpu
from jax.sharding import Mesh
from jax.sharding import PartitionSpec as P

HD = 128
HEADS = 8
BLK = 512
STEP = 10
SEQS = 2
LANES = 128
SUBS = 8
GROUP = 8

norm_eps = 1e-05
beta_first = 0.9
beta_second = 0.999
lamb_eps = 1e-06
weight_decay = 0.01
learn_rate = 0.5
score_scale = HD ** (-0.5)

f32 = jnp.float32
bf16 = jnp.bfloat16
VMEM_BYTES = 56 * 1024 * 1024

ALL = ("sh", "sl", "mb", "mq", "ml")
MODEL = ("mb", "mq", "ml")
COLS = ("mb", "mq")
TEAM = ("sl", "ml")


def dot(left, right):
    return lax.dot_general(left, right, (((1,), (0,)), ((), ())), preferred_element_type=f32)


def dot_t(left, right):
    return lax.dot_general(left, right, (((1,), (1,)), ((), ())), preferred_element_type=f32)


def normalise(values):
    centred = values - jnp.mean(values, axis=-1, keepdims=True)
    inverse = lax.rsqrt(jnp.mean(centred * centred, axis=-1, keepdims=True) + norm_eps)
    return centred * inverse, inverse


def normalise_back(unit, inverse, grad_unit):
    mean_one = jnp.mean(grad_unit, axis=-1, keepdims=True)
    mean_two = jnp.mean(grad_unit * unit, axis=-1, keepdims=True)
    return inverse * (grad_unit - mean_one - unit * mean_two)


def sub_index():
    return lax.broadcasted_iota(jnp.int32, (SUBS, LANES), 0)


def spread(row):
    return jnp.broadcast_to(row, (SUBS, LANES))


def lane_tile(index):
    return slice(index * LANES, (index + 1) * LANES)


def no_state(tiles):
    rows = tiles[0, :SUBS, :]
    return rows - rows


def in_steps(steps, tile, rows):
    span = rows.shape[0] // SUBS

    def move(i, unused):
        steps[tile, pl.ds(pl.multiple_of(i * SUBS, SUBS), SUBS), :] = rows[
            pl.ds(i, SUBS, stride=span), :
        ]
        return unused

    lax.fori_loop(0, span, move, 0, unroll=8)


def from_steps(rows, steps, tile):
    span = rows.shape[0] // SUBS

    def move(i, unused):
        rows[pl.ds(i, SUBS, stride=span), :] = steps[
            tile, pl.ds(pl.multiple_of(i * SUBS, SUBS), SUBS), :
        ]
        return unused

    lax.fori_loop(0, span, move, 0, unroll=8)


def step_rows(i):
    return pl.ds(pl.multiple_of(i * SUBS, SUBS), SUBS)


def norm_kernel(
    place, x_ref, gain_ref, logr_ref, normed_ref, turned_ref, u_tiles, ends_ref, total_ref, rows
):
    unit, unused = normalise(x_ref[...].astype(f32))
    normed_ref[...] = (unit * gain_ref[...]).astype(bf16)
    turned_ref[...] = normed_ref[...].T
    tiles, length, unused = u_tiles.shape
    states = logr_ref.shape[0]
    span = length // SUBS
    for tile in range(tiles):
        start = place[0] * (tiles * LANES) + tile * LANES
        rows[...] = normed_ref[:, pl.ds(pl.multiple_of(start, LANES), LANES)].astype(f32)
        in_steps(u_tiles, tile, rows)
    left = ((SUBS - 1 - sub_index()) * span).astype(f32)
    for tile in range(tiles):
        rate = jnp.exp(logr_ref[:, lane_tile(tile)])
        decay = jnp.exp(-rate)
        decays = [spread(decay[n : n + 1]) for n in range(states)]

        def step(i, held):
            u = u_tiles[tile, step_rows(i), :]
            return tuple(d * h + u for d, h in zip(decays, held))

        zero = no_state(u_tiles)
        held = lax.fori_loop(0, span, step, (zero,) * states, unroll=4)
        for n in range(states):
            ends_ref[n, :, lane_tile(tile)] = held[n]
            total_ref[n : n + 1, lane_tile(tile)] = jnp.sum(
                held[n] * jnp.exp(-left * rate[n : n + 1]), axis=0, keepdims=True
            )


def context_kernel(
    place, u_tiles, ends_ref, all_ref, logr_ref, coef_ref, context_ref, y_tiles, rows
):
    tiles, length, unused = u_tiles.shape
    states = logr_ref.shape[0]
    span = length // SUBS
    index = sub_index()
    before = (index * span).astype(f32)
    for tile in range(tiles):
        rate = jnp.exp(logr_ref[:, lane_tile(tile)])
        decay = jnp.exp(-rate)
        scale = coef_ref[:, lane_tile(tile)] * jnp.sqrt(2.0 * rate)
        incoming = jnp.zeros((states, LANES), f32)
        for j in range(all_ref.shape[0]):
            gap = place[1] - 1 - j
            distance = (jnp.maximum(gap, 0) * length).astype(f32)
            term = jnp.exp(-distance * rate) * all_ref[j, :, lane_tile(tile)].astype(f32)
            incoming = incoming + jnp.where(gap >= 0, term, 0.0)
        for first in range(0, states, GROUP):
            chosen = range(first, first + GROUP)
            starts = []
            for n in chosen:
                row = rate[n : n + 1]
                run = ends_ref[n, :, lane_tile(tile)]
                for d in (1, 2, 4):
                    moved = jnp.exp(-(d * span) * row) * pltpu.roll(run, d, 0)
                    run = run + jnp.where(index >= d, moved, 0.0)
                run = jnp.where(index >= 1, pltpu.roll(run, 1, 0), 0.0)
                starts.append(run + jnp.exp(-before * row) * incoming[n : n + 1])
            decays = [spread(decay[n : n + 1]) for n in chosen]
            scales = [spread(scale[n : n + 1]) for n in chosen]

            def step(i, held):
                at = step_rows(i)
                u = u_tiles[tile, at, :]
                held = tuple(d * h + u for d, h in zip(decays, held))
                parts = [s * h for s, h in zip(scales, held)]
                if first > 0:
                    parts[0] = parts[0] + y_tiles[tile, at, :]
                while len(parts) > 1:
                    parts = [a + b for a, b in zip(parts[::2], parts[1::2])]
                y_tiles[tile, at, :] = parts[0]
                return held

            lax.fori_loop(0, span, step, tuple(starts), unroll=4)
        from_steps(rows, y_tiles, tile)
        context_ref[:, lane_tile(tile)] = rows[...].astype(bf16)


def whole_rows(block):
    return block.reshape(block.shape[0] * block.shape[1], block.shape[2])


def head(index):
    return slice(index * HD, (index + 1) * HD)


def weight_copies(near, far, buffer, place, sems, act):
    count = sems.shape[0]
    half = count // 2
    for k in range(count):
        owner = lax.rem(place[6] + count - k, count)
        for stacks, low in ((near, 0), (far, half)):

            @pl.when((owner >= low) & (owner < low + half))
            def move():
                for r, stack in enumerate(stacks):
                    inner = buffer.at[k, place[2] ^ r]
                    act(pltpu.make_async_copy(stack.at[owner - low], inner, sems.at[k, r]))


def of_heads(buffer, i):
    return jnp.concatenate([whole_rows(buffer[k, :, :, head(i)]) for k in range(buffer.shape[0])], axis=1)


def gradient_slot(row_parts, order, r):
    position = 0
    for bit in reversed(order):
        position = 2 * position + (1 if r & bit else 0)
    return position // (row_parts // 2), position % (row_parts // 2)


def round_orders(row_parts):
    bits = [1 << i for i in range(row_parts.bit_length() - 1)]
    return bits, bits[::-1]


def gradient_pieces(stacks, row_parts, far, slot):
    found = []
    for r in range(row_parts):
        sent, at = gradient_slot(row_parts, round_orders(row_parts)[far], r)
        found.append(stacks[2 * far + sent].at[at, slot])
    return found


def project_kernel(team, col_parts, row_parts, place, normed_ref, cot_ref, *refs):
    contexts, refs = refs[:team], refs[team:]
    near, far, refs = refs[:row_parts], refs[row_parts : 2 * row_parts], refs[2 * row_parts :]
    context_t_ref, cot_t_ref, kept_ref = refs[:3]
    context_ref, weights, sems = refs[3:]
    weight_copies(near, far, weights, place, sems, lambda copy: copy.start())
    width = contexts[0].shape[1]
    for k in range(team):
        lanes = pl.ds(pl.multiple_of((place[0] ^ k) * width, LANES), width)
        context_ref[:, lanes] = contexts[k][...]
    context_t_ref[...] = context_ref[...].T
    cot_t_ref[...] = cot_ref[...].T
    weight_copies(near, far, weights, place, sems, lambda copy: copy.wait())
    kept_ref[0] = dot(normed_ref[...], of_heads(weights, 0)).astype(bf16)
    kept_ref[1] = dot(context_ref[...], of_heads(weights, 1)).astype(bf16)
    kept_ref[2] = dot(context_ref[...], of_heads(weights, 2)).astype(bf16)


def attend_kernel(team, col_parts, row_parts, place, kept_ref, *refs):
    near, far, refs = refs[:row_parts], refs[row_parts : 2 * row_parts], refs[2 * row_parts :]
    part_ref, attended_ref, probs_ref, probs_t_ref, weights, sems = refs
    weight_copies(near, far, weights, place, sems, lambda copy: copy.start())
    length = kept_ref.shape[1]
    rows = lax.broadcasted_iota(jnp.int32, (length, length), 0)
    cols = lax.broadcasted_iota(jnp.int32, (length, length), 1)
    for h in range(col_parts):
        scores = dot_t(kept_ref[0, :, head(h)], kept_ref[1, :, head(h)]) * score_scale
        scores = jnp.where(rows >= cols, scores, -1e30)
        shifted = jnp.exp(scores - jnp.max(scores, axis=-1, keepdims=True))
        inverse = 1.0 / jnp.sum(shifted, axis=-1, keepdims=True)
        probs = (shifted * inverse).astype(bf16)
        probs_ref[h] = probs
        probs_t_ref[h] = probs.T
        attended_ref[:, head(h)] = dot(probs, kept_ref[2, :, head(h)]).astype(bf16)
    weight_copies(near, far, weights, place, sems, lambda copy: copy.wait())
    part_ref[...] = dot_t(attended_ref[...], of_heads(weights, 3)).astype(bf16)


def gelu_parts(hidden, grad_act):
    density = jnp.exp(-0.5 * hidden * hidden)
    t = 1.0 / (1.0 + (0.3275911 * math.sqrt(0.5)) * jnp.abs(hidden))
    series = 0.5 * 1.061405429
    for factor in (-1.453152027, 1.421413741, -0.284496736, 0.254829592):
        series = series * t + 0.5 * factor
    tail = series * t * density
    cdf = jnp.where(hidden >= 0.0, 1.0 - tail, tail)
    slope = cdf + hidden * density * (1.0 / math.sqrt(2.0 * math.pi))
    return (hidden * cdf).astype(bf16), (grad_act * slope).astype(bf16)


def middle_kernel(team, x_ref, gain_ref, *refs):
    parts, (middle_ref, normed_ref, normed_t_ref) = refs[:team], refs[team:]
    attn = parts[0][...].astype(f32)
    for part in parts[1:]:
        attn = attn + part[...].astype(f32)
    middle = x_ref[...].astype(f32) + attn
    middle_ref[...] = middle
    unit, unused = normalise(middle)
    normed_ref[...] = (unit * gain_ref[...]).astype(bf16)
    normed_t_ref[...] = normed_ref[...].T


def feed_kernel(team, col_parts, row_parts, place, normed_ref, normed_t_ref, cot_ref, cot_t_ref, *refs):
    count = col_parts * row_parts
    pieces, refs = refs[:count], refs[count:]
    outs, two_ref, refs = refs[:team], refs[team], refs[team + 1 :]
    stacks, refs = (refs[:4], refs[4:8]), refs[8:]
    up_all, down_all, grad_up, grad_down, activated_all, grad_all, sems = refs
    z = pl.program_id(0)
    half = col_parts // 2
    hidden_cols = grad_up.shape[3]

    def copies(k):
        found = []
        for r in range(row_parts):
            for which, buffer in enumerate((up_all, down_all)):
                outside = pieces[k * row_parts + r].at[:, pl.ds(which * hidden_cols, hidden_cols)]
                inside = buffer.at[place[2] ^ r, :, pl.ds(k * hidden_cols, hidden_cols)]
                found.append(pltpu.make_async_copy(outside, inside, sems.at[which, k, r]))
        return found

    def each_leaving(k, act):
        for which, buffer in enumerate((grad_up, grad_down)):
            for r, piece in enumerate(gradient_pieces(stacks[which], row_parts, k // half, k % half)):
                inner = buffer.at[k, place[2] ^ r]
                act(pltpu.make_async_copy(inner, piece, sems.at[2 + which, k, r]))

    @pl.when(z == 0)
    def start():
        for k in range(col_parts):
            for copy in copies(k):
                copy.start()

    for k in range(col_parts):

        @pl.when(z == k)
        def arrive():
            for copy in copies(k):
                copy.wait()

    at = pl.ds(pl.multiple_of(z * hidden_cols, hidden_cols), hidden_cols)
    hidden = dot(normed_ref[...], whole_rows(up_all[:, :, at]))
    grad_act = dot(cot_ref[...], whole_rows(down_all[:, :, at]))
    activated, grad_pre = gelu_parts(hidden, grad_act)
    activated_all[:, at] = activated
    grad_all[:, at] = grad_pre
    shape = grad_up.shape[1:]
    grad_up[z] = dot(normed_t_ref[...], grad_pre).astype(bf16).reshape(shape)
    grad_down[z] = dot(cot_t_ref[...], activated).astype(bf16).reshape(shape)

    for k in range(col_parts):

        @pl.when(z == k)
        def leave():
            each_leaving(k, lambda copy: copy.start())

    @pl.when(z == col_parts - 1)
    def finish():
        two_ref[...] = dot_t(grad_all[...], whole_rows(up_all[...])).astype(bf16)
        rows = outs[0].shape[0]
        for k in range(team):
            at_rows = pl.ds(pl.multiple_of((place[0] ^ k) * rows, rows), rows)
            outs[k][...] = dot_t(activated_all[at_rows, :], whole_rows(down_all[...])).astype(bf16)
        for k in range(col_parts):
            each_leaving(k, lambda copy: copy.wait())


def attend_back_kernel(team, col_parts, row_parts, place, middle_ref, gain_ref, cot_ref, *refs):
    parts, refs = refs[:team], refs[team:]
    late, refs = refs[:3], refs[3:]
    near, far, refs = refs[:row_parts], refs[row_parts : 2 * row_parts], refs[2 * row_parts :]
    middle_grad_ref, gain_grad_ref, one_ref, low = refs[:4]
    grad_q, grad_k, grad_v = refs[4:7]
    context_grads, refs = refs[7 : 7 + team], refs[7 + team :]
    weights, grad_out, total_low = refs[:3]
    held, (sems, late_sems) = refs[3:6], refs[6:]
    kept_ref, probs_ref, probs_t_ref = held
    weight_copies(near, far, weights, place, sems, lambda copy: copy.start())
    late_copies = [
        pltpu.make_async_copy(outside, inside, late_sems.at[i])
        for i, (outside, inside) in enumerate(zip(late, held))
    ]
    for copy in late_copies:
        copy.start()
    own_rows = middle_ref.shape[0] // team
    grad_two = parts[0][...].astype(f32)
    for part in parts[1:]:
        grad_two = grad_two + part[...].astype(f32)
    unit, inverse = normalise(middle_ref[...])
    grad_gain = grad_two * unit
    rows = lax.broadcasted_iota(jnp.int32, grad_gain.shape, 0)
    first = place[0] * own_rows
    mine = (rows >= first) & (rows < first + own_rows)
    gain_grad_ref[...] = jnp.sum(jnp.where(mine, grad_gain, 0.0), axis=0, keepdims=True)
    grad = cot_ref[...].astype(f32) + normalise_back(unit, inverse, grad_two * gain_ref[...])
    low[...] = grad.astype(bf16)
    for k in range(team):

        @pl.when(place[0] == k)
        def own():
            middle_grad_ref[...] = grad[k * own_rows : (k + 1) * own_rows, :]

    weight_copies(near, far, weights, place, sems, lambda copy: copy.wait())
    for copy in late_copies:
        copy.wait()
    grad_out[...] = dot(low[...], of_heads(weights, 3)).astype(bf16)
    for h in range(col_parts):
        q, k, v = (kept_ref[i, :, head(h)] for i in range(3))
        grad_heads = grad_out[:, head(h)]
        grad_v[:, head(h)] = dot(probs_t_ref[h], grad_heads).astype(bf16)
        probs = probs_ref[h].astype(f32)
        grad_probs = dot_t(grad_heads, v)
        inner = jnp.sum(grad_probs * probs, axis=-1, keepdims=True)
        grad_scores = (probs * (grad_probs - inner)).astype(bf16)
        grad_q[:, head(h)] = (dot(grad_scores, k) * score_scale).astype(bf16)
        turned = dot_t(v, grad_heads) - inner.T
        turned = (probs_t_ref[h].astype(f32) * turned).astype(bf16)
        grad_k[:, head(h)] = (dot(turned, q) * score_scale).astype(bf16)
    total = dot_t(grad_k[...], of_heads(weights, 1)) + dot_t(grad_v[...], of_heads(weights, 2))
    total_low[...] = total.astype(bf16)
    width = context_grads[0].shape[1]
    for k in range(team):
        lanes = pl.ds(pl.multiple_of((place[0] ^ k) * width, LANES), width)
        context_grads[k][...] = total_low[:, lanes]
    one_ref[...] = dot_t(grad_q[...], of_heads(weights, 0)).astype(bf16)


def head_grads_kernel(col_parts, row_parts, place, low, attended_ref, *refs):
    normed_t_ref, context_t_ref, grad_q, grad_k, grad_v = refs[:5]
    stacks, (grads, out_sems) = refs[5:9], refs[9:]
    half = col_parts // 2
    shape = (*grads.shape[1:3], HD)

    def put(i, grad):
        for h in range(col_parts):
            grads[h, :, :, head(i)] = grad[:, head(h)].astype(bf16).reshape(shape)

    put(0, dot(normed_t_ref[...], grad_q[...]))
    put(1, dot(context_t_ref[...], grad_k[...]))
    put(2, dot(context_t_ref[...], grad_v[...]))
    put(3, dot(low[...].T, attended_ref[...]))
    copies = []
    for k in range(col_parts):
        for r, piece in enumerate(gradient_pieces(stacks, row_parts, k // half, k % half)):
            copies.append(pltpu.make_async_copy(grads.at[k, place[2] ^ r], piece, out_sems.at[k, r]))
    for copy in copies:
        copy.start()
    for copy in copies:
        copy.wait()


def adjoint_kernel(team, logr_ref, *refs):
    parts = refs[:team]
    g_tiles, ends_ref, total_ref, rows = refs[team:]
    grad = parts[0][...].astype(f32)
    for part in parts[1:]:
        grad = grad + part[...].astype(f32)
    grad = grad.astype(bf16).astype(f32)
    tiles, length, unused = g_tiles.shape
    states = logr_ref.shape[0]
    span = length // SUBS
    for tile in range(tiles):
        rows[...] = grad[:, lane_tile(tile)]
        in_steps(g_tiles, tile, rows)
    before = (sub_index() * span).astype(f32)
    for tile in range(tiles):
        rate = jnp.exp(logr_ref[:, lane_tile(tile)])
        decay = jnp.exp(-rate)
        for first in range(0, states, GROUP):
            chosen = range(first, first + GROUP)
            decays = [spread(decay[n : n + 1]) for n in chosen]

            def step(i, held):
                g = g_tiles[tile, step_rows(span - 1 - i), :]
                later = []
                for d, (b, w) in zip(decays, held):
                    shrunk = d * b
                    later.append((g + shrunk, d * w + shrunk))
                return tuple(later)

            zero = no_state(g_tiles)
            held = lax.fori_loop(0, span, step, ((zero, zero),) * GROUP, unroll=4)
            for n, (b, w) in zip(chosen, held):
                ends_ref[0, n, :, lane_tile(tile)] = b
                ends_ref[1, n, :, lane_tile(tile)] = w
                shrink = jnp.exp(-before * rate[n : n + 1])
                total_ref[0, n : n + 1, lane_tile(tile)] = jnp.sum(
                    shrink * b, axis=0, keepdims=True
                )
                total_ref[1, n : n + 1, lane_tile(tile)] = jnp.sum(
                    shrink * (w + before * b), axis=0, keepdims=True
                )


def context_back_kernel(
    team, place, g_tiles, u_tiles, ends_ref, all_ref, logr_ref, coef_ref, one_ref, *refs
):
    pieces = refs[:team]
    grad_ssm_ref, y_tiles, full, rows = refs[team:]
    tiles, length, unused = u_tiles.shape
    states = logr_ref.shape[0]
    span = length // SUBS
    width = tiles * LANES
    index = sub_index()
    after = ((SUBS - 1 - index) * span).astype(f32)
    full[...] = one_ref[...].astype(f32)
    group = GROUP
    for tile in range(tiles):
        lanes = lane_tile(tile)
        rate = jnp.exp(logr_ref[:, lanes])
        decay = jnp.exp(-rate)
        root = jnp.sqrt(2.0 * rate)
        scale = coef_ref[:, lanes] * root
        in_b = jnp.zeros((states, LANES), f32)
        in_w = jnp.zeros((states, LANES), f32)
        for j in range(all_ref.shape[0]):
            gap = j - place[1] - 1
            distance = (jnp.maximum(gap, 0) * length).astype(f32)
            shrink = jnp.exp(-distance * rate)
            b, w = all_ref[j, 0, :, lanes].astype(f32), all_ref[j, 1, :, lanes].astype(f32)
            in_b = in_b + jnp.where(gap >= 0, shrink * b, 0.0)
            in_w = in_w + jnp.where(gap >= 0, shrink * (w + distance * b), 0.0)
        for first in range(0, states, group):
            chosen = range(first, first + group)
            starts = []
            for n in chosen:
                row = rate[n : n + 1]
                b, w = ends_ref[0, n, :, lanes], ends_ref[1, n, :, lanes]
                for d in (1, 2, 4):
                    shrink = jnp.exp(-(d * span) * row)
                    next_b = pltpu.roll(b, SUBS - d, 0)
                    next_w = pltpu.roll(w, SUBS - d, 0)
                    inside = index < SUBS - d
                    b, w = (
                        b + jnp.where(inside, shrink * next_b, 0.0),
                        w + jnp.where(inside, shrink * (next_w + (d * span) * next_b), 0.0),
                    )
                inside = index < SUBS - 1
                b = jnp.where(inside, pltpu.roll(b, SUBS - 1, 0), 0.0)
                w = jnp.where(inside, pltpu.roll(w, SUBS - 1, 0), 0.0)
                shrink = jnp.exp(-after * row)
                b_row, w_row = in_b[n : n + 1], in_w[n : n + 1]
                b = b + shrink * b_row
                w = w + shrink * (w_row + after * b_row)
                zero = no_state(u_tiles)
                starts.append((b, w, zero, zero))
            decays = [spread(decay[n : n + 1]) for n in chosen]
            scales = [spread(scale[n : n + 1]) for n in chosen]

            def step(i, held):
                at = step_rows(span - 1 - i)
                g = g_tiles[tile, at, :]
                u = u_tiles[tile, at, :]
                later, parts = [], []
                for d, s, (b, w, sum_b, sum_w) in zip(decays, scales, held):
                    shrunk = d * b
                    w = d * w + shrunk
                    b = g + shrunk
                    later.append((b, w, sum_b + u * b, sum_w + u * w))
                    parts.append(s * b)
                while len(parts) > 1:
                    parts = [p + q for p, q in zip(parts[::2], parts[1::2])]
                if first > 0:
                    parts[0] = parts[0] + y_tiles[tile, at, :]
                y_tiles[tile, at, :] = parts[0]
                return tuple(later)

            held = lax.fori_loop(0, span, step, tuple(starts), unroll=2)
            for n, (unused_b, unused_w, sum_b, sum_w) in zip(chosen, held):
                sum_b = jnp.sum(sum_b, axis=0, keepdims=True)
                sum_w = jnp.sum(sum_w, axis=0, keepdims=True)
                row = slice(n, n + 1)
                grad_ssm_ref[0, row, lanes] = root[row] * sum_b
                grad_ssm_ref[1, row, lanes] = scale[row] * (0.5 * sum_b - rate[row] * sum_w)
        at_lanes = pl.ds(pl.multiple_of(place[0] * width + tile * LANES, LANES), LANES)
        from_steps(rows, y_tiles, tile)
        full[:, at_lanes] += rows[...].astype(bf16).astype(f32)
    count = pieces[0].shape[0]
    for k in range(team):
        at_rows = pl.ds(pl.multiple_of((place[0] ^ k) * count, count), count)
        pieces[k][...] = full[at_rows, :].astype(bf16)


def input_grad_kernel(team, place, x_ref, gain_ref, middle_grad_ref, *refs):
    parts, (out_ref, gain_grad_ref) = refs[:team], refs[team:]
    rows = out_ref.shape[0]
    at_rows = pl.ds(pl.multiple_of(place[0] * rows, rows), rows)
    grad_one = parts[0][...].astype(f32)
    for part in parts[1:]:
        grad_one = grad_one + part[...].astype(f32)
    unit, inverse = normalise(x_ref[at_rows, :].astype(f32))
    gain_grad_ref[...] = jnp.sum(grad_one * unit, axis=0, keepdims=True)
    back = normalise_back(unit, inverse, grad_one * gain_ref[...])
    out_ref[...] = (middle_grad_ref[...] + back).astype(bf16)


def assemble_kernel(halves, low_count, place, own_ref, *refs):
    others, out_ref = refs[:-1], refs[-1]
    count, rows, unused = own_ref.shape
    half = place[4]

    def put(value, sequence, which, member):
        at_rows = pl.ds(pl.multiple_of((which * low_count + member) * rows, rows), rows)
        out_ref[sequence, at_rows, :] = value.astype(out_ref.dtype)

    for sequence in range(count // (halves * low_count)):
        if halves == 1:
            for member in range(low_count):
                put(own_ref[sequence * low_count + member], sequence, 0, member)
        else:
            put(own_ref[sequence * halves + half], sequence, half, 0)
            put(others[0][sequence], sequence, 1 - half, 0)


def pack_kernel(halves, place, qkv_ref, out_ref, up_ref, down_ref, *refs):
    rows = up_ref.shape[0]
    heads, hidden = out_ref.shape[0] // halves, up_ref.shape[1] // halves
    for which in range(halves):
        side = place[4] if which == 0 else 1 - place[4]
        at_heads = pl.ds(pl.multiple_of(side * heads, LANES), heads)
        at_hidden = pl.ds(pl.multiple_of(side * hidden, LANES), hidden)
        if which == 0:
            head_ref = refs[0]
            wide_ref, deep_ref = refs[1].at[:, :hidden], refs[1].at[:, hidden:]
        else:
            packed = refs[2]
            head_ref = packed.at[:, : 4 * heads]
            wide_ref = packed.at[:, 4 * heads : 4 * heads + hidden]
            deep_ref = packed.at[:, 4 * heads + hidden :]
        for i in range(3):
            head_ref[:, i * heads : (i + 1) * heads] = qkv_ref[i, :, at_heads].astype(bf16)
        head_ref[:, 3 * heads :] = out_ref[at_heads, :].T.astype(bf16)
        wide_ref[...] = up_ref[:, at_hidden].astype(bf16)
        deep_ref[...] = down_ref[at_hidden, :].T.astype(bf16)


def small_kernel(ssm_ref, gains_ref, out_ref):
    count = ssm_ref.shape[0]
    out_ref[:count, :] = ssm_ref[...]
    out_ref[count:, :] = gains_ref[...]


def lamb_moments(weight, grad_item, first_old, second_old):
    first_new = beta_first * first_old + (1.0 - beta_first) * grad_item
    second_new = beta_second * second_old + (1.0 - beta_second) * grad_item * grad_item
    direction = (
        first_new
        / (1.0 - beta_first**STEP)
        / (jnp.sqrt(second_new / (1.0 - beta_second**STEP)) + lamb_eps)
        + weight_decay * weight
    )
    return (first_new, second_new, direction)


def place_sums(sums_ref, sums):
    rows = lax.broadcasted_iota(jnp.int32, sums_ref.shape, 0)
    lanes = lax.broadcasted_iota(jnp.int32, sums_ref.shape, 1)
    found = jnp.zeros(sums_ref.shape, f32)
    for index, pair in sums.items():
        for row, value in enumerate(pair):
            found = jnp.where((rows == row) & (lanes == index), value, found)
    sums_ref[...] = found


def moments_kernel(halves, matrices, place, *refs):
    count = 1 + max(item[1] for item in matrices)
    grads, refs = [refs[halves * i : halves * (i + 1)] for i in range(count)], refs[halves * count :]
    arrays = len({(item[1], item[4] is None) for item in matrices})
    ins = [refs[3 * i : 3 * i + 3] for i in range(arrays)]
    outs = [refs[3 * (arrays + i) : 3 * (arrays + i) + 3] for i in range(arrays)]
    sums_ref = refs[6 * arrays]
    keys = []
    sums = {}
    for number, source, column, turned, stacked in matrices:
        key = (source, stacked is None)
        if key not in keys:
            keys.append(key)
        pick = (lambda ref: ref) if stacked is None else (lambda ref, i=stacked: ref.at[i])
        weight, first, second = (pick(ref) for ref in ins[keys.index(key)])
        news = [pick(ref) for ref in outs[keys.index(key)]]
        width = weight.shape[0 if turned else 1] // halves
        rows = weight.shape[1 if turned else 0]
        cols = slice(column * width, (column + 1) * width)
        total_weight = total_update = 0.0
        for which, grad_ref in enumerate(grads[source]):
            side = place[4] if which == 0 else 1 - place[4]
            at = pl.ds(pl.multiple_of(side * width, width), width)
            if which == 0:
                grad = grad_ref[pl.ds(pl.multiple_of(side * rows, rows), rows), cols].astype(f32)
            else:
                grad = grad_ref[:, cols].astype(f32)
            at = (at, slice(None)) if turned else (slice(None), at)
            grad = grad.T if turned else grad
            old = weight[at]
            found = lamb_moments(old, grad, first[at], second[at])
            for ref, value in zip(news, found):
                ref[at] = value
            total_weight = total_weight + jnp.sum(old * old)
            total_update = total_update + jnp.sum(found[2] * found[2])
        sums[number] = (total_weight, total_update)
    place_sums(sums_ref, sums)


def small_moments_kernel(numbers, grads_ref, *refs):
    ins, outs, sums_ref = (refs[:3], refs[3:6]), (refs[6:9], refs[9:12]), refs[12]
    states = (grads_ref.shape[0] - 2) // 2
    sums = {}
    for (weight, first, second), news, start, rows, first_number in (
        (ins[0], outs[0], 2 * states, 1, numbers[0]),
        (ins[1], outs[1], 0, states, numbers[1]),
    ):
        for i in range(2):
            grad = grads_ref[start + i * rows : start + (i + 1) * rows, :]
            at = slice(i * rows, (i + 1) * rows)
            found = lamb_moments(weight[at, :], grad, first[at, :], second[at, :])
            for ref, value in zip(news, found):
                ref[at, :] = value
            sums[first_number + i] = (
                jnp.sum(weight[at, :] * weight[at, :]),
                jnp.sum(found[2] * found[2]),
            )
    place_sums(sums_ref, sums)


def update_kernel(stacks, sums_ref, *refs):
    count = len(stacks)
    weights, directions, news = refs[:count], refs[count : 2 * count], refs[2 * count : 3 * count]
    norms = jnp.sqrt(jnp.sum(sums_ref[...], axis=0))
    refs[3 * count][...] = norms
    ratios = norms[0:1] / norms[1:2]
    lanes = lax.broadcasted_iota(jnp.int32, ratios.shape, 1)
    for numbers, weight, direction, new in zip(stacks, weights, directions, news):
        step = weight.shape[0] // len(numbers)
        for i, number in enumerate(numbers):
            ratio = jnp.sum(jnp.where(lanes == number, ratios, 0.0), axis=1, keepdims=True)
            at = slice(i * step, (i + 1) * step)
            scale = learn_rate * ratio.reshape((1,) * weight.ndim)
            new[at] = weight[at] - scale * direction[at]


def call(
    body, ins, outs, scratch=(), grid=None, in_specs=None, out_specs=None, time=1.0, after=(), token=False
):
    moved = sum(a.size * a.dtype.itemsize for a in list(ins) + list(outs))
    params = pltpu.CompilerParams(vmem_limit_bytes=VMEM_BYTES)
    cost = pl.CostEstimate(flops=int(time * 1.15e9), bytes_accessed=moved, transcendentals=0)
    whole = pl.BlockSpec(memory_space=pltpu.VMEM)
    anywhere = pl.BlockSpec(memory_space=pl.ANY)
    in_specs = list(in_specs or [whole] * len(ins)) + [anywhere] * len(after)
    out_specs = list(out_specs or [whole] * len(outs))
    outs = list(outs)
    first_out = len(ins) + len(after)
    last_out = first_out + len(outs)
    if token:
        outs.append(jax.ShapeDtypeStruct((SUBS, LANES), f32))
        out_specs.append(whole)

    def run(*refs):
        refs = list(refs)
        if token:
            refs[last_out][...] = jnp.zeros((SUBS, LANES), f32)
            del refs[last_out]
        body(*refs[: len(ins)], *refs[first_out:])

    return pl.pallas_call(
        run,
        out_shape=tuple(outs),
        in_specs=in_specs,
        out_specs=tuple(out_specs),
        scratch_shapes=list(scratch),
        compiler_params=params,
        cost_estimate=cost,
        **({} if grid is None else {"grid": grid}),
    )(*ins, *after)


def shaped(shape, kind):
    return jax.ShapeDtypeStruct(tuple(shape), kind)


def on_device(
    tokens,
    cotangent,
    w_qkv,
    w_out,
    w_up,
    w_down,
    norm_gains,
    ssm_param,
    first_qkv,
    second_qkv,
    first_out,
    second_out,
    first_up,
    second_up,
    first_down,
    second_down,
    first_gain,
    second_gain,
    first_ssm,
    second_ssm,
):
    halves = lax.axis_size("sl")
    low_count = lax.axis_size("ml")
    row_parts = lax.axis_size("sh")
    col_parts = lax.axis_size("mb") * lax.axis_size("mq")
    team = halves * low_count
    sl, ml, mb, mq = (lax.axis_index(name) for name in ("sl", "ml", "mb", "mq"))
    rank = sl * low_count + ml
    block_index = lax.axis_index("sh") * halves + mq
    seq_total, length, width = tokens.shape
    assert length == BLK and seq_total == lax.axis_size("mb")
    states = ssm_param.shape[1]
    channels = width // team
    tiles = channels // LANES
    row_count = width // row_parts
    own_rows = length // team
    place = [rank, block_index, lax.axis_index("sh"), lax.axis_index(MODEL), sl, sl ^ mq]
    place.append(lax.axis_index(COLS))
    place = jnp.stack(place).astype(jnp.int32)
    smem = pl.BlockSpec(memory_space=pltpu.SMEM)
    vmem = pl.BlockSpec(memory_space=pltpu.VMEM)

    def permute(value, axes, moves):
        return lax.ppermute(value, axes, moves)

    def swap(value):
        return permute(value, "sl", [(0, 1), (1, 0)])

    def in_order(own, other, axis):
        return jnp.where(
            sl == 0, jnp.concatenate([own, other], axis), jnp.concatenate([other, own], axis)
        )

    def team_send(pieces):
        moved = [pieces[0]]
        for k in range(1, team):
            moved.append(permute(pieces[k], TEAM, [(i, i ^ k) for i in range(team)]))
        return moved

    def pick_block(array):
        own = lax.dynamic_index_in_dim(array, mb, 0, keepdims=False)
        if halves == 1:
            return own, ()
        other = swap(own)
        return jnp.where(sl == mq, own, other), (other,)

    def across(value, bit):
        return permute(value, "sh", [(i, i ^ bit) for i in range(row_parts)])

    def along(value, axes, step):
        count = lax.axis_size(axes)
        return permute(value, axes, [(i, (i + step) % count) for i in range(count)])

    bits = [1 << i for i in range(row_parts.bit_length() - 1)]

    def bit_order(k):
        return bits if k % 2 == 0 else bits[::-1]

    def double_rows(value, order):
        found = {0: value}
        for bit in order:
            for r in list(found):
                found[r | bit] = across(found[r], bit)
        return [found[r] for r in range(row_parts)]

    def add(*items, zero=None):
        total = sum(item.astype(f32) for item in items)
        return (total if zero is None else total + zero[0, 0]).astype(bf16)

    def first_messages(stacks):
        return across(stacks[1], bits[-1]), across(stacks[3], bits[0])

    def second_messages(stacks, first, zero):
        count = first[0].shape[0] // 2
        return [add(stacks[2 * i][count:], first[i][count:], zero=zero) for i in range(2)]

    def halve_rows(keep, arrived, order, send, last):
        items = [keep, arrived]
        for bit in order[-2::-1]:
            count = arrived.shape[0] // 2
            if send is None:
                send = add(*[item[count:] for item in items])
            arrived = across(send, bit)
            items = [item[:count] for item in items] + [arrived]
            send = None
        return add(*[item[0] for item in items], zero=last)

    def halve_both(stacks, first, send, last=None):
        near = halve_rows(stacks[0], first[0], bits, send[0], last)
        return near, halve_rows(stacks[2], first[1], bits[::-1], send[1], last)

    def hold(arrays, after):
        anywhere = pl.BlockSpec(memory_space=pl.ANY)
        return pl.pallas_call(
            lambda *refs: None,
            out_shape=tuple(shaped(item.shape, item.dtype) for item in arrays),
            in_specs=[anywhere] * (len(arrays) + len(after)),
            out_specs=(anywhere,) * len(arrays),
            input_output_aliases={i: i for i in range(len(arrays))},
        )(*arrays, *after)

    def gather_pieces(shard):
        pieces = []
        for k in range(col_parts):
            held = along(held, COLS, 1) if k > 0 else shard
            pieces.append(double_rows(held, bits if k % 2 == 0 else bits[::-1]))
        return pieces

    def sum_over_z(near, far, ring=True):
        if not ring:
            pieces = [stack[k] for stack in (near, far) for k in range(col_parts // 2)]
            moved = [along(piece, COLS, -k) for k, piece in enumerate(pieces) if k > 0]
            return add(pieces[0], *moved)
        held = None
        for stack in (far, near):
            for k in reversed(range(stack.shape[0])):
                held = stack[k] if held is None else add(stack[k], along(held, COLS, -1))
        return held

    def everywhere(value, axes):
        count = lax.axis_size(axes)
        copies = jnp.broadcast_to(value[None], (count, *value.shape))
        return lax.all_to_all(copies, axes, 0, 0, tiled=True)

    rows_dev = w_up.shape[0]
    hidden_cols = w_up.shape[1] // halves
    head_cols = 4 * w_out.shape[0] // halves
    packed_cols = head_cols + 2 * hidden_cols
    sides = [shaped((rows_dev, cols), bf16) for cols in (head_cols, 2 * hidden_cols)]
    shards = call(
        functools.partial(pack_kernel, halves),
        (place, w_qkv, w_out, w_up, w_down),
        sides + [shaped((rows_dev, packed_cols), bf16)] * (halves - 1),
        time=2.4,
        in_specs=[smem] + [vmem] * 4,
    )
    if halves == 2:
        other = swap(shards[2])
        cuts = (0, head_cols, packed_cols)
        shards = [
            in_order(own, other[:, first:last], 0)
            for own, first, last in zip(shards, cuts, cuts[1:])
        ]
    head_shard, hidden_shard = shards[:2]
    hidden_w = gather_pieces(hidden_shard)
    (head_shard,) = hold((head_shard,), (hidden_w[1][0],))
    attn_full = lax.all_gather(head_shard, COLS, axis=0, tiled=False)
    hidden_flat = [piece for group in hidden_w for piece in group]

    small, = call(
        small_kernel,
        (ssm_param.reshape(2 * states, -1), norm_gains),
        (shaped((2 * states + 2, norm_gains.shape[1]), f32),),
        after=hidden_w[0][1:-1],
    )
    small = jnp.transpose(everywhere(small, ALL), (1, 0, 2)).reshape(2 * states + 2, width)
    own_ssm = lax.dynamic_slice_in_dim(
        small[: 2 * states].reshape(2, states, width), rank * channels, channels, 2
    )
    coef, logr = own_ssm[0], own_ssm[1]
    gain_one = small[2 * states : 2 * states + 1]
    gain_two = small[2 * states + 1 : 2 * states + 2]

    x, unused = pick_block(tokens)
    cot, cot_other = pick_block(cotangent)

    anywhere = [pl.BlockSpec(memory_space=pl.ANY)]

    def fixed(*shape):
        return pl.BlockSpec(shape, lambda z: (0,) * len(shape))

    wide = fixed(length, width)
    row = fixed(1, width)

    normed_one, normed_t, u_steps, ends, total = call(
        norm_kernel,
        (place, x, gain_one, logr),
        (
            shaped((length, width), bf16),
            shaped((width, length), bf16),
            shaped((tiles, length, LANES), f32),
            shaped((states, SUBS, channels), f32),
            shaped((states, channels), f32),
        ),
        scratch=[pltpu.VMEM((length, LANES), f32)],
        in_specs=[smem, vmem, vmem, vmem],
        after=(hidden_w[1][0], *cot_other),
        time=5,
    )
    (attn_full,) = hold((attn_full,), (total,))
    attn_w = [
        *double_rows(attn_full[: col_parts // 2], bits),
        *double_rows(attn_full[col_parts // 2 :], bits[::-1]),
    ]
    totals = everywhere(total.astype(bf16), ("sh", "mq"))
    (context_own,) = call(
        context_kernel,
        (place, u_steps, ends, totals, logr, coef),
        (shaped((length, channels), bf16),),
        after=(hidden_w[0][-1], *hidden_w[1][1:-1], hidden_w[-1][0], *attn_w[1 : row_parts - 1]),
        scratch=[pltpu.VMEM((tiles, length, LANES), f32), pltpu.VMEM((length, LANES), f32)],
        in_specs=[smem] + [vmem] * 5,
        time=7,
    )
    contexts = team_send([context_own] * team)

    stack_shape = (row_parts // 2, col_parts // 2, row_count)
    head_stacks = [shaped((*stack_shape, head_cols), bf16)] * 4
    hidden_stacks = [shaped((*stack_shape, hidden_cols), bf16)] * 8
    sizes = (team, col_parts, row_parts)
    head_buffer = pltpu.VMEM((col_parts, row_parts, row_count, 4 * HD), bf16)
    head_sems = pltpu.SemaphoreType.DMA((col_parts, row_parts))
    kept_shape = shaped((3, length, col_parts * HD), bf16)
    flat_shape = shaped((length, col_parts * HD), bf16)
    context_t, cot_t, kept = call(
        functools.partial(project_kernel, *sizes),
        (place, normed_one, cot, *contexts, *attn_w),
        (shaped((width, length), bf16), shaped((width, length), bf16), kept_shape),
        scratch=[pltpu.VMEM((length, width), bf16), head_buffer, head_sems],
        time=1,
        in_specs=[smem] + [vmem] * (2 + team) + anywhere * len(attn_w),
        after=(hidden_w[1][-1], *[piece for group in hidden_w[2:3] for piece in group[1:]]),
    )
    attn_part, attended, probs, probs_t = call(
        functools.partial(attend_kernel, *sizes),
        (place, kept, *attn_w),
        (
            shaped((length, width), bf16),
            flat_shape,
            *[shaped((col_parts, length, length), bf16)] * 2,
        ),
        scratch=[head_buffer, head_sems],
        time=1,
        in_specs=[smem, vmem] + anywhere * len(attn_w),
        after=[piece for group in hidden_w[3:] for piece in group[1:-1]],
    )
    attn_parts = team_send([attn_part] * team)

    middle, normed_two, normed_two_t = call(
        functools.partial(middle_kernel, team),
        (x, gain_two, *attn_parts),
        (shaped((length, width), f32), shaped((length, width), bf16), shaped((width, length), bf16)),
        time=1,
    )
    weight_buffer = pltpu.VMEM((row_parts, row_count, col_parts * hidden_cols), bf16)
    grad_buffer = pltpu.VMEM((col_parts, row_parts, row_count, hidden_cols), bf16)
    fed = call(
        functools.partial(feed_kernel, team, col_parts, row_parts),
        (place, normed_two, normed_two_t, cot, cot_t, *hidden_flat),
        (
            *[shaped((own_rows, width), bf16)] * team,
            shaped((length, width), bf16),
            *hidden_stacks,
        ),
        scratch=[
            *[weight_buffer] * 2,
            *[grad_buffer] * 2,
            *[pltpu.VMEM((length, col_parts * hidden_cols), bf16)] * 2,
            pltpu.SemaphoreType.DMA((4, col_parts, row_parts)),
        ],
        time=18,
        grid=(col_parts,),
        in_specs=[smem, wide, fixed(width, length), wide, fixed(width, length)]
        + anywhere * len(hidden_flat),
        out_specs=[fixed(own_rows, width)] * team + [wide] + anywhere * 8,
    )
    out_pieces, two_part, hidden_grads = fed[:team], fed[team], fed[team + 1 :]
    two_parts = team_send([two_part] * team)

    def rows_of(array, member):
        return lax.dynamic_slice_in_dim(array, member * own_rows, own_rows, 0)

    def share_rows(pieces, kind):
        others = []
        if halves == 2:
            pairs = pieces.reshape(seq_total, halves, own_rows, width)
            others = [swap(lax.dynamic_index_in_dim(pairs, 1 - sl, 1, keepdims=False))]
        (blocks,) = call(
            functools.partial(assemble_kernel, halves, low_count),
            (place, pieces, *others),
            (shaped((seq_total, length, width), kind),),
            time=3.5,
            in_specs=[smem, vmem] + [vmem] * len(others),
        )
        return blocks

    out_pieces = team_send(list(out_pieces))
    result = rows_of(middle, rank) + sum(item.astype(f32) for item in out_pieces)
    result = result.astype(bf16)
    layer_pieces = lax.all_gather(result, MODEL, axis=0, tiled=False)
    layer_out = share_rows(layer_pieces, bf16)

    def both_halves(own):
        if halves == 1:
            return [own]
        return [own, swap(lax.dynamic_slice_in_dim(own, (1 - sl) * rows_dev, rows_dev, 0))]

    middle_grad, gain_two_grad, one_part, low_grad, *rest = call(
        functools.partial(attend_back_kernel, *sizes),
        (place, middle, gain_two, cot, *two_parts, kept, probs, probs_t, *attn_w),
        (
            shaped((own_rows, width), f32),
            shaped((1, width), f32),
            shaped((length, width), bf16),
            shaped((length, width), bf16),
            *[flat_shape] * 3,
            *[shaped((length, channels), bf16)] * team,
        ),
        scratch=[
            head_buffer,
            pltpu.VMEM(flat_shape.shape, bf16),
            pltpu.VMEM((length, width), bf16),
            pltpu.VMEM(kept_shape.shape, bf16),
            *[pltpu.VMEM((col_parts, length, length), bf16)] * 2,
            head_sems,
            pltpu.SemaphoreType.DMA((3,)),
        ],
        time=1,
        in_specs=[smem] + [vmem] * (3 + team) + anywhere * (3 + len(attn_w)),
        after=(result,),
    )
    head_grads, context_grads = rest[:3], rest[3:]
    context_grads = team_send(context_grads)
    *head_stacks, heads_done = call(
        functools.partial(head_grads_kernel, col_parts, row_parts),
        (place, low_grad, attended, normed_t, context_t, *head_grads),
        head_stacks,
        scratch=[head_buffer, head_sems],
        time=8,
        in_specs=[smem] + [vmem] * 7,
        out_specs=anywhere * 4,
        token=True,
    )
    down_first = first_messages(hidden_grads[4:])
    down_second = second_messages(hidden_grads[4:], down_first, heads_done)
    down_sums = halve_both(hidden_grads[4:], down_first, down_second)
    g_steps, adjoint_ends, adjoint_total, adjoint_done = call(
        functools.partial(adjoint_kernel, team),
        (logr, *context_grads),
        (
            shaped((tiles, length, LANES), f32),
            shaped((2, states, SUBS, channels), f32),
            shaped((2, states, channels), f32),
        ),
        scratch=[pltpu.VMEM((length, LANES), f32)],
        time=1,
        after=(heads_done, *down_second),
        token=True,
    )
    up_stacks = list(hidden_grads[:4])
    up_stacks[1::2] = hold(up_stacks[1::2], down_first)
    up_first = first_messages(up_stacks)
    (own_total,) = hold((adjoint_total.astype(bf16),), (*down_sums, *up_first))
    adjoint_totals = everywhere(own_total, ("sh", "mq"))
    grad_down = sum_over_z(*down_sums, False)
    up_second = second_messages(up_stacks, up_first, adjoint_done)
    up_second = hold(up_second, (adjoint_totals,))
    *one_pieces, grad_ssm, context_done = call(
        functools.partial(context_back_kernel, team),
        (place, g_steps, u_steps, adjoint_ends, adjoint_totals, logr, coef, one_part),
        (
            *[shaped((own_rows, width), bf16)] * team,
            shaped((2, states, channels), f32),
        ),
        scratch=[
            pltpu.VMEM((tiles, length, LANES), f32),
            pltpu.VMEM((length, width), f32),
            pltpu.VMEM((length, LANES), f32),
        ],
        in_specs=[smem] + [vmem] * 7,
        time=1,
        after=(*up_second, layer_pieces),
        token=True,
    )
    one_pieces = team_send(one_pieces)
    up_sums = halve_both(up_stacks, up_first, up_second, context_done)
    grad_rows, gain_one_grad, rows_done = call(
        functools.partial(input_grad_kernel, team),
        (place, x, gain_one, middle_grad, *one_pieces),
        (shaped((own_rows, width), bf16), shaped((1, width), f32)),
        in_specs=[smem] + [vmem] * (3 + team),
        time=1,
        after=(grad_down, *up_sums),
        token=True,
    )
    head_stacks[1::2] = hold(head_stacks[1::2], (grad_rows,))
    up_sums = hold(up_sums, head_stacks[1::2])
    head_first = first_messages(head_stacks)
    head_second = second_messages(head_stacks, head_first, rows_done)
    head_sums = halve_both(head_stacks, head_first, head_second)
    grad_up = sum_over_z(*up_sums)
    grad_heads = sum_over_z(*head_sums)
    input_grad = share_rows(lax.all_gather(grad_rows, MODEL, axis=0, tiled=False), f32)

    placed_ssm = lax.dynamic_update_slice_in_dim(
        jnp.zeros((2 * states, width), f32),
        grad_ssm.reshape(2 * states, channels),
        rank * channels,
        1,
    )
    small_grads = jnp.concatenate([placed_ssm, gain_one_grad, gain_two_grad], 0)
    (small_grads,) = hold((small_grads,), head_sums)
    small_grads = small_grads.reshape(2 * states + 2, lax.axis_size(ALL), -1)
    small_grads = lax.all_to_all(jnp.transpose(small_grads, (1, 0, 2)), ALL, 0, 0, tiled=True)
    small_grads = jnp.sum(small_grads, axis=0)

    def moments(matrices, grads, arrays, after=()):
        changed = [shaped(old.shape, f32) for group in arrays for old in group]
        grad_parts = [part for grad in grads for part in both_halves(grad)]
        ins = [item for group in arrays for item in group]
        *found, sums = call(
            functools.partial(moments_kernel, halves, matrices),
            (place, *grad_parts, *ins),
            (*changed, shaped((2, LANES), f32)),
            in_specs=[smem] + [vmem] * (len(grad_parts) + len(ins)),
            after=after,
            time=4,
        )
        return [found[3 * i : 3 * i + 3] for i in range(len(arrays))], sums

    hidden_new, hidden_sums = moments(
        ((4, 0, 0, False, None), (5, 1, 0, True, None)),
        (grad_up, grad_down),
        ((w_up, first_up, second_up), (w_down, first_down, second_down)),
    )
    heads_new, head_sums = moments(
        tuple((i, 0, i, False, i) for i in range(3)) + ((3, 0, 3, True, None),),
        (grad_heads,),
        ((w_qkv, first_qkv, second_qkv), (w_out, first_out, second_out)),
        (layer_out, input_grad),
    )
    own_channels = norm_gains.shape[1]
    ssm_items = [item.reshape(2 * states, own_channels) for item in (ssm_param, first_ssm, second_ssm)]
    small_items = [norm_gains, first_gain, second_gain, *ssm_items]
    *small_new, small_sums = call(
        functools.partial(small_moments_kernel, (6, 8)),
        (small_grads.reshape(2 * states + 2, own_channels), *small_items),
        (*[shaped(item.shape, f32) for item in small_items], shaped((2, LANES), f32)),
    )
    all_sums = everywhere(hidden_sums + head_sums + small_sums, ALL)
    masters = (w_qkv, w_out, w_up, w_down, norm_gains, ssm_items[0])
    news = (*heads_new, *hidden_new, small_new[:3], small_new[3:])
    *weights, norms = call(
        functools.partial(update_kernel, ((0, 1, 2), (3,), (4,), (5,), (6, 7), (8, 9))),
        (all_sums, *masters, *[group[2] for group in news]),
        (*[shaped(item.shape, f32) for item in masters], shaped((2, LANES), f32)),
        time=3.2,
    )
    outputs = [layer_out, input_grad]
    for index, (weight, (first_new, second_new, unused)) in enumerate(zip(weights, news)):
        if index == 4:
            outputs += [weight, first_new, second_new[0], second_new[1]]
        else:
            kept_shape = ssm_param.shape if index == 5 else weight.shape
            outputs += [item.reshape(kept_shape) for item in (weight, first_new, second_new)]
    outputs.append(norms[:, :10])
    return tuple(outputs)


def solution(mesh):
    seq_count, model_count = mesh.shape["seq"], mesh.shape["mp"]
    halves = 2 if HEADS // model_count >= 2 else 1
    sizes = (seq_count // halves, halves, SEQS, halves, model_count // (SEQS * halves))
    fine = Mesh(mesh.devices.reshape(sizes), ALL)
    seq, model = ("sh", "sl"), ("mb", "mq", "ml")
    rows_cols, cols_rows = P(seq, model), P(model, seq)
    token = P(None, seq, None)
    stack = P(None, seq, model)
    gains = P(None, ALL)
    ssm = P(None, None, ALL)
    return jax.shard_map(
        on_device,
        mesh=fine,
        in_specs=(token, token, stack, cols_rows, rows_cols, cols_rows, gains, ssm)
        + (stack,) * 2
        + (cols_rows,) * 2
        + (rows_cols,) * 2
        + (cols_rows,) * 2
        + (gains,) * 2
        + (ssm,) * 2,
        out_specs=(token, token)
        + (stack,) * 3
        + (cols_rows,) * 3
        + (rows_cols,) * 3
        + (cols_rows,) * 3
        + (gains, gains, P(ALL), P(ALL))
        + (ssm,) * 3
        + (P(),),
        check_vma=False,
    )
```

profile of v0, /device:TPU:0, one launch (start us, length us, event | category | flops | bytes accessed | tf_op | source)
XLA Modules:
  0.0 424.8 jit_solution(8496917557943716478)
XLA Ops:
  7.8 2.6 shard_map.363
  12.6 3.0 collective-permute-start.4
  18.6 2.3 dynamic-slice_bitcast_fusion.2
  22.6 7.2 %collective-permute-done.4.refs_4_.refs_1_.refs_9_ = bf16[256,1024]{1,0:T(8,128)(2,1)S(1)} collective-permute-done((bf16[256,1024]{1,0:T(8,128)(2,1)S(1)}, bf16[256,1024]{1,0:T(8,128)(2,1)S(1)}, u32[]{:S(2)}, u32[]{:S(2)}) %collective-permute-start.4) | collective-permute-done | bytes 524320 | tf_op jit(solution)/shard_map/ppermute | solution.py:815
  34.2 4.0 all-to-all-start
  44.7 4.3 %all-to-all-done = f32[32,1,1088]{2,1,0:T(1,128)S(1)} async-done(((f32[32,1,1088]{2,1,0:T(1,128)}), f32[32,1,1088]{2,1,0:T(1,128)S(1)}, u32[]{:S(2)}, u32[]{:S(2)}) %all-to-all-start) | async-done | bytes 139296 | tf_op jit(solution)/shard_map/all_to_all | solution.py:914
  53.8 6.5 %shard_map.365 = (bf16[512,1024]{1,0:T(8,128)(2,1)}, bf16[1024,512]{1,0:T(8,128)(2,1)}, f32[4,512,128]{2,1,0:T(8,128)}, f32[16,8,512]{2,1,0:T(8,128)}, f32[16,512]{1,0:T(8,128)}) custom-call(s32[7]{0:T(128)} %stack.25.refs_0_, bf16[512,1024]{1,0:T(8,128)(2,1)} %broadcast_select_fusion.1.refs_1_.refs_0_, f32[1,1024]{1,0:T(1,128)} %slice.179.refs_2_, ...), custom_call_target="tpu_custom_call" | custom-call | flops 5750000128 | bytes 4526108 | tf_op jit(solution)/shard_map/pallas_call | solution.py:755
  60.3 9.9 %collective-permute-done.9.refs_13_ = bf16[256,1024]{1,0:T(8,128)(2,1)} collective-permute-done((bf16[256,1024]{1,0:T(8,128)(2,1)S(1)}, bf16[256,1024]{1,0:T(8,128)(2,1)}, u32[]{:S(2)}, u32[]{:S(2)}) %collective-permute-start.9) | collective-permute-done | bytes 524320 | tf_op jit(solution)/shard_map/ppermute | solution.py:815
  78.1 3.4 all-to-all-start.1
  83.8 2.7 collective-permute-done.10.refs_9_.refs_17_
  89.4 8.4 %collective-permute-done.11.refs_10_.refs_6_.refs_3_ = bf16[2,256,512]{2,1,0:T(8,128)(2,1)S(1)} collective-permute-done((bf16[2,256,512]{2,1,0:T(8,128)(2,1)S(1)}, bf16[2,256,512]{2,1,0:T(8,128)(2,1)S(1)}, u32[]{:S(2)}, u32[]{:S(2)}) %collective-permute-start.11) | collective-permute-done | bytes 524320 | tf_op jit(solution)/shard_map/ppermute | solution.py:815
  101.7 6.2 %shard_map.368.refs_3_ = bf16[512,512]{1,0:T(8,128)(2,1)} custom-call(s32[7]{0:T(128)} %stack.25.refs_0_, f32[4,512,128]{2,1,0:T(8,128)} %get-tuple-element.115.refs_1_.refs_2_, f32[16,8,512]{2,1,0:T(8,128)} %get-tuple-element.116.refs_2_, bf16[8,16,512]{2,1,0:T(8,128)(2,1)} %copy-done.47, f32[16,512]{1,0:T(8,128)} %get-tuple-element.209.refs_3_.refs_4_.refs_0_.refs_5_, ...), custom_call_target="tpu_custom_call" | custom-call | flops 8049999872 | bytes 2031644 | tf_op jit(solution)/shard_map/pallas_call | solution.py:755
  111.6 14.3 %collective-permute-done.16.refs_11_.refs_8_.refs_15_ = bf16[2,256,512]{2,1,0:T(8,128)(2,1)S(1)} collective-permute-done((bf16[2,256,512]{2,1,0:T(8,128)(2,1)S(1)}, bf16[2,256,512]{2,1,0:T(8,128)(2,1)S(1)}, u32[]{:S(2)}, u32[]{:S(2)}) %collective-permute-start.16) | collective-permute-done | bytes 524320 | tf_op jit(solution)/shard_map/ppermute | solution.py:815
  130.5 6.6 %collective-permute-done.14.refs_8_.refs_5_.refs_12_ = bf16[2,256,512]{2,1,0:T(8,128)(2,1)S(1)} collective-permute-done((bf16[2,256,512]{2,1,0:T(8,128)(2,1)}, bf16[2,256,512]{2,1,0:T(8,128)(2,1)S(1)}, u32[]{:S(2)}, u32[]{:S(2)}) %collective-permute-start.14) | collective-permute-done | bytes 524320 | tf_op jit(solution)/shard_map/ppermute | solution.py:815
  137.1 3.6 collective-permute-done.17.refs_12_.refs_9_.refs_16_
  141.6 7.1 %shard_map.369 = (bf16[1024,512]{1,0:T(8,128)(2,1)}, bf16[1024,512]{1,0:T(8,128)(2,1)}, bf16[3,512,512]{2,1,0:T(8,128)(2,1)}) custom-call(s32[7]{0:T(128)} %stack.25.refs_0_, bf16[512,1024]{1,0:T(8,128)(2,1)} %get-tuple-element.114.refs_1_, bf16[512,1024]{1,0:T(8,128)(2,1)} %broadcast_select_fusion.refs_2_.refs_3_, bf16[512,512]{1,0:T(8,128)(2,1)} %shard_map.368.refs_3_, ...), custom_call_target="tpu_custom_call" | custom-call | flops 1150000000 | bytes 11010076 | tf_op jit(solution)/shard_map/pallas_call | solution.py:755
  149.7 6.3 %shard_map.370 = (bf16[512,1024]{1,0:T(8,128)(2,1)}, bf16[512,512]{1,0:T(8,128)(2,1)}, bf16[4,512,512]{2,1,0:T(8,128)(2,1)}, bf16[4,512,512]{2,1,0:T(8,128)(2,1)}) custom-call(s32[7]{0:T(128)} %stack.25.refs_0_, bf16[3,512,512]{2,1,0:T(8,128)(2,1)} %get-tuple-element.119.refs_1_.refs_6_, bf16[2,256,512]{2,1,0:T(8,128)(2,1)} %copy-done.2, ...), custom_call_target="tpu_custom_call" | custom-call | flops 1150000000 | bytes 11534364 | tf_op jit(solution)/shard_map/pallas_call | solution.py:755
  159.9 4.3 %shard_map.371 = (f32[512,1024]{1,0:T(8,128)}, bf16[512,1024]{1,0:T(8,128)(2,1)}, bf16[1024,512]{1,0:T(8,128)(2,1)}) custom-call(bf16[512,1024]{1,0:T(8,128)(2,1)} %broadcast_select_fusion.1.refs_1_.refs_0_, f32[1,1024]{1,0:T(1,128)} %slice.177.refs_1_.refs_2_, bf16[512,1024]{1,0:T(8,128)(2,1)} %get-tuple-element.120.refs_2_, bf16[512,1024]{1,0:T(8,128)(2,1)} %copy-done.55), custom_call_target="tpu_custom_call" | custom-call | flops 1150000000 | bytes 7344128 | tf_op jit(solution)/shard_map/pallas_call | solution.py:755
  164.2 6.4 %collective-permute-done.25.refs_20_ = bf16[256,1024]{1,0:T(8,128)(2,1)S(1)} collective-permute-done((bf16[256,1024]{1,0:T(8,128)(2,1)}, bf16[256,1024]{1,0:T(8,128)(2,1)S(1)}, u32[]{:S(2)}, u32[]{:S(2)}) %collective-permute-start.25) | collective-permute-done | bytes 524320 | tf_op jit(solution)/shard_map/ppermute | solution.py:815
  171.5 22.0 %shard_map.372 = (bf16[256,1024]{1,0:T(8,128)(2,1)}, bf16[256,1024]{1,0:T(8,128)(2,1)}, bf16[512,1024]{1,0:T(8,128)(2,1)}, bf16[2,2,256,512]{3,2,1,0:T(8,128)(2,...) custom-call(s32[7]{0:T(128)} %stack.25.refs_0_, ...), custom_call_target="tpu_custom_call" | custom-call | flops 20700000256 | bytes 23068700 | tf_op jit(solution)/shard_map/pallas_call | solution.py:755
  197.3 2.2 add_convert_fusion.12.refs_17_
  199.6 15.1 %shard_map.374 = (f32[256,1024]{1,0:T(8,128)}, f32[1,1024]{1,0:T(1,128)}, bf16[512,1024]{1,0:T(8,128)(2,1)}, bf16[512,1024]{1,0:T(8,128)(2,1)}, bf16[512,512]{1,...) custom-call(s32[7]{0:T(128)} %stack.25.refs_0_, ...), custom_call_target="tpu_custom_call" | custom-call | flops 1150000000 | bytes 20979740 | tf_op jit(solution)/shard_map/pallas_call | solution.py:755
  214.7 7.6 %shard_map.375 = (bf16[2,2,256,512]{3,2,1,0:T(8,128)(2,1)}, bf16[2,2,256,512]{3,2,1,0:T(8,128)(2,1)}, bf16[2,2,256,512]{3,2,1,0:T(8,128)(2,1)}, bf16[2,2,256,512]{3,2,1,0:T(8,128)(2,1)}, f32[8,128]{1,0:T(8,128)}) custom-call(s32[7]{0:T(128)} %stack.25.refs_0_, bf16[512,1024]{1,0:T(8,128)(2,1)} %get-tuple-element.133.refs_1_, ...), custom_call_target="tpu_custom_call" | custom-call | flops 9200000000 | bytes 9437212 | tf_op jit(solution)/shard_map/pallas_call | solution.py:755
  223.7 2.6 add_convert_fusion.10.refs_5_
  233.3 6.4 %shard_map.376 = (f32[4,512,128]{2,1,0:T(8,128)}, f32[2,16,8,512]{3,2,1,0:T(8,128)}, f32[2,16,512]{2,1,0:T(8,128)}, f32[8,128]{1,0:T(8,128)}) custom-call(f32[16,512]{1,0:T(8,128)} %get-tuple-element.209.refs_3_.refs_4_.refs_0_.refs_5_, bf16[512,512]{1,0:T(8,128)(2,1)} %get-tuple-element.131.refs_1_, bf16[512,512]{1,0:T(8,128)(2,1)} %collective-permute-done.29.refs_2_, ...), custom_call_target="tpu_custom_call" | custom-call | flops 1150000000 | bytes 2719744 | tf_op jit(solution)/shard_map/pallas_call | solution.py:755
  246.8 18.5 %collective-permute-done.32 = bf16[1,2,256,512]{3,2,1,0:T(8,128)(2,1)S(1)} collective-permute-done((bf16[1,2,256,512]{3,2,1,0:T(8,128)(2,1)S(1)}, bf16[1,2,256,512]{3,2,1,0:T(8,128)(2,1)S(1)}, u32[]{:S(2)}, u32[]{:S(2)}) %collective-permute-start.32) | collective-permute-done | bytes 524320 | tf_op jit(solution)/shard_map/ppermute | solution.py:815
  270.6 3.4 all-to-all-start.2
  274.3 2.9 add_convert_fusion.6.refs_1_
  284.8 12.8 %shard_map.380 = (bf16[256,1024]{1,0:T(8,128)(2,1)}, bf16[256,1024]{1,0:T(8,128)(2,1)}, f32[2,16,512]{2,1,0:T(8,128)}, f32[8,128]{1,0:T(8,128)}) custom-call(s32[7]{0:T(128)} %stack.25.refs_0_, f32[4,512,128]{2,1,0:T(8,128)} %get-tuple-element.145.refs_1_, f32[4,512,128]{2,1,0:T(8,128)} %get-tuple-element.115.refs_1_.refs_2_, ...), custom_call_target="tpu_custom_call" | custom-call | flops 1150000000 | bytes 5111836 | tf_op jit(solution)/shard_map/pallas_call | solution.py:755
  298.8 2.7 fusion.1.refs_8_.refs_1_
  304.0 3.5 shard_map.381
  311.0 2.3 collective-permute-start.43
  315.9 5.9 %collective-permute-done.43 = bf16[256,512]{1,0:T(8,128)(2,1)S(1)} collective-permute-done((bf16[256,512]{1,0:T(8,128)(2,1)S(1)}, bf16[256,512]{1,0:T(8,128)(2,1)S(1)}, u32[]{:S(2)}, u32[]{:S(2)}) %collective-permute-start.43) | collective-permute-done | bytes 262176 | tf_op jit(solution)/shard_map/ppermute | solution.py:815
  322.9 4.4 %collective-permute-start.44 = (bf16[256,512]{1,0:T(8,128)(2,1)S(1)}, bf16[256,512]{1,0:T(8,128)(2,1)S(1)}, u32[]{:S(2)}, u32[]{:S(2)}) collective-permute-start(bf16[256,512]{1,0:T(8,128)(2,1)S(1)} %fusion.5), channel_id=1, source_target_pairs={{0,3},{1,0},{2,1},{3,2},{4,7},{5,4},{6,5},{7,6},{8,11},{9,8},{10,9... | collective-permute-start | bytes 786440 | tf_op jit(solution)/shard_map/ppermute | solution.py:815
  327.3 6.1 %collective-permute-done.50 = bf16[2,2,256,512]{3,2,1,0:T(8,128)(2,1)} collective-permute-done((bf16[2,2,256,512]{3,2,1,0:T(8,128)(2,1)}, bf16[2,2,256,512]{3,2,1,0:T(8,128)(2,1)}, u32[]{:S(2)}, u32[]{:S(2)}) %collective-permute-start.50) | collective-permute-done | bytes 1048608 | tf_op jit(solution)/shard_map/ppermute | solution.py:815
  336.5 3.4 shard_map.373.refs_9_
  339.9 3.2 collective-permute-done.44
  344.1 6.2 %collective-permute-done.51 = bf16[1,2,256,512]{3,2,1,0:T(8,128)(2,1)S(1)} collective-permute-done((bf16[1,2,256,512]{3,2,1,0:T(8,128)(2,1)S(1)}, bf16[1,2,256,512]{3,2,1,0:T(8,128)(2,1)S(1)}, u32[]{:S(2)}, u32[]{:S(2)}) %collective-permute-start.51) | collective-permute-done | bytes 524320 | tf_op jit(solution)/shard_map/ppermute | solution.py:815
  352.5 12.1 %collective-permute-done.45 = bf16[256,512]{1,0:T(8,128)(2,1)S(1)} collective-permute-done((bf16[256,512]{1,0:T(8,128)(2,1)S(1)}, bf16[256,512]{1,0:T(8,128)(2,1)S(1)}, u32[]{:S(2)}, u32[]{:S(2)}) %collective-permute-start.45) | collective-permute-done | bytes 262176 | tf_op jit(solution)/shard_map/ppermute | solution.py:815
  364.8 5.0 %collective-permute-done.52 = bf16[256,512]{1,0:T(8,128)(2,1)S(1)} collective-permute-done((bf16[256,512]{1,0:T(8,128)(2,1)S(1)}, bf16[256,512]{1,0:T(8,128)(2,1)S(1)}, u32[]{:S(2)}, u32[]{:S(2)}) %collective-permute-start.52) | collective-permute-done | bytes 262176 | tf_op jit(solution)/shard_map/ppermute | solution.py:815
  373.9 5.2 %all-to-all-start.3 = ((f32[32,1,1088]{2,1,0:T(1,128)}), f32[32,1,1088]{2,1,0:T(1,128)S(1)}, u32[]{:S(2)}, u32[]{:S(2)}) async-start(f32[32,1,1088]{2,1,0:T(1,128)} %reshape.184), calls=%async_computation.3 | async-start | bytes 294912 | tf_op jit(solution)/shard_map/all_to_all | solution.py:1195
  380.8 3.8 collective-permute-start.54
  385.3 5.0 %shard_map.385 = (f32[128,1024]{1,0:T(8,128)}, f32[128,1024]{1,0:T(8,128)}, f32[128,1024]{1,0:T(8,128)}, f32[1024,128]{1,0:T(8,128)}, f32[1024,128]{1,0:T(8,128)...) custom-call(s32[7]{0:T(128)} %stack.25.refs_0_, bf16[256,512]{1,0:T(8,128)(2,1)} %copy-done.35, ...), custom_call_target="tpu_custom_call" | custom-call | flops 4600000000 | bytes 7078940 | tf_op jit(solution)/shard_map/pallas_call | solution.py:755
  394.5 4.2 shard_map.382.refs_10_
  399.3 3.2 shard_map.386
  403.9 3.0 all-to-all-start.4
  407.4 6.8 %all-to-all-done.4.refs_0_ = f32[32,2,128]{2,1,0:T(2,128)S(1)} async-done(((f32[32,2,128]{2,1,0:T(2,128)}), f32[32,2,128]{2,1,0:T(2,128)S(1)}, u32[]{:S(2)}, u32[]{:S(2)}) %all-to-all-start.4) | async-done | bytes 32800 | tf_op jit(solution)/shard_map/all_to_all | solution.py:914
  414.8 3.2 shard_map.389
  (301 shorter events, 117.8 us)
Async XLA Ops:
  7.2 65.9 %all-gather.7.cloned.1.call-start = ((), (), s32[]{:S(2)}) async-start(), calls=%async_computation.5 | async-start | bytes 1310720 | tf_op jit(solution)/shard_map/all_gather | solution.py:938
  11.9 31.1 %collective-permute-start = (bf16[512,1024]{1,0:T(8,128)(2,1)}, bf16[512,1024]{1,0:T(8,128)(2,1)}, u32[]{:S(2)}, u32[]{:S(2)}) collective-permute-start(bf16[512,1024]{1,0:T(8,128)(2,1)} %dynamic-slice_bitcast_fusion.3), channel_id=1, source_target_pairs={{0,4},{4,0},{1,5},{5,1},{2,6},{6,2},{3,7},{7,3},{8,12},{12,8},{9,1... | collective-permute-start | bytes 3145736 | tf_op jit(solution)/shard_map/ppermute | solution.py:815
  12.6 17.2 %collective-permute-start.4 = (bf16[256,1024]{1,0:T(8,128)(2,1)S(1)}, bf16[256,1024]{1,0:T(8,128)(2,1)S(1)}, u32[]{:S(2)}, u32[]{:S(2)}) collective-permute-start(bf16[256,1024]{1,0:T(8,128)(2,1)S(1)} %maximum_select_fusion.refs_5_), channel_id=1, source_target_pairs={{0,1},{1,2},{2,3},{3,0},{4,5},{5,6},{6,7},{7,4},{8,9},{9,10},{10,1... | collective-permute-start | bytes 1572872 | tf_op jit(solution)/shard_map/ppermute | solution.py:815
  15.6 15.1 %collective-permute-start.2 = (bf16[256,1024]{1,0:T(8,128)(2,1)S(1)}, bf16[256,1024]{1,0:T(8,128)(2,1)}, u32[]{:S(2)}, u32[]{:S(2)}) collective-permute-start(bf16[256,1024]{1,0:T(8,128)(2,1)S(1)} %maximum_select_fusion.refs_5_), channel_id=1, source_target_pairs={{0,8},{8,0},{16,24},{24,16},{1,9},{9,1},{17,25},{25,17},{2,10},{10... | collective-permute-start | bytes 1572872 | tf_op jit(solution)/shard_map/ppermute | solution.py:815
  20.9 32.9 %collective-permute-start.5 = (bf16[512,1024]{1,0:T(8,128)(2,1)}, bf16[512,1024]{1,0:T(8,128)(2,1)}, u32[]{:S(2)}, u32[]{:S(2)}) collective-permute-start(bf16[512,1024]{1,0:T(8,128)(2,1)} %dynamic-slice_bitcast_fusion.2), channel_id=1, source_target_pairs={{0,4},{4,0},{1,5},{5,1},{2,6},{6,2},{3,7},{7,3},{8,12},{12,8},{9,1... | collective-permute-start | bytes 3145736 | tf_op jit(solution)/shard_map/ppermute | solution.py:815
  38.2 32.0 %collective-permute-start.9 = (bf16[256,1024]{1,0:T(8,128)(2,1)S(1)}, bf16[256,1024]{1,0:T(8,128)(2,1)}, u32[]{:S(2)}, u32[]{:S(2)}) collective-permute-start(bf16[256,1024]{1,0:T(8,128)(2,1)S(1)} %copy-done.39), channel_id=1, source_target_pairs={{0,1},{1,2},{2,3},{3,0},{4,5},{5,6},{6,7},{7,4},{8,9},{9,10},{10,1... | collective-permute-start | bytes 1572872 | tf_op jit(solution)/shard_map/ppermute | solution.py:815
  40.0 34.4 %collective-permute-start.8 = (bf16[256,1024]{1,0:T(8,128)(2,1)S(1)}, bf16[256,1024]{1,0:T(8,128)(2,1)}, u32[]{:S(2)}, u32[]{:S(2)}) collective-permute-start(bf16[256,1024]{1,0:T(8,128)(2,1)S(1)} %copy-done.39), channel_id=1, source_target_pairs={{0,16},{8,24},{16,0},{24,8},{1,17},{9,25},{17,1},{25,9},{2,18},{10... | collective-permute-start | bytes 1572872 | tf_op jit(solution)/shard_map/ppermute | solution.py:815
  41.5 34.5 %collective-permute-start.7 = (bf16[256,1024]{1,0:T(8,128)(2,1)S(1)}, bf16[256,1024]{1,0:T(8,128)(2,1)}, u32[]{:S(2)}, u32[]{:S(2)}) collective-permute-start(bf16[256,1024]{1,0:T(8,128)(2,1)S(1)} %copy-done.39), channel_id=1, source_target_pairs={{0,8},{8,0},{16,24},{24,16},{1,9},{9,1},{17,25},{25,17},{2,10},{10... | collective-permute-start | bytes 1572872 | tf_op jit(solution)/shard_map/ppermute | solution.py:815
  42.9 38.8 %collective-permute-start.6 = (bf16[256,1024]{1,0:T(8,128)(2,1)}, bf16[256,1024]{1,0:T(8,128)(2,1)}, u32[]{:S(2)}, u32[]{:S(2)}) collective-permute-start(bf16[256,1024]{1,0:T(8,128)(2,1)} %collective-permute-done.2.refs_2_.refs_6_), channel_id=1, source_target_pairs={{0,16},{8,24},{16,0},{24,8},{1,17},{9,25},{17,1},{25,9},{2,18},{10... | collective-permute-start | bytes 1572872 | tf_op jit(solution)/shard_map/ppermute | solution.py:815
  70.2 16.4 %collective-permute-start.10 = (bf16[256,1024]{1,0:T(8,128)(2,1)}, bf16[256,1024]{1,0:T(8,128)(2,1)}, u32[]{:S(2)}, u32[]{:S(2)}) collective-permute-start(bf16[256,1024]{1,0:T(8,128)(2,1)} %collective-permute-done.9.refs_13_), channel_id=1, source_target_pairs={{0,1},{1,2},{2,3},{3,0},{4,5},{5,6},{6,7},{7,4},{8,9},{9,10},{10,1... | collective-permute-start | bytes 1572872 | tf_op jit(solution)/shard_map/ppermute | solution.py:815
  70.9 17.0 %collective-permute-start.19 = (bf16[256,1024]{1,0:T(8,128)(2,1)}, bf16[256,1024]{1,0:T(8,128)(2,1)}, u32[]{:S(2)}, u32[]{:S(2)}) collective-permute-start(bf16[256,1024]{1,0:T(8,128)(2,1)} %collective-permute-done.9.refs_13_), channel_id=1, source_target_pairs={{0,8},{8,0},{16,24},{24,16},{1,9},{9,1},{17,25},{25,17},{2,10},{10... | collective-permute-start | bytes 1572872 | tf_op jit(solution)/shard_map/ppermute | solution.py:815
  74.4 23.5 %collective-permute-start.11 = (bf16[2,256,512]{2,1,0:T(8,128)(2,1)S(1)}, bf16[2,256,512]{2,1,0:T(8,128)(2,1)S(1)}, u32[]{:S(2)}, u32[]{:S(2)}) collective-permute-start(bf16[2,256,512]{2,1,0:T(8,128)(2,1)S(1)} %get-tuple-element.205.refs_5_.refs_2_.refs_9_), channel_id=1, source_target_pairs={{0,8},{8,0},{16,24},{24,16},{1,9},{9,1},{17,25},{25,17},{2,10},{10... | collective-permute-start | bytes 1572872 | tf_op jit(solution)/shard_map/ppermute | solution.py:815
  75.9 23.7 %collective-permute-start.12 = (bf16[2,256,512]{2,1,0:T(8,128)(2,1)S(1)}, bf16[2,256,512]{2,1,0:T(8,128)(2,1)S(1)}, u32[]{:S(2)}, u32[]{:S(2)}) collective-permute-start(bf16[2,256,512]{2,1,0:T(8,128)(2,1)S(1)} %get-tuple-element.205.refs_5_.refs_2_.refs_9_), channel_id=1, source_target_pairs={{0,16},{8,24},{16,0},{24,8},{1,17},{9,25},{17,1},{25,9},{2,18},{10... | collective-permute-start | bytes 1572872 | tf_op jit(solution)/shard_map/ppermute | solution.py:815
  78.1 23.0 %all-to-all-start.1 = ((bf16[8,16,512]{2,1,0:T(8,128)(2,1)}), bf16[8,16,512]{2,1,0:T(8,128)(2,1)S(1)}, u32[]{:S(2)}, u32[]{:S(2)}) async-start(bf16[8,16,512]{2,1,0:T(8,128)(2,1)} %broadcast_in_dim.11), calls=%async_computation.1 | async-start | bytes 262144 | tf_op jit(solution)/shard_map/all_to_all | solution.py:914
  81.5 203.3 %all-gather.9.cloned.1.call-start = ((), (), s32[]{:S(2)}) async-start(), calls=%async_computation.6 | async-start | bytes 2621440 | tf_op jit(solution)/shard_map/all_gather | solution.py:1081
  81.8 26.2 %collective-permute-start.20 = (bf16[256,1024]{1,0:T(8,128)(2,1)}, bf16[256,1024]{1,0:T(8,128)(2,1)}, u32[]{:S(2)}, u32[]{:S(2)}) collective-permute-start(bf16[256,1024]{1,0:T(8,128)(2,1)} %collective-permute-done.9.refs_13_), channel_id=1, source_target_pairs={{0,16},{8,24},{16,0},{24,8},{1,17},{9,25},{17,1},{25,9},{2,18},{10... | collective-permute-start | bytes 1572872 | tf_op jit(solution)/shard_map/ppermute | solution.py:815
  86.6 23.4 %collective-permute-start.18 = (bf16[256,1024]{1,0:T(8,128)(2,1)}, bf16[256,1024]{1,0:T(8,128)(2,1)}, u32[]{:S(2)}, u32[]{:S(2)}) collective-permute-start(bf16[256,1024]{1,0:T(8,128)(2,1)} %collective-permute-done.8.refs_8_.refs_11_), channel_id=1, source_target_pairs={{0,8},{8,0},{16,24},{24,16},{1,9},{9,1},{17,25},{25,17},{2,10},{10... | collective-permute-start | bytes 1572872 | tf_op jit(solution)/shard_map/ppermute | solution.py:815
  88.0 38.5 %collective-permute-start.21 = (bf16[256,1024]{1,0:T(8,128)(2,1)}, bf16[256,1024]{1,0:T(8,128)(2,1)}, u32[]{:S(2)}, u32[]{:S(2)}) collective-permute-start(bf16[256,1024]{1,0:T(8,128)(2,1)} %collective-permute-done.19.refs_14_), channel_id=1, source_target_pairs={{0,16},{8,24},{16,0},{24,8},{1,17},{9,25},{17,1},{25,9},{2,18},{10... | collective-permute-start | bytes 1572872 | tf_op jit(solution)/shard_map/ppermute | solution.py:815
  97.9 28.0 %collective-permute-start.16 = (bf16[2,256,512]{2,1,0:T(8,128)(2,1)S(1)}, bf16[2,256,512]{2,1,0:T(8,128)(2,1)S(1)}, u32[]{:S(2)}, u32[]{:S(2)}) collective-permute-start(bf16[2,256,512]{2,1,0:T(8,128)(2,1)S(1)} %get-tuple-element.204.refs_9_.refs_6_.refs_13_), channel_id=1, source_target_pairs={{0,16},{8,24},{16,0},{24,8},{1,17},{9,25},{17,1},{25,9},{2,18},{10... | collective-permute-start | bytes 1572872 | tf_op jit(solution)/shard_map/ppermute | solution.py:815
  99.6 28.3 %collective-permute-start.15 = (bf16[2,256,512]{2,1,0:T(8,128)(2,1)S(1)}, bf16[2,256,512]{2,1,0:T(8,128)(2,1)S(1)}, u32[]{:S(2)}, u32[]{:S(2)}) collective-permute-start(bf16[2,256,512]{2,1,0:T(8,128)(2,1)S(1)} %get-tuple-element.204.refs_9_.refs_6_.refs_13_), channel_id=1, source_target_pairs={{0,8},{8,0},{16,24},{24,16},{1,9},{9,1},{17,25},{25,17},{2,10},{10... | collective-permute-start | bytes 1572872 | tf_op jit(solution)/shard_map/ppermute | solution.py:815
  108.0 22.6 %collective-permute-start.13 = (bf16[512,512]{1,0:T(8,128)(2,1)}, bf16[512,512]{1,0:T(8,128)(2,1)S(1)}, u32[]{:S(2)}, u32[]{:S(2)}) collective-permute-start(bf16[512,512]{1,0:T(8,128)(2,1)} %shard_map.368.refs_3_), channel_id=1, source_target_pairs={{0,4},{4,0},{1,5},{5,1},{2,6},{6,2},{3,7},{7,3},{8,12},{12,8},{9,1... | collective-permute-start | bytes 1572872 | tf_op jit(solution)/shard_map/ppermute | solution.py:815
  109.9 27.2 %collective-permute-start.14 = (bf16[2,256,512]{2,1,0:T(8,128)(2,1)}, bf16[2,256,512]{2,1,0:T(8,128)(2,1)S(1)}, u32[]{:S(2)}, u32[]{:S(2)}) collective-permute-start(bf16[2,256,512]{2,1,0:T(8,128)(2,1)} %copy-done.10), channel_id=1, source_target_pairs={{0,16},{8,24},{16,0},{24,8},{1,17},{9,25},{17,1},{25,9},{2,18},{10... | collective-permute-start | bytes 1572872 | tf_op jit(solution)/shard_map/ppermute | solution.py:815
  125.9 14.9 %collective-permute-start.17 = (bf16[2,256,512]{2,1,0:T(8,128)(2,1)S(1)}, bf16[2,256,512]{2,1,0:T(8,128)(2,1)S(1)}, u32[]{:S(2)}, u32[]{:S(2)}) collective-permute-start(bf16[2,256,512]{2,1,0:T(8,128)(2,1)S(1)} %collective-permute-done.16.refs_11_.refs_8_.refs_15_), channel_id=1, source_target_pairs={{0,8},{8,0},{16,24},{24,16},{1,9},{9,1},{17,25},{25,17},{2,10},{10... | collective-permute-start | bytes 1572872 | tf_op jit(solution)/shard_map/ppermute | solution.py:815
  126.5 22.2 %collective-permute-start.23 = (bf16[256,1024]{1,0:T(8,128)(2,1)}, bf16[256,1024]{1,0:T(8,128)(2,1)S(1)}, u32[]{:S(2)}, u32[]{:S(2)}) collective-permute-start(bf16[256,1024]{1,0:T(8,128)(2,1)} %collective-permute-done.10.refs_9_.refs_17_), channel_id=1, source_target_pairs={{0,16},{8,24},{16,0},{24,8},{1,17},{9,25},{17,1},{25,9},{2,18},{10... | collective-permute-start | bytes 1572872 | tf_op jit(solution)/shard_map/ppermute | solution.py:815
  127.9 20.8 %collective-permute-start.22 = (bf16[256,1024]{1,0:T(8,128)(2,1)}, bf16[256,1024]{1,0:T(8,128)(2,1)S(1)}, u32[]{:S(2)}, u32[]{:S(2)}) collective-permute-start(bf16[256,1024]{1,0:T(8,128)(2,1)} %collective-permute-done.10.refs_9_.refs_17_), channel_id=1, source_target_pairs={{0,8},{8,0},{16,24},{24,16},{1,9},{9,1},{17,25},{25,17},{2,10},{10... | collective-permute-start | bytes 1572872 | tf_op jit(solution)/shard_map/ppermute | solution.py:815
  194.1 33.6 %collective-permute-start.30 = (bf16[2,2,256,512]{3,2,1,0:T(8,128)(2,1)}, bf16[2,2,256,512]{3,2,1,0:T(8,128)(2,1)S(1)}, u32[]{:S(2)}, u32[]{:S(2)}) collective-permute-start(bf16[2,2,256,512]{3,2,1,0:T(8,128)(2,1)} %get-tuple-element.142), channel_id=1, source_target_pairs={{0,16},{8,24},{16,0},{24,8},{1,17},{9,25},{17,1},{25,9},{2,18},{10... | collective-permute-start | bytes 3145736 | tf_op jit(solution)/shard_map/ppermute | solution.py:815
  195.5 28.1 %collective-permute-start.31 = (bf16[2,2,256,512]{3,2,1,0:T(8,128)(2,1)}, bf16[2,2,256,512]{3,2,1,0:T(8,128)(2,1)}, u32[]{:S(2)}, u32[]{:S(2)}) collective-permute-start(bf16[2,2,256,512]{3,2,1,0:T(8,128)(2,1)} %get-tuple-element.144), channel_id=1, source_target_pairs={{0,8},{8,0},{16,24},{24,16},{1,9},{9,1},{17,25},{25,17},{2,10},{10... | collective-permute-start | bytes 3145736 | tf_op jit(solution)/shard_map/ppermute | solution.py:815
  226.3 16.2 %collective-permute-start.33 = (bf16[1,2,256,512]{3,2,1,0:T(8,128)(2,1)}, bf16[1,2,256,512]{3,2,1,0:T(8,128)(2,1)}, u32[]{:S(2)}, u32[]{:S(2)}) collective-permute-start(bf16[1,2,256,512]{3,2,1,0:T(8,128)(2,1)} %add_convert_fusion.10.refs_5_), channel_id=1, source_target_pairs={{0,16},{8,24},{16,0},{24,8},{1,17},{9,25},{17,1},{25,9},{2,18},{10... | collective-permute-start | bytes 1572872 | tf_op jit(solution)/shard_map/ppermute | solution.py:815
  228.7 39.0 %collective-permute-start.35 = (bf16[2,2,256,512]{3,2,1,0:T(8,128)(2,1)}, bf16[2,2,256,512]{3,2,1,0:T(8,128)(2,1)S(1)}, u32[]{:S(2)}, u32[]{:S(2)}) collective-permute-start(bf16[2,2,256,512]{3,2,1,0:T(8,128)(2,1)} %get-tuple-element.151), channel_id=1, source_target_pairs={{0,8},{8,0},{16,24},{24,16},{1,9},{9,1},{17,25},{25,17},{2,10},{10... | collective-permute-start | bytes 3145736 | tf_op jit(solution)/shard_map/ppermute | solution.py:815
  229.1 38.5 %collective-permute-start.34 = (bf16[2,2,256,512]{3,2,1,0:T(8,128)(2,1)}, bf16[2,2,256,512]{3,2,1,0:T(8,128)(2,1)S(1)}, u32[]{:S(2)}, u32[]{:S(2)}) collective-permute-start(bf16[2,2,256,512]{3,2,1,0:T(8,128)(2,1)} %get-tuple-element.150), channel_id=1, source_target_pairs={{0,16},{8,24},{16,0},{24,8},{1,17},{9,25},{17,1},{25,9},{2,18},{10... | collective-permute-start | bytes 3145736 | tf_op jit(solution)/shard_map/ppermute | solution.py:815
  231.8 33.6 %collective-permute-start.32 = (bf16[1,2,256,512]{3,2,1,0:T(8,128)(2,1)S(1)}, bf16[1,2,256,512]{3,2,1,0:T(8,128)(2,1)S(1)}, u32[]{:S(2)}, u32[]{:S(2)}) collective-permute-start(bf16[1,2,256,512]{3,2,1,0:T(8,128)(2,1)S(1)} %add_convert_fusion.11.refs_4_), channel_id=1, source_target_pairs={{0,8},{8,0},{16,24},{24,16},{1,9},{9,1},{17,25},{25,17},{2,10},{10... | collective-permute-start | bytes 1572872 | tf_op jit(solution)/shard_map/ppermute | solution.py:815
  244.8 38.0 %collective-permute-start.38 = (bf16[256,512]{1,0:T(8,128)(2,1)}, bf16[256,512]{1,0:T(8,128)(2,1)}, u32[]{:S(2)}, u32[]{:S(2)}) collective-permute-start(bf16[256,512]{1,0:T(8,128)(2,1)} %get-tuple-element.206), channel_id=1, source_target_pairs={{0,2},{1,3},{2,0},{3,1},{4,6},{5,7},{6,4},{7,5},{8,10},{9,11},{10,... | collective-permute-start | bytes 786440 | tf_op jit(solution)/shard_map/ppermute | solution.py:815
  246.2 36.7 %collective-permute-start.39 = (bf16[256,512]{1,0:T(8,128)(2,1)}, bf16[256,512]{1,0:T(8,128)(2,1)}, u32[]{:S(2)}, u32[]{:S(2)}) collective-permute-start(bf16[256,512]{1,0:T(8,128)(2,1)} %get-tuple-element.207), channel_id=1, source_target_pairs={{0,1},{1,2},{2,3},{3,0},{4,5},{5,6},{6,7},{7,4},{8,9},{9,10},{10,1... | collective-permute-start | bytes 786440 | tf_op jit(solution)/shard_map/ppermute | solution.py:815
  266.3 16.5 %collective-permute-start.37 = (bf16[256,512]{1,0:T(8,128)(2,1)}, bf16[256,512]{1,0:T(8,128)(2,1)}, u32[]{:S(2)}, u32[]{:S(2)}) collective-permute-start(bf16[256,512]{1,0:T(8,128)(2,1)} %slice_bitcast_fusion.6), channel_id=1, source_target_pairs={{0,3},{1,0},{2,1},{3,2},{4,7},{5,4},{6,5},{7,6},{8,11},{9,8},{10,9... | collective-permute-start | bytes 786440 | tf_op jit(solution)/shard_map/ppermute | solution.py:815
  274.0 105.1 %all-gather.11.cloned.1.call-start = ((), (), s32[]{:S(2)}) async-start(), calls=%async_computation.7 | async-start | bytes 2621440 | tf_op jit(solution)/shard_map/all_gather | solution.py:1184
  281.7 17.2 %collective-permute-start.41 = (bf16[1,2,256,512]{3,2,1,0:T(8,128)(2,1)}, bf16[1,2,256,512]{3,2,1,0:T(8,128)(2,1)}, u32[]{:S(2)}, u32[]{:S(2)}) collective-permute-start(bf16[1,2,256,512]{3,2,1,0:T(8,128)(2,1)} %get-tuple-element.157.refs_9_), channel_id=1, source_target_pairs={{0,16},{8,24},{16,0},{24,8},{1,17},{9,25},{17,1},{25,9},{2,18},{10... | collective-permute-start | bytes 1572872 | tf_op jit(solution)/shard_map/ppermute | solution.py:815
  282.2 19.4 %collective-permute-start.40 = (bf16[1,2,256,512]{3,2,1,0:T(8,128)(2,1)}, bf16[1,2,256,512]{3,2,1,0:T(8,128)(2,1)S(1)}, u32[]{:S(2)}, u32[]{:S(2)}) collective-permute-start(bf16[1,2,256,512]{3,2,1,0:T(8,128)(2,1)} %get-tuple-element.156.refs_8_), channel_id=1, source_target_pairs={{0,8},{8,0},{16,24},{24,16},{1,9},{9,1},{17,25},{25,17},{2,10},{10... | collective-permute-start | bytes 1572872 | tf_op jit(solution)/shard_map/ppermute | solution.py:815
  307.5 25.9 %collective-permute-start.50 = (bf16[2,2,256,512]{3,2,1,0:T(8,128)(2,1)}, bf16[2,2,256,512]{3,2,1,0:T(8,128)(2,1)}, u32[]{:S(2)}, u32[]{:S(2)}) collective-permute-start(bf16[2,2,256,512]{3,2,1,0:T(8,128)(2,1)} %get-tuple-element.165.refs_3_), channel_id=1, source_target_pairs={{0,8},{8,0},{16,24},{24,16},{1,9},{9,1},{17,25},{25,17},{2,10},{10... | collective-permute-start | bytes 3145736 | tf_op jit(solution)/shard_map/ppermute | solution.py:815
  309.2 27.3 %collective-permute-start.27 = (bf16[2,256,1024]{2,1,0:T(8,128)(2,1)S(1)}, bf16[2,256,1024]{2,1,0:T(8,128)(2,1)}, u32[]{:S(2)}, u32[]{:S(2)}) collective-permute-start(bf16[2,256,1024]{2,1,0:T(8,128)(2,1)S(1)} %dynamic-slice_bitcast_fusion.1), channel_id=1, source_target_pairs={{0,4},{4,0},{1,5},{5,1},{2,6},{6,2},{3,7},{7,3},{8,12},{12,8},{9,1... | collective-permute-start | bytes 3145736 | tf_op jit(solution)/shard_map/ppermute | solution.py:815
  313.3 71.4 %collective-permute-start.47 = (bf16[128,512]{1,0:T(8,128)(2,1)S(1)}, bf16[128,512]{1,0:T(8,128)(2,1)S(1)}, u32[]{:S(2)}, u32[]{:S(2)}) collective-permute-start(bf16[128,512]{1,0:T(8,128)(2,1)S(1)} %constant_dynamic-slice_fusion.1), channel_id=1, source_target_pairs={{0,4},{4,0},{1,5},{5,1},{2,6},{6,2},{3,7},{7,3},{8,12},{12,8},{9,1... | collective-permute-start | bytes 393224 | tf_op jit(solution)/shard_map/ppermute | solution.py:815
  313.4 29.7 %collective-permute-start.48 = (bf16[2,2,256,512]{3,2,1,0:T(8,128)(2,1)S(1)}, bf16[2,2,256,512]{3,2,1,0:T(8,128)(2,1)S(1)}, u32[]{:S(2)}, u32[]{:S(2)}) collective-permute-start(bf16[2,2,256,512]{3,2,1,0:T(8,128)(2,1)S(1)} %copy-done.20), channel_id=1, source_target_pairs={{0,16},{8,24},{16,0},{24,8},{1,17},{9,25},{17,1},{25,9},{2,18},{10... | collective-permute-start | bytes 3145736 | tf_op jit(solution)/shard_map/ppermute | solution.py:815
  322.9 20.1 %collective-permute-start.44 = (bf16[256,512]{1,0:T(8,128)(2,1)S(1)}, bf16[256,512]{1,0:T(8,128)(2,1)S(1)}, u32[]{:S(2)}, u32[]{:S(2)}) collective-permute-start(bf16[256,512]{1,0:T(8,128)(2,1)S(1)} %fusion.5), channel_id=1, source_target_pairs={{0,3},{1,0},{2,1},{3,2},{4,7},{5,4},{6,5},{7,6},{8,11},{9,8},{10,9... | collective-permute-start | bytes 786440 | tf_op jit(solution)/shard_map/ppermute | solution.py:815
  335.3 15.0 %collective-permute-start.51 = (bf16[1,2,256,512]{3,2,1,0:T(8,128)(2,1)S(1)}, bf16[1,2,256,512]{3,2,1,0:T(8,128)(2,1)S(1)}, u32[]{:S(2)}, u32[]{:S(2)}) collective-permute-start(bf16[1,2,256,512]{3,2,1,0:T(8,128)(2,1)S(1)} %add_convert_fusion.1), channel_id=1, source_target_pairs={{0,16},{8,24},{16,0},{24,8},{1,17},{9,25},{17,1},{25,9},{2,18},{10... | collective-permute-start | bytes 1572872 | tf_op jit(solution)/shard_map/ppermute | solution.py:815
  343.1 21.5 %collective-permute-start.45 = (bf16[256,512]{1,0:T(8,128)(2,1)S(1)}, bf16[256,512]{1,0:T(8,128)(2,1)S(1)}, u32[]{:S(2)}, u32[]{:S(2)}) collective-permute-start(bf16[256,512]{1,0:T(8,128)(2,1)S(1)} %fusion.6), channel_id=1, source_target_pairs={{0,3},{1,0},{2,1},{3,2},{4,7},{5,4},{6,5},{7,6},{8,11},{9,8},{10,9... | collective-permute-start | bytes 786440 | tf_op jit(solution)/shard_map/ppermute | solution.py:815
  344.0 26.1 %collective-permute-start.49 = (bf16[1,2,256,512]{3,2,1,0:T(8,128)(2,1)S(1)}, bf16[1,2,256,512]{3,2,1,0:T(8,128)(2,1)S(1)}, u32[]{:S(2)}, u32[]{:S(2)}) collective-permute-start(bf16[1,2,256,512]{3,2,1,0:T(8,128)(2,1)S(1)} %add_convert_fusion.3), channel_id=1, source_target_pairs={{0,8},{8,0},{16,24},{24,16},{1,9},{9,1},{17,25},{25,17},{2,10},{10... | collective-permute-start | bytes 1572872 | tf_op jit(solution)/shard_map/ppermute | solution.py:815
  351.6 18.2 %collective-permute-start.52 = (bf16[256,512]{1,0:T(8,128)(2,1)S(1)}, bf16[256,512]{1,0:T(8,128)(2,1)S(1)}, u32[]{:S(2)}, u32[]{:S(2)}) collective-permute-start(bf16[256,512]{1,0:T(8,128)(2,1)S(1)} %slice_bitcast_fusion), channel_id=1, source_target_pairs={{0,3},{1,0},{2,1},{3,2},{4,7},{5,4},{6,5},{7,6},{8,11},{9,8},{10,9... | collective-permute-start | bytes 786440 | tf_op jit(solution)/shard_map/ppermute | solution.py:815
  364.7 20.0 %collective-permute-start.46 = (bf16[128,512]{1,0:T(8,128)(2,1)S(1)}, bf16[128,512]{1,0:T(8,128)(2,1)}, u32[]{:S(2)}, u32[]{:S(2)}) collective-permute-start(bf16[128,512]{1,0:T(8,128)(2,1)S(1)} %constant_dynamic-slice_fusion.2), channel_id=1, source_target_pairs={{0,4},{4,0},{1,5},{5,1},{2,6},{6,2},{3,7},{7,3},{8,12},{12,8},{9,1... | collective-permute-start | bytes 393224 | tf_op jit(solution)/shard_map/ppermute | solution.py:815
  373.9 16.4 %all-to-all-start.3 = ((f32[32,1,1088]{2,1,0:T(1,128)}), f32[32,1,1088]{2,1,0:T(1,128)S(1)}, u32[]{:S(2)}, u32[]{:S(2)}) async-start(f32[32,1,1088]{2,1,0:T(1,128)} %reshape.184), calls=%async_computation.3 | async-start | bytes 294912 | tf_op jit(solution)/shard_map/all_to_all | solution.py:1195
  (75 other events, 629.6 us)
Sparse Core Ops, SparseCore 0:
  30.8 42.2 all-gather.6
  199.7 45.0 all-gather.8
  309.9 59.9 all-gather.10
where the time goes:
time: 432 us; the launch traced here: 425 us
  waiting for transfers between devices  135 us (31%)
  Pallas kernels  122 us (28%)
  starting transfers between devices  78.2 us (18%)
  local copies, waits for them, and re-layouts  39.7 us (9%)
  other arithmetic  34.3 us (8%)
  between operations  14.9 us (3%)
    pallas_call x19, Pallas kernels, call(): pl.pallas_call(run, out_shape=tuple(outs), in_specs=in_specs, out_specs=t...  122 us
    ppermute x56, waiting for transfers between devices, permute(): return lax.ppermute(value, axes, moves)  121 us
    ppermute x56, starting transfers between devices, permute(): return lax.ppermute(value, axes, moves)  58.6 us
    convert_element_type x17, other arithmetic, add(): return (total if zero is None else total + zero[0, 0]).astype(bf16)  18.7 us
    unnamed x123, local copies, waits for them, and re-layouts  15 us
    all_to_all x4, starting transfers between devices, everywhere(): return lax.all_to_all(copies, axes, 0, 0, tiled=True)  13.8 us
    all_to_all x4, waiting for transfers between devices, everywhere(): return lax.all_to_all(copies, axes, 0, 0, tiled=True)  13.3 us
  transfers between devices with their start and end apart: 64, of which 23 were waited for; matrix products, arithmetic and copies ran while one was open for 14% of the time, Pallas kernels for 19%

commit v1 on v0

--- a/solution.py
+++ b/solution.py
@@ -865,20 +865,22 @@
         count = first[0].shape[0] // 2
         return [add(stacks[2 * i][count:], first[i][count:], zero=zero) for i in range(2)]
 
-    def halve_rows(keep, arrived, order, send, last):
+    def halve_rows(keep, arrived, order, send, last, log):
         items = [keep, arrived]
         for bit in order[-2::-1]:
             count = arrived.shape[0] // 2
             if send is None:
                 send = add(*[item[count:] for item in items])
             arrived = across(send, bit)
+            log.append(arrived)
             items = [item[:count] for item in items] + [arrived]
             send = None
         return add(*[item[0] for item in items], zero=last)
 
-    def halve_both(stacks, first, send, last=None):
-        near = halve_rows(stacks[0], first[0], bits, send[0], last)
-        return near, halve_rows(stacks[2], first[1], bits[::-1], send[1], last)
+    def halve_both(stacks, first, send, last=None, log=None):
+        log = [] if log is None else log
+        near = halve_rows(stacks[0], first[0], bits, send[0], last, log)
+        return near, halve_rows(stacks[2], first[1], bits[::-1], send[1], last, log)
 
     def hold(arrays, after):
         anywhere = pl.BlockSpec(memory_space=pl.ANY)
@@ -933,9 +935,8 @@
             for own, first, last in zip(shards, cuts, cuts[1:])
         ]
     head_shard, hidden_shard = shards[:2]
+    attn_full = lax.all_gather(head_shard, COLS, axis=0, tiled=False)
     hidden_w = gather_pieces(hidden_shard)
-    (head_shard,) = hold((head_shard,), (hidden_w[1][0],))
-    attn_full = lax.all_gather(head_shard, COLS, axis=0, tiled=False)
     hidden_flat = [piece for group in hidden_w for piece in group]
 
     small, = call(
@@ -1112,19 +1113,7 @@
     )
     head_grads, context_grads = rest[:3], rest[3:]
     context_grads = team_send(context_grads)
-    *head_stacks, heads_done = call(
-        functools.partial(head_grads_kernel, col_parts, row_parts),
-        (place, low_grad, attended, normed_t, context_t, *head_grads),
-        head_stacks,
-        scratch=[head_buffer, head_sems],
-        time=8,
-        in_specs=[smem] + [vmem] * 7,
-        out_specs=anywhere * 4,
-        token=True,
-    )
     down_first = first_messages(hidden_grads[4:])
-    down_second = second_messages(hidden_grads[4:], down_first, heads_done)
-    down_sums = halve_both(hidden_grads[4:], down_first, down_second)
     g_steps, adjoint_ends, adjoint_total, adjoint_done = call(
         functools.partial(adjoint_kernel, team),
         (logr, *context_grads),
@@ -1135,17 +1124,15 @@
         ),
         scratch=[pltpu.VMEM((length, LANES), f32)],
         time=1,
-        after=(heads_done, *down_second),
+        after=down_first,
         token=True,
     )
+    adjoint_totals = everywhere(adjoint_total.astype(bf16), ("sh", "mq"))
+    down_second = second_messages(hidden_grads[4:], down_first, adjoint_done)
+    down_second = hold(down_second, (adjoint_totals,))
     up_stacks = list(hidden_grads[:4])
-    up_stacks[1::2] = hold(up_stacks[1::2], down_first)
+    up_stacks[1::2] = hold(up_stacks[1::2], (adjoint_totals,))
     up_first = first_messages(up_stacks)
-    (own_total,) = hold((adjoint_total.astype(bf16),), (*down_sums, *up_first))
-    adjoint_totals = everywhere(own_total, ("sh", "mq"))
-    grad_down = sum_over_z(*down_sums, False)
-    up_second = second_messages(up_stacks, up_first, adjoint_done)
-    up_second = hold(up_second, (adjoint_totals,))
     *one_pieces, grad_ssm, context_done = call(
         functools.partial(context_back_kernel, team),
         (place, g_steps, u_steps, adjoint_ends, adjoint_totals, logr, coef, one_part),
@@ -1160,22 +1147,36 @@
         ],
         in_specs=[smem] + [vmem] * 7,
         time=1,
-        after=(*up_second, layer_pieces),
+        after=(*down_second, *up_stacks[1::2]),
         token=True,
     )
     one_pieces = team_send(one_pieces)
-    up_sums = halve_both(up_stacks, up_first, up_second, context_done)
+    down_arrived = []
+    down_sums = halve_both(
+        hidden_grads[4:], down_first, down_second, context_done, down_arrived
+    )
     grad_rows, gain_one_grad, rows_done = call(
         functools.partial(input_grad_kernel, team),
         (place, x, gain_one, middle_grad, *one_pieces),
         (shaped((own_rows, width), bf16), shaped((1, width), f32)),
         in_specs=[smem] + [vmem] * (3 + team),
         time=1,
-        after=(grad_down, *up_sums),
+        after=(layer_pieces, *down_arrived),
         token=True,
     )
-    head_stacks[1::2] = hold(head_stacks[1::2], (grad_rows,))
-    up_sums = hold(up_sums, head_stacks[1::2])
+    grad_down = sum_over_z(*down_sums, False)
+    head_stacks = call(
+        functools.partial(head_grads_kernel, col_parts, row_parts),
+        (place, low_grad, attended, normed_t, context_t, *head_grads),
+        head_stacks,
+        scratch=[head_buffer, head_sems],
+        time=1,
+        in_specs=[smem] + [vmem] * 7,
+        out_specs=anywhere * 4,
+        after=(grad_rows,),
+    )
+    up_second = second_messages(up_stacks, up_first, rows_done)
+    up_sums = halve_both(up_stacks, up_first, up_second)
     head_first = first_messages(head_stacks)
     head_second = second_messages(head_stacks, head_first, rows_done)
     head_sums = halve_both(head_stacks, head_first, head_second)

time: 432 us -> 432 us (level)
  waiting for transfers between devices: 135 us -> 154 us
  other arithmetic: 34.3 us -> 24.6 us
  local copies, waits for them, and re-layouts: 39.7 us -> 35 us
    all_to_all x4, waiting for transfers between devices: 13.3 us -> 23 us  [everywhere(): return lax.all_to_all(copies, axes, 0, 0, tiled=True)]
    ppermute x56, waiting for transfers between devices: 121 us -> 130 us  [permute(): return lax.ppermute(value, axes, moves)]
    convert_element_type x17 -> x16, other arithmetic: 18.7 us -> 11.8 us  [add(): return (total if zero is None else total + zero[0, 0]).astype(bf16)]
    add x2 -> x0, other arithmetic: 4.38 us -> none  [add(): return (total if zero is None else total + zero[0, 0]).astype(bf16)]
    unnamed x123 -> x113, local copies, waits for them, and re-layouts: 15 us -> 12.8 us
  transfers between devices with their start and end apart: 64 -> 64, of which waited for: 23 -> 30; matrix products, arithmetic and copies ran while one was open for 14% -> 11% of each run, Pallas kernels for 19% -> 20%
where the time goes in v1:
time: 432 us; the launch traced here: 425 us
  waiting for transfers between devices  154 us (36%)
  Pallas kernels  122 us (28%)
  starting transfers between devices  74.8 us (17%)
  local copies, waits for them, and re-layouts  35 us (8%)
  other arithmetic  24.6 us (6%)
  between operations  14.8 us (3%)
    ppermute x56, waiting for transfers between devices, permute(): return lax.ppermute(value, axes, moves)  130 us
    pallas_call x19, Pallas kernels, call(): pl.pallas_call(run, out_shape=tuple(outs), in_specs=in_specs, out_specs=t...  122 us
    ppermute x56, starting transfers between devices, permute(): return lax.ppermute(value, axes, moves)  55.7 us
    all_to_all x4, waiting for transfers between devices, everywhere(): return lax.all_to_all(copies, axes, 0, 0, tiled=True)  23 us
    all_to_all x4, starting transfers between devices, everywhere(): return lax.all_to_all(copies, axes, 0, 0, tiled=True)  16.1 us
    unnamed x113, local copies, waits for them, and re-layouts  12.8 us
    convert_element_type x16, other arithmetic, add(): return (total if zero is None else total + zero[0, 0]).astype(bf16)  11.8 us
  transfers between devices with their start and end apart: 64, of which 30 were waited for; matrix products, arithmetic and copies ran while one was open for 11% of the time, Pallas kernels for 20%

profile of v1, /device:TPU:0, one launch (start us, length us, event | category | flops | bytes accessed | tf_op | source)
XLA Modules:
  0.0 424.8 jit_solution(3879107500505841152)
XLA Ops:
  7.9 2.6 shard_map.363
  12.6 2.9 collective-permute-start.2
  17.1 2.3 dynamic-slice_bitcast_fusion.2
  21.7 6.2 %collective-permute-done.2.refs_2_.refs_6_ = bf16[256,1024]{1,0:T(8,128)(2,1)} collective-permute-done((bf16[256,1024]{1,0:T(8,128)(2,1)S(1)}, bf16[256,1024]{1,0:T(8,128)(2,1)}, u32[]{:S(2)}, u32[]{:S(2)}) %collective-permute-start.2) | collective-permute-done | bytes 524320 | tf_op jit(solution)/shard_map/ppermute | solution.py:815
  32.8 4.9 %all-to-all-start = ((f32[32,1,1088]{2,1,0:T(1,128)}), f32[32,1,1088]{2,1,0:T(1,128)S(1)}, u32[]{:S(2)}, u32[]{:S(2)}) async-start(f32[32,1,1088]{2,1,0:T(1,128)} %reshape.244), calls=%async_computation | async-start | bytes 294912 | tf_op jit(solution)/shard_map/all_to_all | solution.py:916
  39.2 5.3 %collective-permute-start.9 = (bf16[256,1024]{1,0:T(8,128)(2,1)}, bf16[256,1024]{1,0:T(8,128)(2,1)}, u32[]{:S(2)}, u32[]{:S(2)}) collective-permute-start(bf16[256,1024]{1,0:T(8,128)(2,1)} %collective-permute-done.4.refs_4_.refs_9_), channel_id=1, source_target_pairs={{0,1},{1,2},{2,3},{3,0},{4,5},{5,6},{6,7},{7,4},{8,9},{9,10},{10,1... | collective-permute-start | bytes 1572872 | tf_op jit(solution)/shard_map/ppermute | solution.py:815
  54.3 6.5 %shard_map.365 = (bf16[512,1024]{1,0:T(8,128)(2,1)}, bf16[1024,512]{1,0:T(8,128)(2,1)}, f32[4,512,128]{2,1,0:T(8,128)}, f32[16,8,512]{2,1,0:T(8,128)}, f32[16,512]{1,0:T(8,128)}) custom-call(s32[7]{0:T(128)} %stack.25.refs_0_, bf16[512,1024]{1,0:T(8,128)(2,1)} %broadcast_select_fusion.1.refs_1_.refs_0_, f32[1,1024]{1,0:T(1,128)} %slice.181.refs_2_, ...), custom_call_target="tpu_custom_call" | custom-call | flops 5750000128 | bytes 4526108 | tf_op jit(solution)/shard_map/pallas_call | solution.py:755
  60.8 5.4 %collective-permute-done.9.refs_13_ = bf16[256,1024]{1,0:T(8,128)(2,1)} collective-permute-done((bf16[256,1024]{1,0:T(8,128)(2,1)}, bf16[256,1024]{1,0:T(8,128)(2,1)}, u32[]{:S(2)}, u32[]{:S(2)}) %collective-permute-start.9) | collective-permute-done | bytes 524320 | tf_op jit(solution)/shard_map/ppermute | solution.py:815
  70.8 4.4 %all-to-all-start.1 = ((bf16[8,16,512]{2,1,0:T(8,128)(2,1)}), bf16[8,16,512]{2,1,0:T(8,128)(2,1)S(1)}, u32[]{:S(2)}, u32[]{:S(2)}) async-start(bf16[8,16,512]{2,1,0:T(8,128)(2,1)} %broadcast_in_dim.11), calls=%async_computation.1 | async-start | bytes 262144 | tf_op jit(solution)/shard_map/all_to_all | solution.py:916
  77.6 4.5 %collective-permute-done.10.refs_9_.refs_17_ = bf16[256,1024]{1,0:T(8,128)(2,1)} collective-permute-done((bf16[256,1024]{1,0:T(8,128)(2,1)}, bf16[256,1024]{1,0:T(8,128)(2,1)}, u32[]{:S(2)}, u32[]{:S(2)}) %collective-permute-start.10) | collective-permute-done | bytes 524320 | tf_op jit(solution)/shard_map/ppermute | solution.py:815
  83.8 9.4 %collective-permute-done.11.refs_10_.refs_6_.refs_3_ = bf16[2,256,512]{2,1,0:T(8,128)(2,1)S(1)} collective-permute-done((bf16[2,256,512]{2,1,0:T(8,128)(2,1)S(1)}, bf16[2,256,512]{2,1,0:T(8,128)(2,1)S(1)}, u32[]{:S(2)}, u32[]{:S(2)}) %collective-permute-start.11) | collective-permute-done | bytes 524320 | tf_op jit(solution)/shard_map/ppermute | solution.py:815
  94.9 6.2 %shard_map.367.refs_3_ = bf16[512,512]{1,0:T(8,128)(2,1)} custom-call(s32[7]{0:T(128)} %stack.25.refs_0_, f32[4,512,128]{2,1,0:T(8,128)} %get-tuple-element.110.refs_1_.refs_2_, f32[16,8,512]{2,1,0:T(8,128)} %get-tuple-element.111.refs_2_, bf16[8,16,512]{2,1,0:T(8,128)(2,1)} %copy-done.41, f32[16,512]{1,0:T(8,128)} %get-tuple-element.199.refs_3_.refs_4_.refs_0_.refs_5_, ...), custom_call_target="tpu_custom_call" | custom-call | flops 8049999872 | bytes 2031644 | tf_op jit(solution)/shard_map/pallas_call | solution.py:755
  101.2 4.1 collective-permute-done.18.refs_13_.refs_12_
  105.7 2.6 collective-permute-done.16.refs_11_.refs_8_.refs_15_
  109.3 7.0 %collective-permute-done.15.refs_10_.refs_7_.refs_14_ = bf16[2,256,512]{2,1,0:T(8,128)(2,1)S(1)} collective-permute-done((bf16[2,256,512]{2,1,0:T(8,128)(2,1)S(1)}, bf16[2,256,512]{2,1,0:T(8,128)(2,1)S(1)}, u32[]{:S(2)}, u32[]{:S(2)}) %collective-permute-start.15) | collective-permute-done | bytes 524320 | tf_op jit(solution)/shard_map/ppermute | solution.py:815
  116.8 2.8 collective-permute-done.21.refs_16_
  121.8 9.0 %collective-permute-done.14.refs_8_.refs_5_.refs_12_ = bf16[2,256,512]{2,1,0:T(8,128)(2,1)S(1)} collective-permute-done((bf16[2,256,512]{2,1,0:T(8,128)(2,1)}, bf16[2,256,512]{2,1,0:T(8,128)(2,1)S(1)}, u32[]{:S(2)}, u32[]{:S(2)}) %collective-permute-start.14) | collective-permute-done | bytes 524320 | tf_op jit(solution)/shard_map/ppermute | solution.py:815
  131.8 7.2 %shard_map.368 = (bf16[1024,512]{1,0:T(8,128)(2,1)}, bf16[1024,512]{1,0:T(8,128)(2,1)}, bf16[3,512,512]{2,1,0:T(8,128)(2,1)}) custom-call(s32[7]{0:T(128)} %stack.25.refs_0_, bf16[512,1024]{1,0:T(8,128)(2,1)} %get-tuple-element.109.refs_1_, bf16[512,1024]{1,0:T(8,128)(2,1)} %broadcast_select_fusion.refs_2_.refs_3_, bf16[512,512]{1,0:T(8,128)(2,1)} %shard_map.367.refs_3_, ...), custom_call_target="tpu_custom_call" | custom-call | flops 1150000000 | bytes 11010076 | tf_op jit(solution)/shard_map/pallas_call | solution.py:755
  141.8 6.3 %shard_map.369 = (bf16[512,1024]{1,0:T(8,128)(2,1)}, bf16[512,512]{1,0:T(8,128)(2,1)}, bf16[4,512,512]{2,1,0:T(8,128)(2,1)}, bf16[4,512,512]{2,1,0:T(8,128)(2,1)}) custom-call(s32[7]{0:T(128)} %stack.25.refs_0_, bf16[3,512,512]{2,1,0:T(8,128)(2,1)} %get-tuple-element.114.refs_1_.refs_6_, bf16[2,256,512]{2,1,0:T(8,128)(2,1)} %copy-done.1, ...), custom_call_target="tpu_custom_call" | custom-call | flops 1150000000 | bytes 11534364 | tf_op jit(solution)/shard_map/pallas_call | solution.py:755
  152.1 4.3 %shard_map.370 = (f32[512,1024]{1,0:T(8,128)}, bf16[512,1024]{1,0:T(8,128)(2,1)}, bf16[1024,512]{1,0:T(8,128)(2,1)}) custom-call(bf16[512,1024]{1,0:T(8,128)(2,1)} %broadcast_select_fusion.1.refs_1_.refs_0_, f32[1,1024]{1,0:T(1,128)} %slice.179.refs_1_.refs_2_, bf16[512,1024]{1,0:T(8,128)(2,1)} %get-tuple-element.115.refs_2_, bf16[512,1024]{1,0:T(8,128)(2,1)} %copy-done.48), custom_call_target="tpu_custom_call" | custom-call | flops 1150000000 | bytes 7344128 | tf_op jit(solution)/shard_map/pallas_call | solution.py:755
  156.3 6.4 %collective-permute-done.25.refs_20_ = bf16[256,1024]{1,0:T(8,128)(2,1)S(1)} collective-permute-done((bf16[256,1024]{1,0:T(8,128)(2,1)}, bf16[256,1024]{1,0:T(8,128)(2,1)S(1)}, u32[]{:S(2)}, u32[]{:S(2)}) %collective-permute-start.25) | collective-permute-done | bytes 524320 | tf_op jit(solution)/shard_map/ppermute | solution.py:815
  163.6 22.1 %shard_map.371 = (bf16[256,1024]{1,0:T(8,128)(2,1)}, bf16[256,1024]{1,0:T(8,128)(2,1)}, bf16[512,1024]{1,0:T(8,128)(2,1)}, bf16[2,2,256,512]{3,2,1,0:T(8,128)(2,...) custom-call(s32[7]{0:T(128)} %stack.25.refs_0_, ...), custom_call_target="tpu_custom_call" | custom-call | flops 20700000256 | bytes 23068700 | tf_op jit(solution)/shard_map/pallas_call | solution.py:755
  191.8 14.8 %shard_map.373 = (f32[256,1024]{1,0:T(8,128)}, f32[1,1024]{1,0:T(1,128)}, bf16[512,1024]{1,0:T(8,128)(2,1)}, bf16[512,1024]{1,0:T(8,128)(2,1)}, bf16[512,512]{1,...) custom-call(s32[7]{0:T(128)} %stack.25.refs_0_, ...), custom_call_target="tpu_custom_call" | custom-call | flops 1150000000 | bytes 20979740 | tf_op jit(solution)/shard_map/pallas_call | solution.py:755
  206.8 4.9 %collective-permute-done.30.refs_3_ = bf16[2,2,256,512]{3,2,1,0:T(8,128)(2,1)} collective-permute-done((bf16[2,2,256,512]{3,2,1,0:T(8,128)(2,1)}, bf16[2,2,256,512]{3,2,1,0:T(8,128)(2,1)}, u32[]{:S(2)}, u32[]{:S(2)}) %collective-permute-start.30) | collective-permute-done | bytes 1048608 | tf_op jit(solution)/shard_map/ppermute | solution.py:815
  213.0 6.6 %shard_map.374 = (f32[4,512,128]{2,1,0:T(8,128)}, f32[2,16,8,512]{3,2,1,0:T(8,128)}, f32[2,16,512]{2,1,0:T(8,128)}, f32[8,128]{1,0:T(8,128)}) custom-call(f32[16,512]{1,0:T(8,128)} %get-tuple-element.199.refs_3_.refs_4_.refs_0_.refs_5_, bf16[512,512]{1,0:T(8,128)(2,1)} %get-tuple-element.126.refs_1_, bf16[512,512]{1,0:T(8,128)(2,1)} %copy-done.51, ...), custom_call_target="tpu_custom_call" | custom-call | flops 1150000000 | bytes 2719744 | tf_op jit(solution)/shard_map/pallas_call | solution.py:755
  221.2 3.8 all-to-all-start.2
  226.2 3.1 add_convert_fusion.10
  229.3 14.4 %all-to-all-done.2.refs_2_.refs_4_ = bf16[8,2,16,512]{3,2,1,0:T(8,128)(2,1)S(1)} async-done(((bf16[8,2,16,512]{3,2,1,0:T(8,128)(2,1)}), bf16[8,2,16,512]{3,2,1,0:T(8,128)(2,1)S(1)}, u32[]{:S(2)}, u32[]{:S(2)}) %all-to-all-start.2) | async-done | bytes 262176 | tf_op jit(solution)/shard_map/all_to_all | solution.py:916
  247.0 12.9 %shard_map.377 = (bf16[256,1024]{1,0:T(8,128)(2,1)}, bf16[256,1024]{1,0:T(8,128)(2,1)}, f32[2,16,512]{2,1,0:T(8,128)}, f32[8,128]{1,0:T(8,128)}) custom-call(s32[7]{0:T(128)} %stack.25.refs_0_, f32[4,512,128]{2,1,0:T(8,128)} %get-tuple-element.130.refs_1_, f32[4,512,128]{2,1,0:T(8,128)} %get-tuple-element.110.refs_1_.refs_2_, ...), custom_call_target="tpu_custom_call" | custom-call | flops 1150000000 | bytes 5111836 | tf_op jit(solution)/shard_map/pallas_call | solution.py:755
  268.7 2.3 collective-permute-done.44
  271.9 12.4 %collective-permute-done.45 = bf16[256,512]{1,0:T(8,128)(2,1)S(1)} collective-permute-done((bf16[256,512]{1,0:T(8,128)(2,1)}, bf16[256,512]{1,0:T(8,128)(2,1)S(1)}, u32[]{:S(2)}, u32[]{:S(2)}) %collective-permute-start.45) | collective-permute-done | bytes 262176 | tf_op jit(solution)/shard_map/ppermute | solution.py:815
  287.1 3.6 shard_map.378
  294.3 7.1 %shard_map.381 = (bf16[2,2,256,512]{3,2,1,0:T(8,128)(2,1)}, bf16[2,2,256,512]{3,2,1,0:T(8,128)(2,1)}, bf16[2,2,256,512]{3,2,1,0:T(8,128)(2,1)}, bf16[2,2,256,512]{3,2,1,0:T(8,128)(2,1)}) custom-call(s32[7]{0:T(128)} %stack.25.refs_0_, bf16[512,1024]{1,0:T(8,128)(2,1)} %get-tuple-element.151.refs_1_, bf16[512,512]{1,0:T(8,128)(2,1)} %get-tuple-element.152.refs_2_, ...), custom_call_target="tpu_custom_call" | custom-call | flops 1150000000 | bytes 9437212 | tf_op jit(solution)/shard_map/pallas_call | solution.py:755
  310.1 28.2 %collective-permute-done.37 = bf16[1,2,256,512]{3,2,1,0:T(8,128)(2,1)S(1)} collective-permute-done((bf16[1,2,256,512]{3,2,1,0:T(8,128)(2,1)S(1)}, bf16[1,2,256,512]{3,2,1,0:T(8,128)(2,1)S(1)}, u32[]{:S(2)}, u32[]{:S(2)}) %collective-permute-start.37) | collective-permute-done | bytes 524320 | tf_op jit(solution)/shard_map/ppermute | solution.py:815
  338.5 7.5 %collective-permute-done.40 = bf16[256,512]{1,0:T(8,128)(2,1)S(1)} collective-permute-done((bf16[256,512]{1,0:T(8,128)(2,1)S(1)}, bf16[256,512]{1,0:T(8,128)(2,1)S(1)}, u32[]{:S(2)}, u32[]{:S(2)}) %collective-permute-start.40) | collective-permute-done | bytes 262176 | tf_op jit(solution)/shard_map/ppermute | solution.py:815
  352.9 3.3 shard_map.372.refs_9_
  356.3 2.5 collective-permute-start.42
  358.8 2.7 collective-permute-done.51
  364.4 4.0 collective-permute-done.52
  368.4 4.3 %collective-permute-start.53 = (bf16[256,512]{1,0:T(8,128)(2,1)S(1)}, bf16[256,512]{1,0:T(8,128)(2,1)S(1)}, u32[]{:S(2)}, u32[]{:S(2)}) collective-permute-start(bf16[256,512]{1,0:T(8,128)(2,1)S(1)} %fusion), channel_id=1, source_target_pairs={{0,3},{1,0},{2,1},{3,2},{4,7},{5,4},{6,5},{7,6},{8,11},{9,8},{10,9... | collective-permute-start | bytes 786440 | tf_op jit(solution)/shard_map/ppermute | solution.py:815
  376.5 2.6 all-to-all-start.3
  380.7 3.9 collective-permute-start.54
  385.3 5.0 %shard_map.380 = (f32[128,1024]{1,0:T(8,128)}, f32[128,1024]{1,0:T(8,128)}, f32[128,1024]{1,0:T(8,128)}, f32[1024,128]{1,0:T(8,128)}, f32[1024,128]{1,0:T(8,128)...) custom-call(s32[7]{0:T(128)} %stack.25.refs_0_, bf16[256,512]{1,0:T(8,128)(2,1)} %copy-done.31, bf16[128,512]{1,0:T(8,128)(2,1)} %copy-done.52, ...), custom_call_target="tpu_custom_call" | custom-call | flops 4600000000 | bytes 7078940 | tf_op jit(solution)/shard_map/pallas_call | solution.py:755
  394.5 4.2 shard_map.379.refs_10_
  399.3 3.2 shard_map.382
  403.9 3.0 all-to-all-start.4
  407.4 6.8 %all-to-all-done.4.refs_0_ = f32[32,2,128]{2,1,0:T(2,128)S(1)} async-done(((f32[32,2,128]{2,1,0:T(2,128)}), f32[32,2,128]{2,1,0:T(2,128)S(1)}, u32[]{:S(2)}, u32[]{:S(2)}) %all-to-all-start.4) | async-done | bytes 32800 | tf_op jit(solution)/shard_map/all_to_all | solution.py:916
  414.8 3.2 shard_map.385
  (285 shorter events, 107.3 us)
Async XLA Ops:
  7.2 60.0 %all-gather.6.cloned.1.call-start = ((), (), s32[]{:S(2)}) async-start(), calls=%async_computation.5 | async-start | bytes 1310720 | tf_op jit(solution)/shard_map/all_gather | solution.py:938
  11.9 32.5 %collective-permute-start = (bf16[512,1024]{1,0:T(8,128)(2,1)}, bf16[512,1024]{1,0:T(8,128)(2,1)}, u32[]{:S(2)}, u32[]{:S(2)}) collective-permute-start(bf16[512,1024]{1,0:T(8,128)(2,1)} %dynamic-slice_bitcast_fusion.3), channel_id=1, source_target_pairs={{0,4},{4,0},{1,5},{5,1},{2,6},{6,2},{3,7},{7,3},{8,12},{12,8},{9,1... | collective-permute-start | bytes 3145736 | tf_op jit(solution)/shard_map/ppermute | solution.py:815
  12.6 15.3 %collective-permute-start.2 = (bf16[256,1024]{1,0:T(8,128)(2,1)S(1)}, bf16[256,1024]{1,0:T(8,128)(2,1)}, u32[]{:S(2)}, u32[]{:S(2)}) collective-permute-start(bf16[256,1024]{1,0:T(8,128)(2,1)S(1)} %maximum_select_fusion.refs_5_), channel_id=1, source_target_pairs={{0,8},{8,0},{16,24},{24,16},{1,9},{9,1},{17,25},{25,17},{2,10},{10... | collective-permute-start | bytes 1572872 | tf_op jit(solution)/shard_map/ppermute | solution.py:815
  15.6 13.8 %collective-permute-start.3 = (bf16[256,1024]{1,0:T(8,128)(2,1)S(1)}, bf16[256,1024]{1,0:T(8,128)(2,1)}, u32[]{:S(2)}, u32[]{:S(2)}) collective-permute-start(bf16[256,1024]{1,0:T(8,128)(2,1)S(1)} %maximum_select_fusion.refs_5_), channel_id=1, source_target_pairs={{0,16},{8,24},{16,0},{24,8},{1,17},{9,25},{17,1},{25,9},{2,18},{10... | collective-permute-start | bytes 1572872 | tf_op jit(solution)/shard_map/ppermute | solution.py:815
  19.4 34.9 %collective-permute-start.5 = (bf16[512,1024]{1,0:T(8,128)(2,1)}, bf16[512,1024]{1,0:T(8,128)(2,1)}, u32[]{:S(2)}, u32[]{:S(2)}) collective-permute-start(bf16[512,1024]{1,0:T(8,128)(2,1)} %dynamic-slice_bitcast_fusion.2), channel_id=1, source_target_pairs={{0,4},{4,0},{1,5},{5,1},{2,6},{6,2},{3,7},{7,3},{8,12},{12,8},{9,1... | collective-permute-start | bytes 3145736 | tf_op jit(solution)/shard_map/ppermute | solution.py:815
  19.4 19.8 %collective-permute-start.4 = (bf16[256,1024]{1,0:T(8,128)(2,1)S(1)}, bf16[256,1024]{1,0:T(8,128)(2,1)}, u32[]{:S(2)}, u32[]{:S(2)}) collective-permute-start(bf16[256,1024]{1,0:T(8,128)(2,1)S(1)} %maximum_select_fusion.refs_5_), channel_id=1, source_target_pairs={{0,1},{1,2},{2,3},{3,0},{4,5},{5,6},{6,7},{7,4},{8,9},{9,10},{10,1... | collective-permute-start | bytes 1572872 | tf_op jit(solution)/shard_map/ppermute | solution.py:815
  32.8 16.7 %all-to-all-start = ((f32[32,1,1088]{2,1,0:T(1,128)}), f32[32,1,1088]{2,1,0:T(1,128)S(1)}, u32[]{:S(2)}, u32[]{:S(2)}) async-start(f32[32,1,1088]{2,1,0:T(1,128)} %reshape.244), calls=%async_computation | async-start | bytes 294912 | tf_op jit(solution)/shard_map/all_to_all | solution.py:916
  39.2 27.0 %collective-permute-start.9 = (bf16[256,1024]{1,0:T(8,128)(2,1)}, bf16[256,1024]{1,0:T(8,128)(2,1)}, u32[]{:S(2)}, u32[]{:S(2)}) collective-permute-start(bf16[256,1024]{1,0:T(8,128)(2,1)} %collective-permute-done.4.refs_4_.refs_9_), channel_id=1, source_target_pairs={{0,1},{1,2},{2,3},{3,0},{4,5},{5,6},{6,7},{7,4},{8,9},{9,10},{10,1... | collective-permute-start | bytes 1572872 | tf_op jit(solution)/shard_map/ppermute | solution.py:815
  44.5 24.1 %collective-permute-start.8 = (bf16[256,1024]{1,0:T(8,128)(2,1)}, bf16[256,1024]{1,0:T(8,128)(2,1)S(1)}, u32[]{:S(2)}, u32[]{:S(2)}) collective-permute-start(bf16[256,1024]{1,0:T(8,128)(2,1)} %collective-permute-done.4.refs_4_.refs_9_), channel_id=1, source_target_pairs={{0,16},{8,24},{16,0},{24,8},{1,17},{9,25},{17,1},{25,9},{2,18},{10... | collective-permute-start | bytes 1572872 | tf_op jit(solution)/shard_map/ppermute | solution.py:815
  44.5 25.2 %collective-permute-start.7 = (bf16[256,1024]{1,0:T(8,128)(2,1)}, bf16[256,1024]{1,0:T(8,128)(2,1)}, u32[]{:S(2)}, u32[]{:S(2)}) collective-permute-start(bf16[256,1024]{1,0:T(8,128)(2,1)} %collective-permute-done.4.refs_4_.refs_9_), channel_id=1, source_target_pairs={{0,8},{8,0},{16,24},{24,16},{1,9},{9,1},{17,25},{25,17},{2,10},{10... | collective-permute-start | bytes 1572872 | tf_op jit(solution)/shard_map/ppermute | solution.py:815
  44.5 31.0 %collective-permute-start.6 = (bf16[256,1024]{1,0:T(8,128)(2,1)}, bf16[256,1024]{1,0:T(8,128)(2,1)}, u32[]{:S(2)}, u32[]{:S(2)}) collective-permute-start(bf16[256,1024]{1,0:T(8,128)(2,1)} %collective-permute-done.2.refs_2_.refs_6_), channel_id=1, source_target_pairs={{0,16},{8,24},{16,0},{24,8},{1,17},{9,25},{17,1},{25,9},{2,18},{10... | collective-permute-start | bytes 1572872 | tf_op jit(solution)/shard_map/ppermute | solution.py:815
  66.2 15.9 %collective-permute-start.10 = (bf16[256,1024]{1,0:T(8,128)(2,1)}, bf16[256,1024]{1,0:T(8,128)(2,1)}, u32[]{:S(2)}, u32[]{:S(2)}) collective-permute-start(bf16[256,1024]{1,0:T(8,128)(2,1)} %collective-permute-done.9.refs_13_), channel_id=1, source_target_pairs={{0,1},{1,2},{2,3},{3,0},{4,5},{5,6},{6,7},{7,4},{8,9},{9,10},{10,1... | collective-permute-start | bytes 1572872 | tf_op jit(solution)/shard_map/ppermute | solution.py:815
  66.2 17.1 %collective-permute-start.19 = (bf16[256,1024]{1,0:T(8,128)(2,1)}, bf16[256,1024]{1,0:T(8,128)(2,1)}, u32[]{:S(2)}, u32[]{:S(2)}) collective-permute-start(bf16[256,1024]{1,0:T(8,128)(2,1)} %collective-permute-done.9.refs_13_), channel_id=1, source_target_pairs={{0,8},{8,0},{16,24},{24,16},{1,9},{9,1},{17,25},{25,17},{2,10},{10... | collective-permute-start | bytes 1572872 | tf_op jit(solution)/shard_map/ppermute | solution.py:815
  68.5 24.7 %collective-permute-start.11 = (bf16[2,256,512]{2,1,0:T(8,128)(2,1)S(1)}, bf16[2,256,512]{2,1,0:T(8,128)(2,1)S(1)}, u32[]{:S(2)}, u32[]{:S(2)}) collective-permute-start(bf16[2,256,512]{2,1,0:T(8,128)(2,1)S(1)} %get-tuple-element.195.refs_5_.refs_2_.refs_9_), channel_id=1, source_target_pairs={{0,8},{8,0},{16,24},{24,16},{1,9},{9,1},{17,25},{25,17},{2,10},{10... | collective-permute-start | bytes 1572872 | tf_op jit(solution)/shard_map/ppermute | solution.py:815
  69.6 24.1 %collective-permute-start.12 = (bf16[2,256,512]{2,1,0:T(8,128)(2,1)S(1)}, bf16[2,256,512]{2,1,0:T(8,128)(2,1)S(1)}, u32[]{:S(2)}, u32[]{:S(2)}) collective-permute-start(bf16[2,256,512]{2,1,0:T(8,128)(2,1)S(1)} %get-tuple-element.195.refs_5_.refs_2_.refs_9_), channel_id=1, source_target_pairs={{0,16},{8,24},{16,0},{24,8},{1,17},{9,25},{17,1},{25,9},{2,18},{10... | collective-permute-start | bytes 1572872 | tf_op jit(solution)/shard_map/ppermute | solution.py:815
  70.8 23.4 %all-to-all-start.1 = ((bf16[8,16,512]{2,1,0:T(8,128)(2,1)}), bf16[8,16,512]{2,1,0:T(8,128)(2,1)S(1)}, u32[]{:S(2)}, u32[]{:S(2)}) async-start(bf16[8,16,512]{2,1,0:T(8,128)(2,1)} %broadcast_in_dim.11), calls=%async_computation.1 | async-start | bytes 262144 | tf_op jit(solution)/shard_map/all_to_all | solution.py:916
  75.2 211.8 %all-gather.8.cloned.1.call-start = ((), (), s32[]{:S(2)}) async-start(), calls=%async_computation.6 | async-start | bytes 2621440 | tf_op jit(solution)/shard_map/all_gather | solution.py:1082
  75.5 25.6 %collective-permute-start.20 = (bf16[256,1024]{1,0:T(8,128)(2,1)}, bf16[256,1024]{1,0:T(8,128)(2,1)}, u32[]{:S(2)}, u32[]{:S(2)}) collective-permute-start(bf16[256,1024]{1,0:T(8,128)(2,1)} %collective-permute-done.9.refs_13_), channel_id=1, source_target_pairs={{0,16},{8,24},{16,0},{24,8},{1,17},{9,25},{17,1},{25,9},{2,18},{10... | collective-permute-start | bytes 1572872 | tf_op jit(solution)/shard_map/ppermute | solution.py:815
  82.1 23.2 %collective-permute-start.18 = (bf16[256,1024]{1,0:T(8,128)(2,1)}, bf16[256,1024]{1,0:T(8,128)(2,1)}, u32[]{:S(2)}, u32[]{:S(2)}) collective-permute-start(bf16[256,1024]{1,0:T(8,128)(2,1)} %copy-done.49), channel_id=1, source_target_pairs={{0,8},{8,0},{16,24},{24,16},{1,9},{9,1},{17,25},{25,17},{2,10},{10... | collective-permute-start | bytes 1572872 | tf_op jit(solution)/shard_map/ppermute | solution.py:815
  83.3 25.0 %collective-permute-start.16 = (bf16[2,256,512]{2,1,0:T(8,128)(2,1)S(1)}, bf16[2,256,512]{2,1,0:T(8,128)(2,1)S(1)}, u32[]{:S(2)}, u32[]{:S(2)}) collective-permute-start(bf16[2,256,512]{2,1,0:T(8,128)(2,1)S(1)} %get-tuple-element.194.refs_9_.refs_6_.refs_13_), channel_id=1, source_target_pairs={{0,16},{8,24},{16,0},{24,8},{1,17},{9,25},{17,1},{25,9},{2,18},{10... | collective-permute-start | bytes 1572872 | tf_op jit(solution)/shard_map/ppermute | solution.py:815
  93.2 23.2 %collective-permute-start.15 = (bf16[2,256,512]{2,1,0:T(8,128)(2,1)S(1)}, bf16[2,256,512]{2,1,0:T(8,128)(2,1)S(1)}, u32[]{:S(2)}, u32[]{:S(2)}) collective-permute-start(bf16[2,256,512]{2,1,0:T(8,128)(2,1)S(1)} %get-tuple-element.194.refs_9_.refs_6_.refs_13_), channel_id=1, source_target_pairs={{0,8},{8,0},{16,24},{24,16},{1,9},{9,1},{17,25},{25,17},{2,10},{10... | collective-permute-start | bytes 1572872 | tf_op jit(solution)/shard_map/ppermute | solution.py:815
  93.7 26.0 %collective-permute-start.21 = (bf16[256,1024]{1,0:T(8,128)(2,1)}, bf16[256,1024]{1,0:T(8,128)(2,1)}, u32[]{:S(2)}, u32[]{:S(2)}) collective-permute-start(bf16[256,1024]{1,0:T(8,128)(2,1)} %collective-permute-done.19.refs_14_), channel_id=1, source_target_pairs={{0,16},{8,24},{16,0},{24,8},{1,17},{9,25},{17,1},{25,9},{2,18},{10... | collective-permute-start | bytes 1572872 | tf_op jit(solution)/shard_map/ppermute | solution.py:815
  101.1 20.7 %collective-permute-start.13 = (bf16[512,512]{1,0:T(8,128)(2,1)}, bf16[512,512]{1,0:T(8,128)(2,1)S(1)}, u32[]{:S(2)}, u32[]{:S(2)}) collective-permute-start(bf16[512,512]{1,0:T(8,128)(2,1)} %shard_map.367.refs_3_), channel_id=1, source_target_pairs={{0,4},{4,0},{1,5},{5,1},{2,6},{6,2},{3,7},{7,3},{8,12},{12,8},{9,1... | collective-permute-start | bytes 1572872 | tf_op jit(solution)/shard_map/ppermute | solution.py:815
  105.3 25.5 %collective-permute-start.14 = (bf16[2,256,512]{2,1,0:T(8,128)(2,1)}, bf16[2,256,512]{2,1,0:T(8,128)(2,1)S(1)}, u32[]{:S(2)}, u32[]{:S(2)}) collective-permute-start(bf16[2,256,512]{2,1,0:T(8,128)(2,1)} %copy-done.6), channel_id=1, source_target_pairs={{0,16},{8,24},{16,0},{24,8},{1,17},{9,25},{17,1},{25,9},{2,18},{10... | collective-permute-start | bytes 1572872 | tf_op jit(solution)/shard_map/ppermute | solution.py:815
  108.3 22.5 %collective-permute-start.17 = (bf16[2,256,512]{2,1,0:T(8,128)(2,1)S(1)}, bf16[2,256,512]{2,1,0:T(8,128)(2,1)S(1)}, u32[]{:S(2)}, u32[]{:S(2)}) collective-permute-start(bf16[2,256,512]{2,1,0:T(8,128)(2,1)S(1)} %collective-permute-done.16.refs_11_.refs_8_.refs_15_), channel_id=1, source_target_pairs={{0,8},{8,0},{16,24},{24,16},{1,9},{9,1},{17,25},{25,17},{2,10},{10... | collective-permute-start | bytes 1572872 | tf_op jit(solution)/shard_map/ppermute | solution.py:815
  116.4 24.5 %collective-permute-start.23 = (bf16[256,1024]{1,0:T(8,128)(2,1)}, bf16[256,1024]{1,0:T(8,128)(2,1)S(1)}, u32[]{:S(2)}, u32[]{:S(2)}) collective-permute-start(bf16[256,1024]{1,0:T(8,128)(2,1)} %collective-permute-done.10.refs_9_.refs_17_), channel_id=1, source_target_pairs={{0,16},{8,24},{16,0},{24,8},{1,17},{9,25},{17,1},{25,9},{2,18},{10... | collective-permute-start | bytes 1572872 | tf_op jit(solution)/shard_map/ppermute | solution.py:815
  119.7 21.2 %collective-permute-start.22 = (bf16[256,1024]{1,0:T(8,128)(2,1)}, bf16[256,1024]{1,0:T(8,128)(2,1)S(1)}, u32[]{:S(2)}, u32[]{:S(2)}) collective-permute-start(bf16[256,1024]{1,0:T(8,128)(2,1)} %collective-permute-done.10.refs_9_.refs_17_), channel_id=1, source_target_pairs={{0,8},{8,0},{16,24},{24,16},{1,9},{9,1},{17,25},{25,17},{2,10},{10... | collective-permute-start | bytes 1572872 | tf_op jit(solution)/shard_map/ppermute | solution.py:815
  148.2 14.6 %collective-permute-start.25 = (bf16[256,1024]{1,0:T(8,128)(2,1)}, bf16[256,1024]{1,0:T(8,128)(2,1)S(1)}, u32[]{:S(2)}, u32[]{:S(2)}) collective-permute-start(bf16[256,1024]{1,0:T(8,128)(2,1)} %copy-done.35), channel_id=1, source_target_pairs={{0,8},{8,0},{16,24},{24,16},{1,9},{9,1},{17,25},{25,17},{2,10},{10... | collective-permute-start | bytes 1572872 | tf_op jit(solution)/shard_map/ppermute | solution.py:815
  186.3 25.5 %collective-permute-start.30 = (bf16[2,2,256,512]{3,2,1,0:T(8,128)(2,1)}, bf16[2,2,256,512]{3,2,1,0:T(8,128)(2,1)}, u32[]{:S(2)}, u32[]{:S(2)}) collective-permute-start(bf16[2,2,256,512]{3,2,1,0:T(8,128)(2,1)} %get-tuple-element.128), channel_id=1, source_target_pairs={{0,16},{8,24},{16,0},{24,8},{1,17},{9,25},{17,1},{25,9},{2,18},{10... | collective-permute-start | bytes 3145736 | tf_op jit(solution)/shard_map/ppermute | solution.py:815
  186.8 25.1 %collective-permute-start.31 = (bf16[2,2,256,512]{3,2,1,0:T(8,128)(2,1)}, bf16[2,2,256,512]{3,2,1,0:T(8,128)(2,1)S(1)}, u32[]{:S(2)}, u32[]{:S(2)}) collective-permute-start(bf16[2,2,256,512]{3,2,1,0:T(8,128)(2,1)} %get-tuple-element.129), channel_id=1, source_target_pairs={{0,8},{8,0},{16,24},{24,16},{1,9},{9,1},{17,25},{25,17},{2,10},{10... | collective-permute-start | bytes 3145736 | tf_op jit(solution)/shard_map/ppermute | solution.py:815
  221.2 22.6 %all-to-all-start.2 = ((bf16[8,2,16,512]{3,2,1,0:T(8,128)(2,1)}), bf16[8,2,16,512]{3,2,1,0:T(8,128)(2,1)S(1)}, u32[]{:S(2)}, u32[]{:S(2)}) async-start(bf16[8,2,16,512]{3,2,1,0:T(8,128)(2,1)} %broadcast_in_dim.12), calls=%async_computation.2 | async-start | bytes 524288 | tf_op jit(solution)/shard_map/all_to_all | solution.py:916
  224.9 154.2 %all-gather.10.cloned.1.call-start = ((), (), s32[]{:S(2)}) async-start(), calls=%async_computation.7 | async-start | bytes 2621440 | tf_op jit(solution)/shard_map/all_gather | solution.py:1185
  244.4 16.8 %collective-permute-start.33 = (bf16[1,2,256,512]{3,2,1,0:T(8,128)(2,1)}, bf16[1,2,256,512]{3,2,1,0:T(8,128)(2,1)S(1)}, u32[]{:S(2)}, u32[]{:S(2)}) collective-permute-start(bf16[1,2,256,512]{3,2,1,0:T(8,128)(2,1)} %get-tuple-element.137.refs_8_), channel_id=1, source_target_pairs={{0,8},{8,0},{16,24},{24,16},{1,9},{9,1},{17,25},{25,17},{2,10},{10... | collective-permute-start | bytes 1572872 | tf_op jit(solution)/shard_map/ppermute | solution.py:815
  244.4 18.9 %collective-permute-start.34 = (bf16[1,2,256,512]{3,2,1,0:T(8,128)(2,1)}, bf16[1,2,256,512]{3,2,1,0:T(8,128)(2,1)S(1)}, u32[]{:S(2)}, u32[]{:S(2)}) collective-permute-start(bf16[1,2,256,512]{3,2,1,0:T(8,128)(2,1)} %get-tuple-element.138.refs_9_), channel_id=1, source_target_pairs={{0,16},{8,24},{16,0},{24,8},{1,17},{9,25},{17,1},{25,9},{2,18},{10... | collective-permute-start | bytes 1572872 | tf_op jit(solution)/shard_map/ppermute | solution.py:815
  245.6 46.3 %collective-permute-start.38 = (bf16[2,2,256,512]{3,2,1,0:T(8,128)(2,1)}, bf16[2,2,256,512]{3,2,1,0:T(8,128)(2,1)}, u32[]{:S(2)}, u32[]{:S(2)}) collective-permute-start(bf16[2,2,256,512]{3,2,1,0:T(8,128)(2,1)} %get-tuple-element.142.refs_11_), channel_id=1, source_target_pairs={{0,8},{8,0},{16,24},{24,16},{1,9},{9,1},{17,25},{25,17},{2,10},{10... | collective-permute-start | bytes 3145736 | tf_op jit(solution)/shard_map/ppermute | solution.py:815
  265.3 19.0 %collective-permute-start.45 = (bf16[256,512]{1,0:T(8,128)(2,1)}, bf16[256,512]{1,0:T(8,128)(2,1)S(1)}, u32[]{:S(2)}, u32[]{:S(2)}) collective-permute-start(bf16[256,512]{1,0:T(8,128)(2,1)} %get-tuple-element.196), channel_id=1, source_target_pairs={{0,2},{1,3},{2,0},{3,1},{4,6},{5,7},{6,4},{7,5},{8,10},{9,11},{10,... | collective-permute-start | bytes 786440 | tf_op jit(solution)/shard_map/ppermute | solution.py:815
  265.3 19.7 %collective-permute-start.46 = (bf16[256,512]{1,0:T(8,128)(2,1)}, bf16[256,512]{1,0:T(8,128)(2,1)}, u32[]{:S(2)}, u32[]{:S(2)}) collective-permute-start(bf16[256,512]{1,0:T(8,128)(2,1)} %get-tuple-element.197), channel_id=1, source_target_pairs={{0,1},{1,2},{2,3},{3,0},{4,5},{5,6},{6,7},{7,4},{8,9},{9,10},{10,1... | collective-permute-start | bytes 786440 | tf_op jit(solution)/shard_map/ppermute | solution.py:815
  267.2 37.3 %collective-permute-start.36 = (bf16[2,2,256,512]{3,2,1,0:T(8,128)(2,1)S(1)}, bf16[2,2,256,512]{3,2,1,0:T(8,128)(2,1)S(1)}, u32[]{:S(2)}, u32[]{:S(2)}) collective-permute-start(bf16[2,2,256,512]{3,2,1,0:T(8,128)(2,1)S(1)} %copy-done.13), channel_id=1, source_target_pairs={{0,16},{8,24},{16,0},{24,8},{1,17},{9,25},{17,1},{25,9},{2,18},{10... | collective-permute-start | bytes 3145736 | tf_op jit(solution)/shard_map/ppermute | solution.py:815
  271.0 16.0 %collective-permute-start.32 = (bf16[256,1024]{1,0:T(8,128)(2,1)}, bf16[256,1024]{1,0:T(8,128)(2,1)}, u32[]{:S(2)}, u32[]{:S(2)}) collective-permute-start(bf16[256,1024]{1,0:T(8,128)(2,1)} %get-tuple-element.144), channel_id=1, source_target_pairs={{0,4},{4,0},{1,5},{5,1},{2,6},{6,2},{3,7},{7,3},{8,12},{12,8},{9,1... | collective-permute-start | bytes 1572872 | tf_op jit(solution)/shard_map/ppermute | solution.py:815
  287.0 97.6 %collective-permute-start.47 = (bf16[128,512]{1,0:T(8,128)(2,1)}, bf16[128,512]{1,0:T(8,128)(2,1)}, u32[]{:S(2)}, u32[]{:S(2)}) collective-permute-start(bf16[128,512]{1,0:T(8,128)(2,1)} %constant_dynamic-slice_fusion.1), channel_id=1, source_target_pairs={{0,4},{4,0},{1,5},{5,1},{2,6},{6,2},{3,7},{7,3},{8,12},{12,8},{9,1... | collective-permute-start | bytes 393224 | tf_op jit(solution)/shard_map/ppermute | solution.py:815
  293.7 14.9 %collective-permute-start.39 = (bf16[1,2,256,512]{3,2,1,0:T(8,128)(2,1)S(1)}, bf16[1,2,256,512]{3,2,1,0:T(8,128)(2,1)}, u32[]{:S(2)}, u32[]{:S(2)}) collective-permute-start(bf16[1,2,256,512]{3,2,1,0:T(8,128)(2,1)S(1)} %add_convert_fusion.7), channel_id=1, source_target_pairs={{0,16},{8,24},{16,0},{24,8},{1,17},{9,25},{17,1},{25,9},{2,18},{10... | collective-permute-start | bytes 1572872 | tf_op jit(solution)/shard_map/ppermute | solution.py:815
  301.5 46.7 %collective-permute-start.50 = (bf16[2,2,256,512]{3,2,1,0:T(8,128)(2,1)}, bf16[2,2,256,512]{3,2,1,0:T(8,128)(2,1)S(1)}, u32[]{:S(2)}, u32[]{:S(2)}) collective-permute-start(bf16[2,2,256,512]{3,2,1,0:T(8,128)(2,1)} %get-tuple-element.161), channel_id=1, source_target_pairs={{0,8},{8,0},{16,24},{24,16},{1,9},{9,1},{17,25},{25,17},{2,10},{10... | collective-permute-start | bytes 3145736 | tf_op jit(solution)/shard_map/ppermute | solution.py:815
  303.0 47.5 %collective-permute-start.48 = (bf16[2,2,256,512]{3,2,1,0:T(8,128)(2,1)}, bf16[2,2,256,512]{3,2,1,0:T(8,128)(2,1)S(1)}, u32[]{:S(2)}, u32[]{:S(2)}) collective-permute-start(bf16[2,2,256,512]{3,2,1,0:T(8,128)(2,1)} %get-tuple-element.159), channel_id=1, source_target_pairs={{0,16},{8,24},{16,0},{24,8},{1,17},{9,25},{17,1},{25,9},{2,18},{10... | collective-permute-start | bytes 3145736 | tf_op jit(solution)/shard_map/ppermute | solution.py:815
  305.3 33.0 %collective-permute-start.37 = (bf16[1,2,256,512]{3,2,1,0:T(8,128)(2,1)S(1)}, bf16[1,2,256,512]{3,2,1,0:T(8,128)(2,1)S(1)}, u32[]{:S(2)}, u32[]{:S(2)}) collective-permute-start(bf16[1,2,256,512]{3,2,1,0:T(8,128)(2,1)S(1)} %add_convert_fusion.9), channel_id=1, source_target_pairs={{0,8},{8,0},{16,24},{24,16},{1,9},{9,1},{17,25},{25,17},{2,10},{10... | collective-permute-start | bytes 1572872 | tf_op jit(solution)/shard_map/ppermute | solution.py:815
  308.6 44.3 %collective-permute-start.27 = (bf16[2,256,1024]{2,1,0:T(8,128)(2,1)S(1)}, bf16[2,256,1024]{2,1,0:T(8,128)(2,1)}, u32[]{:S(2)}, u32[]{:S(2)}) collective-permute-start(bf16[2,256,1024]{2,1,0:T(8,128)(2,1)S(1)} %dynamic-slice_bitcast_fusion.1), channel_id=1, source_target_pairs={{0,4},{4,0},{1,5},{5,1},{2,6},{6,2},{3,7},{7,3},{8,12},{12,8},{9,1... | collective-permute-start | bytes 3145736 | tf_op jit(solution)/shard_map/ppermute | solution.py:815
  351.4 21.4 %collective-permute-start.49 = (bf16[1,2,256,512]{3,2,1,0:T(8,128)(2,1)S(1)}, bf16[1,2,256,512]{3,2,1,0:T(8,128)(2,1)S(1)}, u32[]{:S(2)}, u32[]{:S(2)}) collective-permute-start(bf16[1,2,256,512]{3,2,1,0:T(8,128)(2,1)S(1)} %add_convert_fusion.3), channel_id=1, source_target_pairs={{0,8},{8,0},{16,24},{24,16},{1,9},{9,1},{17,25},{25,17},{2,10},{10... | collective-permute-start | bytes 1572872 | tf_op jit(solution)/shard_map/ppermute | solution.py:815
  364.3 20.4 %collective-permute-start.43 = (bf16[128,512]{1,0:T(8,128)(2,1)S(1)}, bf16[128,512]{1,0:T(8,128)(2,1)S(1)}, u32[]{:S(2)}, u32[]{:S(2)}) collective-permute-start(bf16[128,512]{1,0:T(8,128)(2,1)S(1)} %constant_dynamic-slice_fusion.2), channel_id=1, source_target_pairs={{0,4},{4,0},{1,5},{5,1},{2,6},{6,2},{3,7},{7,3},{8,12},{12,8},{9,1... | collective-permute-start | bytes 393224 | tf_op jit(solution)/shard_map/ppermute | solution.py:815
  380.5 14.0 %collective-permute-start.35 = (bf16[2,256,1024]{2,1,0:T(8,128)(2,1)S(1)}, bf16[2,256,1024]{2,1,0:T(8,128)(2,1)}, u32[]{:S(2)}, u32[]{:S(2)}) collective-permute-start(bf16[2,256,1024]{2,1,0:T(8,128)(2,1)S(1)} %dynamic-slice_bitcast_fusion), channel_id=1, source_target_pairs={{0,4},{4,0},{1,5},{5,1},{2,6},{6,2},{3,7},{7,3},{8,12},{12,8},{9,1... | collective-permute-start | bytes 3145736 | tf_op jit(solution)/shard_map/ppermute | solution.py:815
  (70 other events, 595.4 us)
Sparse Core Ops, SparseCore 0:
  21.9 45.3 all-gather.5
  206.9 46.6 all-gather.7
  292.0 45.9 all-gather.9

commit v2 on v0

--- a/solution.py
+++ b/solution.py
@@ -865,7 +865,7 @@
         count = first[0].shape[0] // 2
         return [add(stacks[2 * i][count:], first[i][count:], zero=zero) for i in range(2)]
 
-    def halve_rows(keep, arrived, order, send, last):
+    def halve_rows(keep, arrived, order, send):
         items = [keep, arrived]
         for bit in order[-2::-1]:
             count = arrived.shape[0] // 2
@@ -874,11 +874,11 @@
             arrived = across(send, bit)
             items = [item[:count] for item in items] + [arrived]
             send = None
-        return add(*[item[0] for item in items], zero=last)
-
-    def halve_both(stacks, first, send, last=None):
-        near = halve_rows(stacks[0], first[0], bits, send[0], last)
-        return near, halve_rows(stacks[2], first[1], bits[::-1], send[1], last)
+        return [item[0] for item in items]
+
+    def halve_both(stacks, first, send):
+        near = halve_rows(stacks[0], first[0], bits, send[0])
+        return near, halve_rows(stacks[2], first[1], bits[::-1], send[1])
 
     def hold(arrays, after):
         anywhere = pl.BlockSpec(memory_space=pl.ANY)
@@ -933,9 +933,8 @@
             for own, first, last in zip(shards, cuts, cuts[1:])
         ]
     head_shard, hidden_shard = shards[:2]
+    attn_full = lax.all_gather(head_shard, COLS, axis=0, tiled=False)
     hidden_w = gather_pieces(hidden_shard)
-    (head_shard,) = hold((head_shard,), (hidden_w[1][0],))
-    attn_full = lax.all_gather(head_shard, COLS, axis=0, tiled=False)
     hidden_flat = [piece for group in hidden_w for piece in group]
 
     small, = call(
@@ -1112,19 +1111,16 @@
     )
     head_grads, context_grads = rest[:3], rest[3:]
     context_grads = team_send(context_grads)
-    *head_stacks, heads_done = call(
+    head_stacks = call(
         functools.partial(head_grads_kernel, col_parts, row_parts),
         (place, low_grad, attended, normed_t, context_t, *head_grads),
         head_stacks,
         scratch=[head_buffer, head_sems],
-        time=8,
+        time=1,
         in_specs=[smem] + [vmem] * 7,
         out_specs=anywhere * 4,
-        token=True,
     )
     down_first = first_messages(hidden_grads[4:])
-    down_second = second_messages(hidden_grads[4:], down_first, heads_done)
-    down_sums = halve_both(hidden_grads[4:], down_first, down_second)
     g_steps, adjoint_ends, adjoint_total, adjoint_done = call(
         functools.partial(adjoint_kernel, team),
         (logr, *context_grads),
@@ -1135,18 +1131,16 @@
         ),
         scratch=[pltpu.VMEM((length, LANES), f32)],
         time=1,
-        after=(heads_done, *down_second),
+        after=(*down_first, head_stacks[0]),
         token=True,
     )
+    adjoint_totals = everywhere(adjoint_total.astype(bf16), ("sh", "mq"))
+    down_second = second_messages(hidden_grads[4:], down_first, adjoint_done)
+    down_second = hold(down_second, (adjoint_totals,))
     up_stacks = list(hidden_grads[:4])
-    up_stacks[1::2] = hold(up_stacks[1::2], down_first)
+    up_stacks[1::2] = hold(up_stacks[1::2], (adjoint_totals,))
     up_first = first_messages(up_stacks)
-    (own_total,) = hold((adjoint_total.astype(bf16),), (*down_sums, *up_first))
-    adjoint_totals = everywhere(own_total, ("sh", "mq"))
-    grad_down = sum_over_z(*down_sums, False)
-    up_second = second_messages(up_stacks, up_first, adjoint_done)
-    up_second = hold(up_second, (adjoint_totals,))
-    *one_pieces, grad_ssm, context_done = call(
+    *one_pieces, grad_ssm = call(
         functools.partial(context_back_kernel, team),
         (place, g_steps, u_steps, adjoint_ends, adjoint_totals, logr, coef, one_part),
         (
@@ -1160,25 +1154,28 @@
         ],
         in_specs=[smem] + [vmem] * 7,
         time=1,
-        after=(*up_second, layer_pieces),
-        token=True,
+        after=(*down_second, *up_stacks[1::2]),
     )
     one_pieces = team_send(one_pieces)
-    up_sums = halve_both(up_stacks, up_first, up_second, context_done)
+    down_parts = halve_both(hidden_grads[4:], down_first, down_second)
     grad_rows, gain_one_grad, rows_done = call(
         functools.partial(input_grad_kernel, team),
         (place, x, gain_one, middle_grad, *one_pieces),
         (shaped((own_rows, width), bf16), shaped((1, width), f32)),
         in_specs=[smem] + [vmem] * (3 + team),
         time=1,
-        after=(grad_down, *up_sums),
+        after=(layer_pieces, *[parts[-1] for parts in down_parts]),
         token=True,
     )
+    down_sums = [add(*parts, zero=rows_done) for parts in down_parts]
+    up_second = second_messages(up_stacks, up_first, rows_done)
+    up_sums = [add(*parts) for parts in halve_both(up_stacks, up_first, up_second)]
+    head_stacks = list(head_stacks)
     head_stacks[1::2] = hold(head_stacks[1::2], (grad_rows,))
-    up_sums = hold(up_sums, head_stacks[1::2])
     head_first = first_messages(head_stacks)
     head_second = second_messages(head_stacks, head_first, rows_done)
-    head_sums = halve_both(head_stacks, head_first, head_second)
+    head_sums = [add(*parts) for parts in halve_both(head_stacks, head_first, head_second)]
+    grad_down = sum_over_z(*down_sums)
     grad_up = sum_over_z(*up_sums)
     grad_heads = sum_over_z(*head_sums)
     input_grad = share_rows(lax.all_gather(grad_rows, MODEL, axis=0, tiled=False), f32)

time: 432 us -> 431 us (level)
  waiting for transfers between devices: 135 us -> 158 us
  starting transfers between devices: 78.2 us -> 68.3 us
  other arithmetic: 34.3 us -> 25.3 us
    ppermute x56, waiting for transfers between devices: 121 us -> 144 us  [permute(): return lax.ppermute(value, axes, moves)]
    ppermute x56, starting transfers between devices: 58.6 us -> 49.6 us  [permute(): return lax.ppermute(value, axes, moves)]
    add x2 -> x0, other arithmetic: 4.38 us -> none  [add(): return (total if zero is None else total + zero[0, 0]).astype(bf16)]
    convert_element_type x17 -> x20, other arithmetic: 18.7 us -> 15.9 us  [add(): return (total if zero is None else total + zero[0, 0]).astype(bf16)]
    unnamed x123 -> x131, local copies, waits for them, and re-layouts: 15 us -> 16.8 us
  transfers between devices with their start and end apart: 64 -> 64, of which waited for: 23 -> 31; matrix products, arithmetic and copies ran while one was open for 14% -> 10% of each run, Pallas kernels for 19% -> 20%
where the time goes in v2:
time: 431 us; the launch traced here: 424 us
  waiting for transfers between devices  158 us (37%)
  Pallas kernels  122 us (28%)
  starting transfers between devices  68.3 us (16%)
  local copies, waits for them, and re-layouts  36.2 us (8%)
  other arithmetic  25.3 us (6%)
  between operations  14.9 us (3%)
    ppermute x56, waiting for transfers between devices, permute(): return lax.ppermute(value, axes, moves)  144 us
    pallas_call x19, Pallas kernels, call(): pl.pallas_call(run, out_shape=tuple(outs), in_specs=in_specs, out_specs=t...  122 us
    ppermute x56, starting transfers between devices, permute(): return lax.ppermute(value, axes, moves)  49.6 us
    unnamed x131, local copies, waits for them, and re-layouts  16.8 us
    convert_element_type x20, other arithmetic, add(): return (total if zero is None else total + zero[0, 0]).astype(bf16)  15.9 us
    all_to_all x4, starting transfers between devices, everywhere(): return lax.all_to_all(copies, axes, 0, 0, tiled=True)  15.6 us
    all_to_all x4, waiting for transfers between devices, everywhere(): return lax.all_to_all(copies, axes, 0, 0, tiled=True)  13 us
  transfers between devices with their start and end apart: 64, of which 31 were waited for; matrix products, arithmetic and copies ran while one was open for 10% of the time, Pallas kernels for 20%

profile of v2, /device:TPU:0, one launch (start us, length us, event | category | flops | bytes accessed | tf_op | source)
XLA Modules:
  0.0 424.4 jit_solution(11890863052108868234)
XLA Ops:
  7.9 2.6 shard_map.363
  12.7 2.9 collective-permute-start.2
  17.1 2.3 dynamic-slice_bitcast_fusion.2
  21.8 6.2 %collective-permute-done.2.refs_2_.refs_6_ = bf16[256,1024]{1,0:T(8,128)(2,1)} collective-permute-done((bf16[256,1024]{1,0:T(8,128)(2,1)S(1)}, bf16[256,1024]{1,0:T(8,128)(2,1)}, u32[]{:S(2)}, u32[]{:S(2)}) %collective-permute-start.2) | collective-permute-done | bytes 524320 | tf_op jit(solution)/shard_map/ppermute | solution.py:815
  32.8 4.9 %all-to-all-start = ((f32[32,1,1088]{2,1,0:T(1,128)}), f32[32,1,1088]{2,1,0:T(1,128)S(1)}, u32[]{:S(2)}, u32[]{:S(2)}) async-start(f32[32,1,1088]{2,1,0:T(1,128)} %reshape.232), calls=%async_computation | async-start | bytes 294912 | tf_op jit(solution)/shard_map/all_to_all | solution.py:914
  39.2 5.3 %collective-permute-start.9 = (bf16[256,1024]{1,0:T(8,128)(2,1)}, bf16[256,1024]{1,0:T(8,128)(2,1)}, u32[]{:S(2)}, u32[]{:S(2)}) collective-permute-start(bf16[256,1024]{1,0:T(8,128)(2,1)} %collective-permute-done.4.refs_4_.refs_9_), channel_id=1, source_target_pairs={{0,1},{1,2},{2,3},{3,0},{4,5},{5,6},{6,7},{7,4},{8,9},{9,10},{10,1... | collective-permute-start | bytes 1572872 | tf_op jit(solution)/shard_map/ppermute | solution.py:815
  54.3 6.5 %shard_map.365 = (bf16[512,1024]{1,0:T(8,128)(2,1)}, bf16[1024,512]{1,0:T(8,128)(2,1)}, f32[4,512,128]{2,1,0:T(8,128)}, f32[16,8,512]{2,1,0:T(8,128)}, f32[16,512]{1,0:T(8,128)}) custom-call(s32[7]{0:T(128)} %stack.25.refs_0_, bf16[512,1024]{1,0:T(8,128)(2,1)} %broadcast_select_fusion.1.refs_1_.refs_0_, f32[1,1024]{1,0:T(1,128)} %slice.175.refs_2_, ...), custom_call_target="tpu_custom_call" | custom-call | flops 5750000128 | bytes 4526108 | tf_op jit(solution)/shard_map/pallas_call | solution.py:755
  60.8 5.4 %collective-permute-done.9.refs_13_ = bf16[256,1024]{1,0:T(8,128)(2,1)} collective-permute-done((bf16[256,1024]{1,0:T(8,128)(2,1)}, bf16[256,1024]{1,0:T(8,128)(2,1)}, u32[]{:S(2)}, u32[]{:S(2)}) %collective-permute-start.9) | collective-permute-done | bytes 524320 | tf_op jit(solution)/shard_map/ppermute | solution.py:815
  70.8 4.5 %all-to-all-start.1 = ((bf16[8,16,512]{2,1,0:T(8,128)(2,1)}), bf16[8,16,512]{2,1,0:T(8,128)(2,1)S(1)}, u32[]{:S(2)}, u32[]{:S(2)}) async-start(bf16[8,16,512]{2,1,0:T(8,128)(2,1)} %broadcast_in_dim.11), calls=%async_computation.1 | async-start | bytes 262144 | tf_op jit(solution)/shard_map/all_to_all | solution.py:914
  77.6 4.5 %collective-permute-done.10.refs_9_.refs_17_ = bf16[256,1024]{1,0:T(8,128)(2,1)} collective-permute-done((bf16[256,1024]{1,0:T(8,128)(2,1)}, bf16[256,1024]{1,0:T(8,128)(2,1)}, u32[]{:S(2)}, u32[]{:S(2)}) %collective-permute-start.10) | collective-permute-done | bytes 524320 | tf_op jit(solution)/shard_map/ppermute | solution.py:815
  84.6 8.6 %collective-permute-done.11.refs_10_.refs_6_.refs_3_ = bf16[2,256,512]{2,1,0:T(8,128)(2,1)S(1)} collective-permute-done((bf16[2,256,512]{2,1,0:T(8,128)(2,1)S(1)}, bf16[2,256,512]{2,1,0:T(8,128)(2,1)S(1)}, u32[]{:S(2)}, u32[]{:S(2)}) %collective-permute-start.11) | collective-permute-done | bytes 524320 | tf_op jit(solution)/shard_map/ppermute | solution.py:815
  94.9 6.2 %shard_map.367.refs_3_ = bf16[512,512]{1,0:T(8,128)(2,1)} custom-call(s32[7]{0:T(128)} %stack.25.refs_0_, f32[4,512,128]{2,1,0:T(8,128)} %get-tuple-element.111.refs_1_.refs_2_, f32[16,8,512]{2,1,0:T(8,128)} %get-tuple-element.112.refs_2_, bf16[8,16,512]{2,1,0:T(8,128)(2,1)} %copy-done.49, f32[16,512]{1,0:T(8,128)} %get-tuple-element.199.refs_3_.refs_4_.refs_0_.refs_5_, ...), custom_call_target="tpu_custom_call" | custom-call | flops 8049999872 | bytes 2031644 | tf_op jit(solution)/shard_map/pallas_call | solution.py:755
  101.2 4.1 collective-permute-done.18.refs_13_.refs_12_
  105.7 2.6 collective-permute-done.16.refs_11_.refs_8_.refs_15_
  109.4 7.0 %collective-permute-done.15.refs_10_.refs_7_.refs_14_ = bf16[2,256,512]{2,1,0:T(8,128)(2,1)S(1)} collective-permute-done((bf16[2,256,512]{2,1,0:T(8,128)(2,1)S(1)}, bf16[2,256,512]{2,1,0:T(8,128)(2,1)S(1)}, u32[]{:S(2)}, u32[]{:S(2)}) %collective-permute-start.15) | collective-permute-done | bytes 524320 | tf_op jit(solution)/shard_map/ppermute | solution.py:815
  116.9 2.8 collective-permute-done.21.refs_16_
  121.8 9.0 %collective-permute-done.14.refs_8_.refs_5_.refs_12_ = bf16[2,256,512]{2,1,0:T(8,128)(2,1)S(1)} collective-permute-done((bf16[2,256,512]{2,1,0:T(8,128)(2,1)}, bf16[2,256,512]{2,1,0:T(8,128)(2,1)S(1)}, u32[]{:S(2)}, u32[]{:S(2)}) %collective-permute-start.14) | collective-permute-done | bytes 524320 | tf_op jit(solution)/shard_map/ppermute | solution.py:815
  131.9 7.1 %shard_map.368 = (bf16[1024,512]{1,0:T(8,128)(2,1)}, bf16[1024,512]{1,0:T(8,128)(2,1)}, bf16[3,512,512]{2,1,0:T(8,128)(2,1)}) custom-call(s32[7]{0:T(128)} %stack.25.refs_0_, bf16[512,1024]{1,0:T(8,128)(2,1)} %get-tuple-element.110.refs_1_, bf16[512,1024]{1,0:T(8,128)(2,1)} %broadcast_select_fusion.refs_2_.refs_3_, bf16[512,512]{1,0:T(8,128)(2,1)} %shard_map.367.refs_3_, ...), custom_call_target="tpu_custom_call" | custom-call | flops 1150000000 | bytes 11010076 | tf_op jit(solution)/shard_map/pallas_call | solution.py:755
  141.9 6.3 %shard_map.369 = (bf16[512,1024]{1,0:T(8,128)(2,1)}, bf16[512,512]{1,0:T(8,128)(2,1)}, bf16[4,512,512]{2,1,0:T(8,128)(2,1)}, bf16[4,512,512]{2,1,0:T(8,128)(2,1)}) custom-call(s32[7]{0:T(128)} %stack.25.refs_0_, bf16[3,512,512]{2,1,0:T(8,128)(2,1)} %get-tuple-element.115.refs_1_.refs_6_, bf16[2,256,512]{2,1,0:T(8,128)(2,1)} %copy-done.1, ...), custom_call_target="tpu_custom_call" | custom-call | flops 1150000000 | bytes 11534364 | tf_op jit(solution)/shard_map/pallas_call | solution.py:755
  152.1 4.3 %shard_map.370 = (f32[512,1024]{1,0:T(8,128)}, bf16[512,1024]{1,0:T(8,128)(2,1)}, bf16[1024,512]{1,0:T(8,128)(2,1)}) custom-call(bf16[512,1024]{1,0:T(8,128)(2,1)} %broadcast_select_fusion.1.refs_1_.refs_0_, f32[1,1024]{1,0:T(1,128)} %slice.173.refs_1_.refs_2_, bf16[512,1024]{1,0:T(8,128)(2,1)} %get-tuple-element.116.refs_2_, bf16[512,1024]{1,0:T(8,128)(2,1)} %copy-done.56), custom_call_target="tpu_custom_call" | custom-call | flops 1150000000 | bytes 7344128 | tf_op jit(solution)/shard_map/pallas_call | solution.py:755
  156.4 6.4 %collective-permute-done.25.refs_20_ = bf16[256,1024]{1,0:T(8,128)(2,1)S(1)} collective-permute-done((bf16[256,1024]{1,0:T(8,128)(2,1)}, bf16[256,1024]{1,0:T(8,128)(2,1)S(1)}, u32[]{:S(2)}, u32[]{:S(2)}) %collective-permute-start.25) | collective-permute-done | bytes 524320 | tf_op jit(solution)/shard_map/ppermute | solution.py:815
  163.6 22.1 %shard_map.371 = (bf16[256,1024]{1,0:T(8,128)(2,1)}, bf16[256,1024]{1,0:T(8,128)(2,1)}, bf16[512,1024]{1,0:T(8,128)(2,1)}, bf16[2,2,256,512]{3,2,1,0:T(8,128)(2,...) custom-call(s32[7]{0:T(128)} %stack.25.refs_0_, ...), custom_call_target="tpu_custom_call" | custom-call | flops 20700000256 | bytes 23068700 | tf_op jit(solution)/shard_map/pallas_call | solution.py:755
  194.0 15.1 %shard_map.373 = (f32[256,1024]{1,0:T(8,128)}, f32[1,1024]{1,0:T(1,128)}, bf16[512,1024]{1,0:T(8,128)(2,1)}, bf16[512,1024]{1,0:T(8,128)(2,1)}, bf16[512,512]{1,...) custom-call(s32[7]{0:T(128)} %stack.25.refs_0_, ...), custom_call_target="tpu_custom_call" | custom-call | flops 1150000000 | bytes 20979740 | tf_op jit(solution)/shard_map/pallas_call | solution.py:755
  209.3 7.0 %shard_map.374 = (bf16[2,2,256,512]{3,2,1,0:T(8,128)(2,1)}, bf16[2,2,256,512]{3,2,1,0:T(8,128)(2,1)}, bf16[2,2,256,512]{3,2,1,0:T(8,128)(2,1)}, bf16[2,2,256,512]{3,2,1,0:T(8,128)(2,1)}) custom-call(s32[7]{0:T(128)} %stack.25.refs_0_, bf16[512,1024]{1,0:T(8,128)(2,1)} %get-tuple-element.131.refs_1_, bf16[512,512]{1,0:T(8,128)(2,1)} %get-tuple-element.132.refs_2_, ...), custom_call_target="tpu_custom_call" | custom-call | flops 1150000000 | bytes 9437212 | tf_op jit(solution)/shard_map/pallas_call | solution.py:755
  217.8 6.5 %shard_map.375 = (f32[4,512,128]{2,1,0:T(8,128)}, f32[2,16,8,512]{3,2,1,0:T(8,128)}, f32[2,16,512]{2,1,0:T(8,128)}, f32[8,128]{1,0:T(8,128)}) custom-call(f32[16,512]{1,0:T(8,128)} %get-tuple-element.199.refs_3_.refs_4_.refs_0_.refs_5_, bf16[512,512]{1,0:T(8,128)(2,1)} %get-tuple-element.127.refs_1_, bf16[512,512]{1,0:T(8,128)(2,1)} %copy-done.59, ...), custom_call_target="tpu_custom_call" | custom-call | flops 1150000000 | bytes 2719744 | tf_op jit(solution)/shard_map/pallas_call | solution.py:755
  225.9 3.4 all-to-all-start.2
  230.7 3.1 add_convert_fusion.8
  233.8 4.4 %all-to-all-done.2.refs_2_.refs_4_ = bf16[8,2,16,512]{3,2,1,0:T(8,128)(2,1)S(1)} async-done(((bf16[8,2,16,512]{3,2,1,0:T(8,128)(2,1)}), bf16[8,2,16,512]{3,2,1,0:T(8,128)(2,1)S(1)}, u32[]{:S(2)}, u32[]{:S(2)}) %all-to-all-start.2) | async-done | bytes 262176 | tf_op jit(solution)/shard_map/all_to_all | solution.py:914
  239.0 12.8 %shard_map.378 = (bf16[256,1024]{1,0:T(8,128)(2,1)}, bf16[256,1024]{1,0:T(8,128)(2,1)}, f32[2,16,512]{2,1,0:T(8,128)}) custom-call(s32[7]{0:T(128)} %stack.25.refs_0_, f32[4,512,128]{2,1,0:T(8,128)} %get-tuple-element.139.refs_1_, f32[4,512,128]{2,1,0:T(8,128)} %get-tuple-element.111.refs_1_.refs_2_, f32[2,16,8,512]{3,2,1,0:T(8,128)} %get-tuple-element.140.refs_3_, ...), custom_call_target="tpu_custom_call" | custom-call | flops 1150000000 | bytes 5111836 | tf_op jit(solution)/shard_map/pallas_call | solution.py:755
  256.8 9.8 %collective-permute-done.33 = bf16[1,2,256,512]{3,2,1,0:T(8,128)(2,1)S(1)} collective-permute-done((bf16[1,2,256,512]{3,2,1,0:T(8,128)(2,1)S(1)}, bf16[1,2,256,512]{3,2,1,0:T(8,128)(2,1)S(1)}, u32[]{:S(2)}, u32[]{:S(2)}) %collective-permute-start.33) | collective-permute-done | bytes 524320 | tf_op jit(solution)/shard_map/ppermute | solution.py:815
  267.6 3.5 shard_map.379
  279.0 10.2 %collective-permute-done.38 = bf16[2,2,256,512]{3,2,1,0:T(8,128)(2,1)} collective-permute-done((bf16[2,2,256,512]{3,2,1,0:T(8,128)(2,1)}, bf16[2,2,256,512]{3,2,1,0:T(8,128)(2,1)}, u32[]{:S(2)}, u32[]{:S(2)}) %collective-permute-start.38) | collective-permute-done | bytes 1048608 | tf_op jit(solution)/shard_map/ppermute | solution.py:815
  292.3 17.0 %collective-permute-done.44 = bf16[256,512]{1,0:T(8,128)(2,1)S(1)} collective-permute-done((bf16[256,512]{1,0:T(8,128)(2,1)S(1)}, bf16[256,512]{1,0:T(8,128)(2,1)S(1)}, u32[]{:S(2)}, u32[]{:S(2)}) %collective-permute-start.44) | collective-permute-done | bytes 262176 | tf_op jit(solution)/shard_map/ppermute | solution.py:815
  312.2 13.9 %collective-permute-done.45 = bf16[256,512]{1,0:T(8,128)(2,1)S(1)} collective-permute-done((bf16[256,512]{1,0:T(8,128)(2,1)S(1)}, bf16[256,512]{1,0:T(8,128)(2,1)S(1)}, u32[]{:S(2)}, u32[]{:S(2)}) %collective-permute-start.45) | collective-permute-done | bytes 262176 | tf_op jit(solution)/shard_map/ppermute | solution.py:815
  329.0 10.6 %collective-permute-done.37 = bf16[1,2,256,512]{3,2,1,0:T(8,128)(2,1)S(1)} collective-permute-done((bf16[1,2,256,512]{3,2,1,0:T(8,128)(2,1)S(1)}, bf16[1,2,256,512]{3,2,1,0:T(8,128)(2,1)S(1)}, u32[]{:S(2)}, u32[]{:S(2)}) %collective-permute-start.37) | collective-permute-done | bytes 524320 | tf_op jit(solution)/shard_map/ppermute | solution.py:815
  341.0 5.9 %collective-permute-done.40 = bf16[256,512]{1,0:T(8,128)(2,1)S(1)} collective-permute-done((bf16[256,512]{1,0:T(8,128)(2,1)S(1)}, bf16[256,512]{1,0:T(8,128)(2,1)S(1)}, u32[]{:S(2)}, u32[]{:S(2)}) %collective-permute-start.40) | collective-permute-done | bytes 262176 | tf_op jit(solution)/shard_map/ppermute | solution.py:815
  354.8 3.4 shard_map.372.refs_9_
  358.4 2.9 collective-permute-done.51
  361.9 4.8 %collective-permute-done.42 = bf16[256,512]{1,0:T(8,128)(2,1)S(1)} collective-permute-done((bf16[256,512]{1,0:T(8,128)(2,1)S(1)}, bf16[256,512]{1,0:T(8,128)(2,1)S(1)}, u32[]{:S(2)}, u32[]{:S(2)}) %collective-permute-start.42) | collective-permute-done | bytes 262176 | tf_op jit(solution)/shard_map/ppermute | solution.py:815
  367.0 2.6 collective-permute-done.52
  375.7 2.6 all-to-all-start.3
  379.8 3.9 collective-permute-start.54
  385.1 5.0 %shard_map.381 = (f32[128,1024]{1,0:T(8,128)}, f32[128,1024]{1,0:T(8,128)}, f32[128,1024]{1,0:T(8,128)}, f32[1024,128]{1,0:T(8,128)}, f32[1024,128]{1,0:T(8,128)...) custom-call(s32[7]{0:T(128)} %stack.25.refs_0_, bf16[256,512]{1,0:T(8,128)(2,1)} %copy-done.39, bf16[128,512]{1,0:T(8,128)(2,1)} %copy-done.61, ...), custom_call_target="tpu_custom_call" | custom-call | flops 4600000000 | bytes 7078940 | tf_op jit(solution)/shard_map/pallas_call | solution.py:755
  394.3 4.2 shard_map.380.refs_10_
  399.1 3.2 shard_map.383
  403.7 2.8 all-to-all-start.4
  407.0 6.8 %all-to-all-done.4.refs_0_ = f32[32,2,128]{2,1,0:T(2,128)S(1)} async-done(((f32[32,2,128]{2,1,0:T(2,128)}), f32[32,2,128]{2,1,0:T(2,128)S(1)}, u32[]{:S(2)}, u32[]{:S(2)}) %all-to-all-start.4) | async-done | bytes 32800 | tf_op jit(solution)/shard_map/all_to_all | solution.py:914
  414.4 3.2 shard_map.386
  (304 shorter events, 109.3 us)
Async XLA Ops:
  7.2 60.1 %all-gather.6.cloned.1.call-start = ((), (), s32[]{:S(2)}) async-start(), calls=%async_computation.5 | async-start | bytes 1310720 | tf_op jit(solution)/shard_map/all_gather | solution.py:936
  12.0 32.5 %collective-permute-start = (bf16[512,1024]{1,0:T(8,128)(2,1)}, bf16[512,1024]{1,0:T(8,128)(2,1)}, u32[]{:S(2)}, u32[]{:S(2)}) collective-permute-start(bf16[512,1024]{1,0:T(8,128)(2,1)} %dynamic-slice_bitcast_fusion.3), channel_id=1, source_target_pairs={{0,4},{4,0},{1,5},{5,1},{2,6},{6,2},{3,7},{7,3},{8,12},{12,8},{9,1... | collective-permute-start | bytes 3145736 | tf_op jit(solution)/shard_map/ppermute | solution.py:815
  12.7 15.3 %collective-permute-start.2 = (bf16[256,1024]{1,0:T(8,128)(2,1)S(1)}, bf16[256,1024]{1,0:T(8,128)(2,1)}, u32[]{:S(2)}, u32[]{:S(2)}) collective-permute-start(bf16[256,1024]{1,0:T(8,128)(2,1)S(1)} %maximum_select_fusion.refs_5_), channel_id=1, source_target_pairs={{0,8},{8,0},{16,24},{24,16},{1,9},{9,1},{17,25},{25,17},{2,10},{10... | collective-permute-start | bytes 1572872 | tf_op jit(solution)/shard_map/ppermute | solution.py:815
  15.6 13.8 %collective-permute-start.3 = (bf16[256,1024]{1,0:T(8,128)(2,1)S(1)}, bf16[256,1024]{1,0:T(8,128)(2,1)}, u32[]{:S(2)}, u32[]{:S(2)}) collective-permute-start(bf16[256,1024]{1,0:T(8,128)(2,1)S(1)} %maximum_select_fusion.refs_5_), channel_id=1, source_target_pairs={{0,16},{8,24},{16,0},{24,8},{1,17},{9,25},{17,1},{25,9},{2,18},{10... | collective-permute-start | bytes 1572872 | tf_op jit(solution)/shard_map/ppermute | solution.py:815
  19.4 34.9 %collective-permute-start.5 = (bf16[512,1024]{1,0:T(8,128)(2,1)}, bf16[512,1024]{1,0:T(8,128)(2,1)}, u32[]{:S(2)}, u32[]{:S(2)}) collective-permute-start(bf16[512,1024]{1,0:T(8,128)(2,1)} %dynamic-slice_bitcast_fusion.2), channel_id=1, source_target_pairs={{0,4},{4,0},{1,5},{5,1},{2,6},{6,2},{3,7},{7,3},{8,12},{12,8},{9,1... | collective-permute-start | bytes 3145736 | tf_op jit(solution)/shard_map/ppermute | solution.py:815
  19.4 19.8 %collective-permute-start.4 = (bf16[256,1024]{1,0:T(8,128)(2,1)S(1)}, bf16[256,1024]{1,0:T(8,128)(2,1)}, u32[]{:S(2)}, u32[]{:S(2)}) collective-permute-start(bf16[256,1024]{1,0:T(8,128)(2,1)S(1)} %maximum_select_fusion.refs_5_), channel_id=1, source_target_pairs={{0,1},{1,2},{2,3},{3,0},{4,5},{5,6},{6,7},{7,4},{8,9},{9,10},{10,1... | collective-permute-start | bytes 1572872 | tf_op jit(solution)/shard_map/ppermute | solution.py:815
  32.8 16.7 %all-to-all-start = ((f32[32,1,1088]{2,1,0:T(1,128)}), f32[32,1,1088]{2,1,0:T(1,128)S(1)}, u32[]{:S(2)}, u32[]{:S(2)}) async-start(f32[32,1,1088]{2,1,0:T(1,128)} %reshape.232), calls=%async_computation | async-start | bytes 294912 | tf_op jit(solution)/shard_map/all_to_all | solution.py:914
  39.2 27.0 %collective-permute-start.9 = (bf16[256,1024]{1,0:T(8,128)(2,1)}, bf16[256,1024]{1,0:T(8,128)(2,1)}, u32[]{:S(2)}, u32[]{:S(2)}) collective-permute-start(bf16[256,1024]{1,0:T(8,128)(2,1)} %collective-permute-done.4.refs_4_.refs_9_), channel_id=1, source_target_pairs={{0,1},{1,2},{2,3},{3,0},{4,5},{5,6},{6,7},{7,4},{8,9},{9,10},{10,1... | collective-permute-start | bytes 1572872 | tf_op jit(solution)/shard_map/ppermute | solution.py:815
  44.5 24.1 %collective-permute-start.8 = (bf16[256,1024]{1,0:T(8,128)(2,1)}, bf16[256,1024]{1,0:T(8,128)(2,1)S(1)}, u32[]{:S(2)}, u32[]{:S(2)}) collective-permute-start(bf16[256,1024]{1,0:T(8,128)(2,1)} %collective-permute-done.4.refs_4_.refs_9_), channel_id=1, source_target_pairs={{0,16},{8,24},{16,0},{24,8},{1,17},{9,25},{17,1},{25,9},{2,18},{10... | collective-permute-start | bytes 1572872 | tf_op jit(solution)/shard_map/ppermute | solution.py:815
  44.5 25.2 %collective-permute-start.7 = (bf16[256,1024]{1,0:T(8,128)(2,1)}, bf16[256,1024]{1,0:T(8,128)(2,1)}, u32[]{:S(2)}, u32[]{:S(2)}) collective-permute-start(bf16[256,1024]{1,0:T(8,128)(2,1)} %collective-permute-done.4.refs_4_.refs_9_), channel_id=1, source_target_pairs={{0,8},{8,0},{16,24},{24,16},{1,9},{9,1},{17,25},{25,17},{2,10},{10... | collective-permute-start | bytes 1572872 | tf_op jit(solution)/shard_map/ppermute | solution.py:815
  44.5 31.1 %collective-permute-start.6 = (bf16[256,1024]{1,0:T(8,128)(2,1)}, bf16[256,1024]{1,0:T(8,128)(2,1)}, u32[]{:S(2)}, u32[]{:S(2)}) collective-permute-start(bf16[256,1024]{1,0:T(8,128)(2,1)} %collective-permute-done.2.refs_2_.refs_6_), channel_id=1, source_target_pairs={{0,16},{8,24},{16,0},{24,8},{1,17},{9,25},{17,1},{25,9},{2,18},{10... | collective-permute-start | bytes 1572872 | tf_op jit(solution)/shard_map/ppermute | solution.py:815
  66.2 15.9 %collective-permute-start.10 = (bf16[256,1024]{1,0:T(8,128)(2,1)}, bf16[256,1024]{1,0:T(8,128)(2,1)}, u32[]{:S(2)}, u32[]{:S(2)}) collective-permute-start(bf16[256,1024]{1,0:T(8,128)(2,1)} %collective-permute-done.9.refs_13_), channel_id=1, source_target_pairs={{0,1},{1,2},{2,3},{3,0},{4,5},{5,6},{6,7},{7,4},{8,9},{9,10},{10,1... | collective-permute-start | bytes 1572872 | tf_op jit(solution)/shard_map/ppermute | solution.py:815
  66.2 17.1 %collective-permute-start.19 = (bf16[256,1024]{1,0:T(8,128)(2,1)}, bf16[256,1024]{1,0:T(8,128)(2,1)S(1)}, u32[]{:S(2)}, u32[]{:S(2)}) collective-permute-start(bf16[256,1024]{1,0:T(8,128)(2,1)} %collective-permute-done.9.refs_13_), channel_id=1, source_target_pairs={{0,8},{8,0},{16,24},{24,16},{1,9},{9,1},{17,25},{25,17},{2,10},{10... | collective-permute-start | bytes 1572872 | tf_op jit(solution)/shard_map/ppermute | solution.py:815
  68.6 24.7 %collective-permute-start.11 = (bf16[2,256,512]{2,1,0:T(8,128)(2,1)S(1)}, bf16[2,256,512]{2,1,0:T(8,128)(2,1)S(1)}, u32[]{:S(2)}, u32[]{:S(2)}) collective-permute-start(bf16[2,256,512]{2,1,0:T(8,128)(2,1)S(1)} %get-tuple-element.197.refs_5_.refs_2_.refs_9_), channel_id=1, source_target_pairs={{0,8},{8,0},{16,24},{24,16},{1,9},{9,1},{17,25},{25,17},{2,10},{10... | collective-permute-start | bytes 1572872 | tf_op jit(solution)/shard_map/ppermute | solution.py:815
  69.7 24.1 %collective-permute-start.12 = (bf16[2,256,512]{2,1,0:T(8,128)(2,1)S(1)}, bf16[2,256,512]{2,1,0:T(8,128)(2,1)S(1)}, u32[]{:S(2)}, u32[]{:S(2)}) collective-permute-start(bf16[2,256,512]{2,1,0:T(8,128)(2,1)S(1)} %get-tuple-element.197.refs_5_.refs_2_.refs_9_), channel_id=1, source_target_pairs={{0,16},{8,24},{16,0},{24,8},{1,17},{9,25},{17,1},{25,9},{2,18},{10... | collective-permute-start | bytes 1572872 | tf_op jit(solution)/shard_map/ppermute | solution.py:815
  70.8 23.4 %all-to-all-start.1 = ((bf16[8,16,512]{2,1,0:T(8,128)(2,1)}), bf16[8,16,512]{2,1,0:T(8,128)(2,1)S(1)}, u32[]{:S(2)}, u32[]{:S(2)}) async-start(bf16[8,16,512]{2,1,0:T(8,128)(2,1)} %broadcast_in_dim.11), calls=%async_computation.1 | async-start | bytes 262144 | tf_op jit(solution)/shard_map/all_to_all | solution.py:914
  75.3 191.4 %all-gather.8.cloned.1.call-start = ((), (), s32[]{:S(2)}) async-start(), calls=%async_computation.6 | async-start | bytes 2621440 | tf_op jit(solution)/shard_map/all_gather | solution.py:1080
  75.6 25.6 %collective-permute-start.20 = (bf16[256,1024]{1,0:T(8,128)(2,1)}, bf16[256,1024]{1,0:T(8,128)(2,1)}, u32[]{:S(2)}, u32[]{:S(2)}) collective-permute-start(bf16[256,1024]{1,0:T(8,128)(2,1)} %collective-permute-done.9.refs_13_), channel_id=1, source_target_pairs={{0,16},{8,24},{16,0},{24,8},{1,17},{9,25},{17,1},{25,9},{2,18},{10... | collective-permute-start | bytes 1572872 | tf_op jit(solution)/shard_map/ppermute | solution.py:815
  82.1 23.2 %collective-permute-start.18 = (bf16[256,1024]{1,0:T(8,128)(2,1)}, bf16[256,1024]{1,0:T(8,128)(2,1)}, u32[]{:S(2)}, u32[]{:S(2)}) collective-permute-start(bf16[256,1024]{1,0:T(8,128)(2,1)} %copy-done.57), channel_id=1, source_target_pairs={{0,8},{8,0},{16,24},{24,16},{1,9},{9,1},{17,25},{25,17},{2,10},{10... | collective-permute-start | bytes 1572872 | tf_op jit(solution)/shard_map/ppermute | solution.py:815
  84.1 24.2 %collective-permute-start.16 = (bf16[2,256,512]{2,1,0:T(8,128)(2,1)S(1)}, bf16[2,256,512]{2,1,0:T(8,128)(2,1)S(1)}, u32[]{:S(2)}, u32[]{:S(2)}) collective-permute-start(bf16[2,256,512]{2,1,0:T(8,128)(2,1)S(1)} %get-tuple-element.196.refs_9_.refs_6_.refs_13_), channel_id=1, source_target_pairs={{0,16},{8,24},{16,0},{24,8},{1,17},{9,25},{17,1},{25,9},{2,18},{10... | collective-permute-start | bytes 1572872 | tf_op jit(solution)/shard_map/ppermute | solution.py:815
  93.2 23.2 %collective-permute-start.15 = (bf16[2,256,512]{2,1,0:T(8,128)(2,1)S(1)}, bf16[2,256,512]{2,1,0:T(8,128)(2,1)S(1)}, u32[]{:S(2)}, u32[]{:S(2)}) collective-permute-start(bf16[2,256,512]{2,1,0:T(8,128)(2,1)S(1)} %get-tuple-element.196.refs_9_.refs_6_.refs_13_), channel_id=1, source_target_pairs={{0,8},{8,0},{16,24},{24,16},{1,9},{9,1},{17,25},{25,17},{2,10},{10... | collective-permute-start | bytes 1572872 | tf_op jit(solution)/shard_map/ppermute | solution.py:815
  93.7 26.0 %collective-permute-start.21 = (bf16[256,1024]{1,0:T(8,128)(2,1)}, bf16[256,1024]{1,0:T(8,128)(2,1)}, u32[]{:S(2)}, u32[]{:S(2)}) collective-permute-start(bf16[256,1024]{1,0:T(8,128)(2,1)} %copy-done.41), channel_id=1, source_target_pairs={{0,16},{8,24},{16,0},{24,8},{1,17},{9,25},{17,1},{25,9},{2,18},{10... | collective-permute-start | bytes 1572872 | tf_op jit(solution)/shard_map/ppermute | solution.py:815
  101.1 20.7 %collective-permute-start.13 = (bf16[512,512]{1,0:T(8,128)(2,1)}, bf16[512,512]{1,0:T(8,128)(2,1)S(1)}, u32[]{:S(2)}, u32[]{:S(2)}) collective-permute-start(bf16[512,512]{1,0:T(8,128)(2,1)} %shard_map.367.refs_3_), channel_id=1, source_target_pairs={{0,4},{4,0},{1,5},{5,1},{2,6},{6,2},{3,7},{7,3},{8,12},{12,8},{9,1... | collective-permute-start | bytes 1572872 | tf_op jit(solution)/shard_map/ppermute | solution.py:815
  105.3 25.5 %collective-permute-start.14 = (bf16[2,256,512]{2,1,0:T(8,128)(2,1)}, bf16[2,256,512]{2,1,0:T(8,128)(2,1)S(1)}, u32[]{:S(2)}, u32[]{:S(2)}) collective-permute-start(bf16[2,256,512]{2,1,0:T(8,128)(2,1)} %copy-done.8), channel_id=1, source_target_pairs={{0,16},{8,24},{16,0},{24,8},{1,17},{9,25},{17,1},{25,9},{2,18},{10... | collective-permute-start | bytes 1572872 | tf_op jit(solution)/shard_map/ppermute | solution.py:815
  108.3 22.5 %collective-permute-start.17 = (bf16[2,256,512]{2,1,0:T(8,128)(2,1)S(1)}, bf16[2,256,512]{2,1,0:T(8,128)(2,1)S(1)}, u32[]{:S(2)}, u32[]{:S(2)}) collective-permute-start(bf16[2,256,512]{2,1,0:T(8,128)(2,1)S(1)} %collective-permute-done.16.refs_11_.refs_8_.refs_15_), channel_id=1, source_target_pairs={{0,8},{8,0},{16,24},{24,16},{1,9},{9,1},{17,25},{25,17},{2,10},{10... | collective-permute-start | bytes 1572872 | tf_op jit(solution)/shard_map/ppermute | solution.py:815
  116.4 24.5 %collective-permute-start.23 = (bf16[256,1024]{1,0:T(8,128)(2,1)}, bf16[256,1024]{1,0:T(8,128)(2,1)S(1)}, u32[]{:S(2)}, u32[]{:S(2)}) collective-permute-start(bf16[256,1024]{1,0:T(8,128)(2,1)} %collective-permute-done.10.refs_9_.refs_17_), channel_id=1, source_target_pairs={{0,16},{8,24},{16,0},{24,8},{1,17},{9,25},{17,1},{25,9},{2,18},{10... | collective-permute-start | bytes 1572872 | tf_op jit(solution)/shard_map/ppermute | solution.py:815
  119.7 21.2 %collective-permute-start.22 = (bf16[256,1024]{1,0:T(8,128)(2,1)}, bf16[256,1024]{1,0:T(8,128)(2,1)S(1)}, u32[]{:S(2)}, u32[]{:S(2)}) collective-permute-start(bf16[256,1024]{1,0:T(8,128)(2,1)} %collective-permute-done.10.refs_9_.refs_17_), channel_id=1, source_target_pairs={{0,8},{8,0},{16,24},{24,16},{1,9},{9,1},{17,25},{25,17},{2,10},{10... | collective-permute-start | bytes 1572872 | tf_op jit(solution)/shard_map/ppermute | solution.py:815
  148.2 14.6 %collective-permute-start.25 = (bf16[256,1024]{1,0:T(8,128)(2,1)}, bf16[256,1024]{1,0:T(8,128)(2,1)S(1)}, u32[]{:S(2)}, u32[]{:S(2)}) collective-permute-start(bf16[256,1024]{1,0:T(8,128)(2,1)} %copy-done.44), channel_id=1, source_target_pairs={{0,8},{8,0},{16,24},{24,16},{1,9},{9,1},{17,25},{25,17},{2,10},{10... | collective-permute-start | bytes 1572872 | tf_op jit(solution)/shard_map/ppermute | solution.py:815
  190.2 26.1 %collective-permute-start.30 = (bf16[2,2,256,512]{3,2,1,0:T(8,128)(2,1)}, bf16[2,2,256,512]{3,2,1,0:T(8,128)(2,1)S(1)}, u32[]{:S(2)}, u32[]{:S(2)}) collective-permute-start(bf16[2,2,256,512]{3,2,1,0:T(8,128)(2,1)} %get-tuple-element.129), channel_id=1, source_target_pairs={{0,16},{8,24},{16,0},{24,8},{1,17},{9,25},{17,1},{25,9},{2,18},{10... | collective-permute-start | bytes 3145736 | tf_op jit(solution)/shard_map/ppermute | solution.py:815
  190.8 25.6 %collective-permute-start.31 = (bf16[2,2,256,512]{3,2,1,0:T(8,128)(2,1)}, bf16[2,2,256,512]{3,2,1,0:T(8,128)(2,1)S(1)}, u32[]{:S(2)}, u32[]{:S(2)}) collective-permute-start(bf16[2,2,256,512]{3,2,1,0:T(8,128)(2,1)} %get-tuple-element.130), channel_id=1, source_target_pairs={{0,8},{8,0},{16,24},{24,16},{1,9},{9,1},{17,25},{25,17},{2,10},{10... | collective-permute-start | bytes 3145736 | tf_op jit(solution)/shard_map/ppermute | solution.py:815
  229.3 149.0 %all-gather.10.cloned.1.call-start = ((), (), s32[]{:S(2)}) async-start(), calls=%async_computation.7 | async-start | bytes 2621440 | tf_op jit(solution)/shard_map/all_gather | solution.py:1181
  251.8 14.8 %collective-permute-start.33 = (bf16[1,2,256,512]{3,2,1,0:T(8,128)(2,1)S(1)}, bf16[1,2,256,512]{3,2,1,0:T(8,128)(2,1)S(1)}, u32[]{:S(2)}, u32[]{:S(2)}) collective-permute-start(bf16[1,2,256,512]{3,2,1,0:T(8,128)(2,1)S(1)} %copy-done.3), channel_id=1, source_target_pairs={{0,8},{8,0},{16,24},{24,16},{1,9},{9,1},{17,25},{25,17},{2,10},{10... | collective-permute-start | bytes 1572872 | tf_op jit(solution)/shard_map/ppermute | solution.py:815
  252.0 14.7 %collective-permute-start.34 = (bf16[1,2,256,512]{3,2,1,0:T(8,128)(2,1)S(1)}, bf16[1,2,256,512]{3,2,1,0:T(8,128)(2,1)S(1)}, u32[]{:S(2)}, u32[]{:S(2)}) collective-permute-start(bf16[1,2,256,512]{3,2,1,0:T(8,128)(2,1)S(1)} %copy-done.2), channel_id=1, source_target_pairs={{0,16},{8,24},{16,0},{24,8},{1,17},{9,25},{17,1},{25,9},{2,18},{10... | collective-permute-start | bytes 1572872 | tf_op jit(solution)/shard_map/ppermute | solution.py:815
  253.0 57.3 %collective-permute-start.36 = (bf16[2,2,256,512]{3,2,1,0:T(8,128)(2,1)S(1)}, bf16[2,2,256,512]{3,2,1,0:T(8,128)(2,1)}, u32[]{:S(2)}, u32[]{:S(2)}) collective-permute-start(bf16[2,2,256,512]{3,2,1,0:T(8,128)(2,1)S(1)} %copy-done.15), channel_id=1, source_target_pairs={{0,16},{8,24},{16,0},{24,8},{1,17},{9,25},{17,1},{25,9},{2,18},{10... | collective-permute-start | bytes 3145736 | tf_op jit(solution)/shard_map/ppermute | solution.py:815
  254.0 35.2 %collective-permute-start.38 = (bf16[2,2,256,512]{3,2,1,0:T(8,128)(2,1)}, bf16[2,2,256,512]{3,2,1,0:T(8,128)(2,1)}, u32[]{:S(2)}, u32[]{:S(2)}) collective-permute-start(bf16[2,2,256,512]{3,2,1,0:T(8,128)(2,1)} %get-tuple-element.151.refs_11_), channel_id=1, source_target_pairs={{0,8},{8,0},{16,24},{24,16},{1,9},{9,1},{17,25},{25,17},{2,10},{10... | collective-permute-start | bytes 3145736 | tf_op jit(solution)/shard_map/ppermute | solution.py:815
  271.1 77.6 %collective-permute-start.50 = (bf16[2,2,256,512]{3,2,1,0:T(8,128)(2,1)}, bf16[2,2,256,512]{3,2,1,0:T(8,128)(2,1)S(1)}, u32[]{:S(2)}, u32[]{:S(2)}) collective-permute-start(bf16[2,2,256,512]{3,2,1,0:T(8,128)(2,1)} %get-tuple-element.163), channel_id=1, source_target_pairs={{0,8},{8,0},{16,24},{24,16},{1,9},{9,1},{17,25},{25,17},{2,10},{10... | collective-permute-start | bytes 3145736 | tf_op jit(solution)/shard_map/ppermute | solution.py:815
  274.2 77.0 %collective-permute-start.48 = (bf16[2,2,256,512]{3,2,1,0:T(8,128)(2,1)}, bf16[2,2,256,512]{3,2,1,0:T(8,128)(2,1)S(1)}, u32[]{:S(2)}, u32[]{:S(2)}) collective-permute-start(bf16[2,2,256,512]{3,2,1,0:T(8,128)(2,1)} %get-tuple-element.161), channel_id=1, source_target_pairs={{0,16},{8,24},{16,0},{24,8},{1,17},{9,25},{17,1},{25,9},{2,18},{10... | collective-permute-start | bytes 3145736 | tf_op jit(solution)/shard_map/ppermute | solution.py:815
  274.9 79.8 %collective-permute-start.27 = (bf16[2,256,1024]{2,1,0:T(8,128)(2,1)S(1)}, bf16[2,256,1024]{2,1,0:T(8,128)(2,1)}, u32[]{:S(2)}, u32[]{:S(2)}) collective-permute-start(bf16[2,256,1024]{2,1,0:T(8,128)(2,1)S(1)} %dynamic-slice_bitcast_fusion.1), channel_id=1, source_target_pairs={{0,4},{4,0},{1,5},{5,1},{2,6},{6,2},{3,7},{7,3},{8,12},{12,8},{9,1... | collective-permute-start | bytes 3145736 | tf_op jit(solution)/shard_map/ppermute | solution.py:815
  289.2 20.1 %collective-permute-start.44 = (bf16[256,512]{1,0:T(8,128)(2,1)S(1)}, bf16[256,512]{1,0:T(8,128)(2,1)S(1)}, u32[]{:S(2)}, u32[]{:S(2)}) collective-permute-start(bf16[256,512]{1,0:T(8,128)(2,1)S(1)} %slice_bitcast_fusion.4), channel_id=1, source_target_pairs={{0,3},{1,0},{2,1},{3,2},{4,7},{5,4},{6,5},{7,6},{8,11},{9,8},{10,9... | collective-permute-start | bytes 786440 | tf_op jit(solution)/shard_map/ppermute | solution.py:815
  309.3 18.4 %collective-permute-start.39 = (bf16[1,2,256,512]{3,2,1,0:T(8,128)(2,1)S(1)}, bf16[1,2,256,512]{3,2,1,0:T(8,128)(2,1)S(1)}, u32[]{:S(2)}, u32[]{:S(2)}) collective-permute-start(bf16[1,2,256,512]{3,2,1,0:T(8,128)(2,1)S(1)} %add_convert_fusion.5), channel_id=1, source_target_pairs={{0,16},{8,24},{16,0},{24,8},{1,17},{9,25},{17,1},{25,9},{2,18},{10... | collective-permute-start | bytes 1572872 | tf_op jit(solution)/shard_map/ppermute | solution.py:815
  310.3 15.8 %collective-permute-start.45 = (bf16[256,512]{1,0:T(8,128)(2,1)S(1)}, bf16[256,512]{1,0:T(8,128)(2,1)S(1)}, u32[]{:S(2)}, u32[]{:S(2)}) collective-permute-start(bf16[256,512]{1,0:T(8,128)(2,1)S(1)} %fusion.7), channel_id=1, source_target_pairs={{0,3},{1,0},{2,1},{3,2},{4,7},{5,4},{6,5},{7,6},{8,11},{9,8},{10,9... | collective-permute-start | bytes 786440 | tf_op jit(solution)/shard_map/ppermute | solution.py:815
  326.1 13.5 %collective-permute-start.37 = (bf16[1,2,256,512]{3,2,1,0:T(8,128)(2,1)S(1)}, bf16[1,2,256,512]{3,2,1,0:T(8,128)(2,1)S(1)}, u32[]{:S(2)}, u32[]{:S(2)}) collective-permute-start(bf16[1,2,256,512]{3,2,1,0:T(8,128)(2,1)S(1)} %add_convert_fusion.7), channel_id=1, source_target_pairs={{0,8},{8,0},{16,24},{24,16},{1,9},{9,1},{17,25},{25,17},{2,10},{10... | collective-permute-start | bytes 1572872 | tf_op jit(solution)/shard_map/ppermute | solution.py:815
  340.9 42.9 %collective-permute-start.47 = (bf16[128,512]{1,0:T(8,128)(2,1)S(1)}, bf16[128,512]{1,0:T(8,128)(2,1)S(1)}, u32[]{:S(2)}, u32[]{:S(2)}) collective-permute-start(bf16[128,512]{1,0:T(8,128)(2,1)S(1)} %constant_dynamic-slice_fusion.1), channel_id=1, source_target_pairs={{0,4},{4,0},{1,5},{5,1},{2,6},{6,2},{3,7},{7,3},{8,12},{12,8},{9,1... | collective-permute-start | bytes 393224 | tf_op jit(solution)/shard_map/ppermute | solution.py:815
  353.1 18.8 %collective-permute-start.49 = (bf16[1,2,256,512]{3,2,1,0:T(8,128)(2,1)S(1)}, bf16[1,2,256,512]{3,2,1,0:T(8,128)(2,1)S(1)}, u32[]{:S(2)}, u32[]{:S(2)}) collective-permute-start(bf16[1,2,256,512]{3,2,1,0:T(8,128)(2,1)S(1)} %add_convert_fusion.3), channel_id=1, source_target_pairs={{0,8},{8,0},{16,24},{24,16},{1,9},{9,1},{17,25},{25,17},{2,10},{10... | collective-permute-start | bytes 1572872 | tf_op jit(solution)/shard_map/ppermute | solution.py:815
  366.9 16.9 %collective-permute-start.43 = (bf16[128,512]{1,0:T(8,128)(2,1)S(1)}, bf16[128,512]{1,0:T(8,128)(2,1)S(1)}, u32[]{:S(2)}, u32[]{:S(2)}) collective-permute-start(bf16[128,512]{1,0:T(8,128)(2,1)S(1)} %constant_dynamic-slice_fusion.2), channel_id=1, source_target_pairs={{0,4},{4,0},{1,5},{5,1},{2,6},{6,2},{3,7},{7,3},{8,12},{12,8},{9,1... | collective-permute-start | bytes 393224 | tf_op jit(solution)/shard_map/ppermute | solution.py:815
  375.7 14.4 %all-to-all-start.3 = ((f32[32,1,1088]{2,1,0:T(1,128)}), f32[32,1,1088]{2,1,0:T(1,128)S(1)}, u32[]{:S(2)}, u32[]{:S(2)}) async-start(f32[32,1,1088]{2,1,0:T(1,128)} %reshape.234), calls=%async_computation.3 | async-start | bytes 294912 | tf_op jit(solution)/shard_map/all_to_all | solution.py:1192
  379.6 14.7 %collective-permute-start.35 = (bf16[2,256,1024]{2,1,0:T(8,128)(2,1)S(1)}, bf16[2,256,1024]{2,1,0:T(8,128)(2,1)}, u32[]{:S(2)}, u32[]{:S(2)}) collective-permute-start(bf16[2,256,1024]{2,1,0:T(8,128)(2,1)S(1)} %dynamic-slice_bitcast_fusion), channel_id=1, source_target_pairs={{0,4},{4,0},{1,5},{5,1},{2,6},{6,2},{3,7},{7,3},{8,12},{12,8},{9,1... | collective-permute-start | bytes 3145736 | tf_op jit(solution)/shard_map/ppermute | solution.py:815
  379.8 14.2 %collective-permute-start.54 = (bf16[256,512]{1,0:T(8,128)(2,1)S(1)}, bf16[256,512]{1,0:T(8,128)(2,1)S(1)}, u32[]{:S(2)}, u32[]{:S(2)}) collective-permute-start(bf16[256,512]{1,0:T(8,128)(2,1)S(1)} %fusion.5), channel_id=1, source_target_pairs={{0,3},{1,0},{2,1},{3,2},{4,7},{5,4},{6,5},{7,6},{8,11},{9,8},{10,9... | collective-permute-start | bytes 786440 | tf_op jit(solution)/shard_map/ppermute | solution.py:815
  (79 other events, 586.8 us)
Sparse Core Ops, SparseCore 0:
  21.9 45.3 all-gather.5
  190.2 45.2 all-gather.7
  271.2 54.0 all-gather.9

commit v3 on v2

--- a/solution.py
+++ b/solution.py
@@ -1174,9 +1174,11 @@
     head_stacks[1::2] = hold(head_stacks[1::2], (grad_rows,))
     head_first = first_messages(head_stacks)
     head_second = second_messages(head_stacks, head_first, rows_done)
-    head_sums = [add(*parts) for parts in halve_both(head_stacks, head_first, head_second)]
+    down_sums = hold(down_sums, head_second)
+    up_sums = hold(up_sums, head_second)
     grad_down = sum_over_z(*down_sums)
     grad_up = sum_over_z(*up_sums)
+    head_sums = [add(*parts) for parts in halve_both(head_stacks, head_first, head_second)]
     grad_heads = sum_over_z(*head_sums)
     input_grad = share_rows(lax.all_gather(grad_rows, MODEL, axis=0, tiled=False), f32)
 

time: 431 us -> 429 us (level)
  waiting for transfers between devices: 158 us -> 131 us
  starting transfers between devices: 68.3 us -> 80.6 us
  other arithmetic: 25.3 us -> 33.4 us
  local copies, waits for them, and re-layouts: 36.2 us -> 40.9 us
    ppermute x56, waiting for transfers between devices: 144 us -> 114 us  [permute(): return lax.ppermute(value, axes, moves)]
    ppermute x56, starting transfers between devices: 49.6 us -> 61.2 us  [permute(): return lax.ppermute(value, axes, moves)]
    convert_element_type x20, other arithmetic: 15.9 us -> 23.7 us  [add(): return (total if zero is None else total + zero[0, 0]).astype(bf16)]
    unnamed x131 -> x151, local copies, waits for them, and re-layouts: 16.8 us -> 17.8 us
  transfers between devices with their start and end apart: 64 -> 64, of which waited for: 31 -> 29; matrix products, arithmetic and copies ran while one was open for 10% -> 13% of each run, Pallas kernels for 20% -> 20%
where the time goes in v3:
time: 429 us; the launch traced here: 422 us
  waiting for transfers between devices  131 us (31%)
  Pallas kernels  122 us (28%)
  starting transfers between devices  80.6 us (19%)
  local copies, waits for them, and re-layouts  40.9 us (10%)
  other arithmetic  33.4 us (8%)
  between operations  14.9 us (3%)
    pallas_call x19, Pallas kernels, call(): pl.pallas_call(run, out_shape=tuple(outs), in_specs=in_specs, out_specs=t...  122 us
    ppermute x56, waiting for transfers between devices, permute(): return lax.ppermute(value, axes, moves)  114 us
    ppermute x56, starting transfers between devices, permute(): return lax.ppermute(value, axes, moves)  61.2 us
    convert_element_type x20, other arithmetic, add(): return (total if zero is None else total + zero[0, 0]).astype(bf16)  23.7 us
    unnamed x151, local copies, waits for them, and re-layouts  17.8 us
    all_to_all x4, starting transfers between devices, everywhere(): return lax.all_to_all(copies, axes, 0, 0, tiled=True)  16.4 us
    all_to_all x4, waiting for transfers between devices, everywhere(): return lax.all_to_all(copies, axes, 0, 0, tiled=True)  13.5 us
  transfers between devices with their start and end apart: 64, of which 29 were waited for; matrix products, arithmetic and copies ran while one was open for 13% of the time, Pallas kernels for 20%

profile of v3, /device:TPU:0, one launch (start us, length us, event | category | flops | bytes accessed | tf_op | source)
XLA Modules:
  0.0 422.3 jit_solution(5347145012217596593)
XLA Ops:
  7.8 2.6 shard_map.363
  12.6 2.9 collective-permute-start.2
  17.0 2.3 dynamic-slice_bitcast_fusion.2
  21.7 6.2 %collective-permute-done.2.refs_2_.refs_6_ = bf16[256,1024]{1,0:T(8,128)(2,1)} collective-permute-done((bf16[256,1024]{1,0:T(8,128)(2,1)S(1)}, bf16[256,1024]{1,0:T(8,128)(2,1)}, u32[]{:S(2)}, u32[]{:S(2)}) %collective-permute-start.2) | collective-permute-done | bytes 524320 | tf_op jit(solution)/shard_map/ppermute | solution.py:815
  32.7 4.9 %all-to-all-start = ((f32[32,1,1088]{2,1,0:T(1,128)}), f32[32,1,1088]{2,1,0:T(1,128)S(1)}, u32[]{:S(2)}, u32[]{:S(2)}) async-start(f32[32,1,1088]{2,1,0:T(1,128)} %reshape.224), calls=%async_computation | async-start | bytes 294912 | tf_op jit(solution)/shard_map/all_to_all | solution.py:914
  39.1 5.3 %collective-permute-start.9 = (bf16[256,1024]{1,0:T(8,128)(2,1)}, bf16[256,1024]{1,0:T(8,128)(2,1)}, u32[]{:S(2)}, u32[]{:S(2)}) collective-permute-start(bf16[256,1024]{1,0:T(8,128)(2,1)} %collective-permute-done.4.refs_4_.refs_9_), channel_id=1, source_target_pairs={{0,1},{1,2},{2,3},{3,0},{4,5},{5,6},{6,7},{7,4},{8,9},{9,10},{10,1... | collective-permute-start | bytes 1572872 | tf_op jit(solution)/shard_map/ppermute | solution.py:815
  54.2 6.5 %shard_map.365 = (bf16[512,1024]{1,0:T(8,128)(2,1)}, bf16[1024,512]{1,0:T(8,128)(2,1)}, f32[4,512,128]{2,1,0:T(8,128)}, f32[16,8,512]{2,1,0:T(8,128)}, f32[16,512]{1,0:T(8,128)}) custom-call(s32[7]{0:T(128)} %stack.25.refs_0_, bf16[512,1024]{1,0:T(8,128)(2,1)} %broadcast_select_fusion.1.refs_1_.refs_0_, f32[1,1024]{1,0:T(1,128)} %slice.171.refs_2_, ...), custom_call_target="tpu_custom_call" | custom-call | flops 5750000128 | bytes 4526108 | tf_op jit(solution)/shard_map/pallas_call | solution.py:755
  60.7 5.4 %collective-permute-done.9.refs_13_ = bf16[256,1024]{1,0:T(8,128)(2,1)} collective-permute-done((bf16[256,1024]{1,0:T(8,128)(2,1)}, bf16[256,1024]{1,0:T(8,128)(2,1)}, u32[]{:S(2)}, u32[]{:S(2)}) %collective-permute-start.9) | collective-permute-done | bytes 524320 | tf_op jit(solution)/shard_map/ppermute | solution.py:815
  70.7 4.4 %all-to-all-start.1 = ((bf16[8,16,512]{2,1,0:T(8,128)(2,1)}), bf16[8,16,512]{2,1,0:T(8,128)(2,1)S(1)}, u32[]{:S(2)}, u32[]{:S(2)}) async-start(bf16[8,16,512]{2,1,0:T(8,128)(2,1)} %broadcast_in_dim.11), calls=%async_computation.1 | async-start | bytes 262144 | tf_op jit(solution)/shard_map/all_to_all | solution.py:914
  77.5 4.5 %collective-permute-done.10.refs_9_.refs_17_ = bf16[256,1024]{1,0:T(8,128)(2,1)} collective-permute-done((bf16[256,1024]{1,0:T(8,128)(2,1)}, bf16[256,1024]{1,0:T(8,128)(2,1)}, u32[]{:S(2)}, u32[]{:S(2)}) %collective-permute-start.10) | collective-permute-done | bytes 524320 | tf_op jit(solution)/shard_map/ppermute | solution.py:815
  84.6 8.6 %collective-permute-done.11.refs_10_.refs_6_.refs_3_ = bf16[2,256,512]{2,1,0:T(8,128)(2,1)S(1)} collective-permute-done((bf16[2,256,512]{2,1,0:T(8,128)(2,1)S(1)}, bf16[2,256,512]{2,1,0:T(8,128)(2,1)S(1)}, u32[]{:S(2)}, u32[]{:S(2)}) %collective-permute-start.11) | collective-permute-done | bytes 524320 | tf_op jit(solution)/shard_map/ppermute | solution.py:815
  94.8 6.2 %shard_map.367.refs_3_ = bf16[512,512]{1,0:T(8,128)(2,1)} custom-call(s32[7]{0:T(128)} %stack.25.refs_0_, f32[4,512,128]{2,1,0:T(8,128)} %get-tuple-element.115.refs_1_.refs_2_, f32[16,8,512]{2,1,0:T(8,128)} %get-tuple-element.116.refs_2_, bf16[8,16,512]{2,1,0:T(8,128)(2,1)} %copy-done.58, f32[16,512]{1,0:T(8,128)} %get-tuple-element.207.refs_3_.refs_4_.refs_0_.refs_5_, ...), custom_call_target="tpu_custom_call" | custom-call | flops 8049999872 | bytes 2031644 | tf_op jit(solution)/shard_map/pallas_call | solution.py:755
  101.1 4.1 collective-permute-done.18.refs_13_.refs_12_
  105.6 2.6 collective-permute-done.16.refs_11_.refs_8_.refs_15_
  109.3 7.0 %collective-permute-done.15.refs_10_.refs_7_.refs_14_ = bf16[2,256,512]{2,1,0:T(8,128)(2,1)S(1)} collective-permute-done((bf16[2,256,512]{2,1,0:T(8,128)(2,1)S(1)}, bf16[2,256,512]{2,1,0:T(8,128)(2,1)S(1)}, u32[]{:S(2)}, u32[]{:S(2)}) %collective-permute-start.15) | collective-permute-done | bytes 524320 | tf_op jit(solution)/shard_map/ppermute | solution.py:815
  116.8 2.8 collective-permute-done.21.refs_16_
  121.7 9.0 %collective-permute-done.14.refs_8_.refs_5_.refs_12_ = bf16[2,256,512]{2,1,0:T(8,128)(2,1)S(1)} collective-permute-done((bf16[2,256,512]{2,1,0:T(8,128)(2,1)}, bf16[2,256,512]{2,1,0:T(8,128)(2,1)S(1)}, u32[]{:S(2)}, u32[]{:S(2)}) %collective-permute-start.14) | collective-permute-done | bytes 524320 | tf_op jit(solution)/shard_map/ppermute | solution.py:815
  131.8 7.1 %shard_map.368 = (bf16[1024,512]{1,0:T(8,128)(2,1)}, bf16[1024,512]{1,0:T(8,128)(2,1)}, bf16[3,512,512]{2,1,0:T(8,128)(2,1)}) custom-call(s32[7]{0:T(128)} %stack.25.refs_0_, bf16[512,1024]{1,0:T(8,128)(2,1)} %get-tuple-element.114.refs_1_, bf16[512,1024]{1,0:T(8,128)(2,1)} %broadcast_select_fusion.refs_2_.refs_3_, bf16[512,512]{1,0:T(8,128)(2,1)} %shard_map.367.refs_3_, ...), custom_call_target="tpu_custom_call" | custom-call | flops 1150000000 | bytes 11010076 | tf_op jit(solution)/shard_map/pallas_call | solution.py:755
  141.8 6.3 %shard_map.369 = (bf16[512,1024]{1,0:T(8,128)(2,1)}, bf16[512,512]{1,0:T(8,128)(2,1)}, bf16[4,512,512]{2,1,0:T(8,128)(2,1)}, bf16[4,512,512]{2,1,0:T(8,128)(2,1)}) custom-call(s32[7]{0:T(128)} %stack.25.refs_0_, bf16[3,512,512]{2,1,0:T(8,128)(2,1)} %get-tuple-element.119.refs_1_.refs_6_, bf16[2,256,512]{2,1,0:T(8,128)(2,1)} %copy-done.1, ...), custom_call_target="tpu_custom_call" | custom-call | flops 1150000000 | bytes 11534364 | tf_op jit(solution)/shard_map/pallas_call | solution.py:755
  152.1 4.3 %shard_map.370 = (f32[512,1024]{1,0:T(8,128)}, bf16[512,1024]{1,0:T(8,128)(2,1)}, bf16[1024,512]{1,0:T(8,128)(2,1)}) custom-call(bf16[512,1024]{1,0:T(8,128)(2,1)} %broadcast_select_fusion.1.refs_1_.refs_0_, f32[1,1024]{1,0:T(1,128)} %slice.169.refs_1_.refs_2_, bf16[512,1024]{1,0:T(8,128)(2,1)} %get-tuple-element.120.refs_2_, bf16[512,1024]{1,0:T(8,128)(2,1)} %copy-done.66), custom_call_target="tpu_custom_call" | custom-call | flops 1150000000 | bytes 7344128 | tf_op jit(solution)/shard_map/pallas_call | solution.py:755
  156.4 6.3 %collective-permute-done.25.refs_20_ = bf16[256,1024]{1,0:T(8,128)(2,1)S(1)} collective-permute-done((bf16[256,1024]{1,0:T(8,128)(2,1)}, bf16[256,1024]{1,0:T(8,128)(2,1)S(1)}, u32[]{:S(2)}, u32[]{:S(2)}) %collective-permute-start.25) | collective-permute-done | bytes 524320 | tf_op jit(solution)/shard_map/ppermute | solution.py:815
  163.5 22.1 %shard_map.371 = (bf16[256,1024]{1,0:T(8,128)(2,1)}, bf16[256,1024]{1,0:T(8,128)(2,1)}, bf16[512,1024]{1,0:T(8,128)(2,1)}, bf16[2,2,256,512]{3,2,1,0:T(8,128)(2,...) custom-call(s32[7]{0:T(128)} %stack.25.refs_0_, ...), custom_call_target="tpu_custom_call" | custom-call | flops 20700000256 | bytes 23068700 | tf_op jit(solution)/shard_map/pallas_call | solution.py:755
  185.7 2.2 collective-permute-done.26
  194.0 15.1 %shard_map.373 = (f32[256,1024]{1,0:T(8,128)}, f32[1,1024]{1,0:T(1,128)}, bf16[512,1024]{1,0:T(8,128)(2,1)}, bf16[512,1024]{1,0:T(8,128)(2,1)}, bf16[512,512]{1,...) custom-call(s32[7]{0:T(128)} %stack.25.refs_0_, ...), custom_call_target="tpu_custom_call" | custom-call | flops 1150000000 | bytes 20979740 | tf_op jit(solution)/shard_map/pallas_call | solution.py:755
  209.3 7.0 %shard_map.374 = (bf16[2,2,256,512]{3,2,1,0:T(8,128)(2,1)}, bf16[2,2,256,512]{3,2,1,0:T(8,128)(2,1)}, bf16[2,2,256,512]{3,2,1,0:T(8,128)(2,1)}, bf16[2,2,256,512]{3,2,1,0:T(8,128)(2,1)}) custom-call(s32[7]{0:T(128)} %stack.25.refs_0_, bf16[512,1024]{1,0:T(8,128)(2,1)} %get-tuple-element.135.refs_1_, bf16[512,512]{1,0:T(8,128)(2,1)} %get-tuple-element.136.refs_2_, ...), custom_call_target="tpu_custom_call" | custom-call | flops 1150000000 | bytes 9437212 | tf_op jit(solution)/shard_map/pallas_call | solution.py:755
  217.8 6.4 %shard_map.375 = (f32[4,512,128]{2,1,0:T(8,128)}, f32[2,16,8,512]{3,2,1,0:T(8,128)}, f32[2,16,512]{2,1,0:T(8,128)}, f32[8,128]{1,0:T(8,128)}) custom-call(f32[16,512]{1,0:T(8,128)} %get-tuple-element.207.refs_3_.refs_4_.refs_0_.refs_5_, bf16[512,512]{1,0:T(8,128)(2,1)} %get-tuple-element.131.refs_1_, bf16[512,512]{1,0:T(8,128)(2,1)} %copy-done.69, ...), custom_call_target="tpu_custom_call" | custom-call | flops 1150000000 | bytes 2719744 | tf_op jit(solution)/shard_map/pallas_call | solution.py:755
  225.8 3.4 all-to-all-start.2
  230.8 2.6 add_convert_fusion.8.refs_1_
  233.4 5.0 %all-to-all-done.2.refs_2_.refs_4_ = bf16[8,2,16,512]{3,2,1,0:T(8,128)(2,1)S(1)} async-done(((bf16[8,2,16,512]{3,2,1,0:T(8,128)(2,1)}), bf16[8,2,16,512]{3,2,1,0:T(8,128)(2,1)S(1)}, u32[]{:S(2)}, u32[]{:S(2)}) %all-to-all-start.2) | async-done | bytes 262176 | tf_op jit(solution)/shard_map/all_to_all | solution.py:914
  241.9 12.8 %shard_map.378 = (bf16[256,1024]{1,0:T(8,128)(2,1)}, bf16[256,1024]{1,0:T(8,128)(2,1)}, f32[2,16,512]{2,1,0:T(8,128)}) custom-call(s32[7]{0:T(128)} %stack.25.refs_0_, f32[4,512,128]{2,1,0:T(8,128)} %get-tuple-element.143.refs_1_, f32[4,512,128]{2,1,0:T(8,128)} %get-tuple-element.115.refs_1_.refs_2_, f32[2,16,8,512]{3,2,1,0:T(8,128)} %get-tuple-element.144.refs_3_, ...), custom_call_target="tpu_custom_call" | custom-call | flops 1150000000 | bytes 5111836 | tf_op jit(solution)/shard_map/pallas_call | solution.py:755
  258.5 17.1 %collective-permute-done.33 = bf16[1,2,256,512]{3,2,1,0:T(8,128)(2,1)S(1)} collective-permute-done((bf16[1,2,256,512]{3,2,1,0:T(8,128)(2,1)S(1)}, bf16[1,2,256,512]{3,2,1,0:T(8,128)(2,1)S(1)}, u32[]{:S(2)}, u32[]{:S(2)}) %collective-permute-start.33) | collective-permute-done | bytes 524320 | tf_op jit(solution)/shard_map/ppermute | solution.py:815
  278.0 3.5 shard_map.379
  286.2 2.5 add_convert_fusion.5
  295.4 24.1 %collective-permute-done.39 = bf16[1,2,256,512]{3,2,1,0:T(8,128)(2,1)S(1)} collective-permute-done((bf16[1,2,256,512]{3,2,1,0:T(8,128)(2,1)S(1)}, bf16[1,2,256,512]{3,2,1,0:T(8,128)(2,1)S(1)}, u32[]{:S(2)}, u32[]{:S(2)}) %collective-permute-start.39) | collective-permute-done | bytes 524320 | tf_op jit(solution)/shard_map/ppermute | solution.py:815
  333.5 3.3 shard_map.372.refs_9_
  338.1 3.9 collective-permute-start.47
  343.8 3.9 collective-permute-start.43
  350.6 3.3 collective-permute-start.48
  355.7 3.9 collective-permute-start.44
  364.4 2.6 all-to-all-start.3
  368.0 3.7 collective-permute-start.53
  373.5 2.3 all-to-all-done.3
  383.9 5.0 %shard_map.384 = (f32[128,1024]{1,0:T(8,128)}, f32[128,1024]{1,0:T(8,128)}, f32[128,1024]{1,0:T(8,128)}, f32[1024,128]{1,0:T(8,128)}, f32[1024,128]{1,0:T(8,128)...) custom-call(s32[7]{0:T(128)} %stack.25.refs_0_, bf16[256,512]{1,0:T(8,128)(2,1)} %copy-done.48, bf16[128,512]{1,0:T(8,128)(2,1)} %copy-done.71, ...), custom_call_target="tpu_custom_call" | custom-call | flops 4600000000 | bytes 7078940 | tf_op jit(solution)/shard_map/pallas_call | solution.py:755
  391.4 4.2 shard_map.380.refs_10_
  396.3 3.2 shard_map.385
  400.8 3.6 all-to-all-start.4
  404.9 6.8 %all-to-all-done.4.refs_0_ = f32[32,2,128]{2,1,0:T(2,128)S(1)} async-done(((f32[32,2,128]{2,1,0:T(2,128)}), f32[32,2,128]{2,1,0:T(2,128)S(1)}, u32[]{:S(2)}, u32[]{:S(2)}) %all-to-all-start.4) | async-done | bytes 32800 | tf_op jit(solution)/shard_map/all_to_all | solution.py:914
  412.3 3.2 shard_map.388
  (326 shorter events, 121.3 us)
Async XLA Ops:
  7.2 60.0 %all-gather.6.cloned.1.call-start = ((), (), s32[]{:S(2)}) async-start(), calls=%async_computation.5 | async-start | bytes 1310720 | tf_op jit(solution)/shard_map/all_gather | solution.py:936
  11.9 32.5 %collective-permute-start = (bf16[512,1024]{1,0:T(8,128)(2,1)}, bf16[512,1024]{1,0:T(8,128)(2,1)}, u32[]{:S(2)}, u32[]{:S(2)}) collective-permute-start(bf16[512,1024]{1,0:T(8,128)(2,1)} %dynamic-slice_bitcast_fusion.3), channel_id=1, source_target_pairs={{0,4},{4,0},{1,5},{5,1},{2,6},{6,2},{3,7},{7,3},{8,12},{12,8},{9,1... | collective-permute-start | bytes 3145736 | tf_op jit(solution)/shard_map/ppermute | solution.py:815
  12.6 15.3 %collective-permute-start.2 = (bf16[256,1024]{1,0:T(8,128)(2,1)S(1)}, bf16[256,1024]{1,0:T(8,128)(2,1)}, u32[]{:S(2)}, u32[]{:S(2)}) collective-permute-start(bf16[256,1024]{1,0:T(8,128)(2,1)S(1)} %maximum_select_fusion.refs_5_), channel_id=1, source_target_pairs={{0,8},{8,0},{16,24},{24,16},{1,9},{9,1},{17,25},{25,17},{2,10},{10... | collective-permute-start | bytes 1572872 | tf_op jit(solution)/shard_map/ppermute | solution.py:815
  15.5 13.8 %collective-permute-start.3 = (bf16[256,1024]{1,0:T(8,128)(2,1)S(1)}, bf16[256,1024]{1,0:T(8,128)(2,1)}, u32[]{:S(2)}, u32[]{:S(2)}) collective-permute-start(bf16[256,1024]{1,0:T(8,128)(2,1)S(1)} %maximum_select_fusion.refs_5_), channel_id=1, source_target_pairs={{0,16},{8,24},{16,0},{24,8},{1,17},{9,25},{17,1},{25,9},{2,18},{10... | collective-permute-start | bytes 1572872 | tf_op jit(solution)/shard_map/ppermute | solution.py:815
  19.3 34.9 %collective-permute-start.5 = (bf16[512,1024]{1,0:T(8,128)(2,1)}, bf16[512,1024]{1,0:T(8,128)(2,1)}, u32[]{:S(2)}, u32[]{:S(2)}) collective-permute-start(bf16[512,1024]{1,0:T(8,128)(2,1)} %dynamic-slice_bitcast_fusion.2), channel_id=1, source_target_pairs={{0,4},{4,0},{1,5},{5,1},{2,6},{6,2},{3,7},{7,3},{8,12},{12,8},{9,1... | collective-permute-start | bytes 3145736 | tf_op jit(solution)/shard_map/ppermute | solution.py:815
  19.3 19.8 %collective-permute-start.4 = (bf16[256,1024]{1,0:T(8,128)(2,1)S(1)}, bf16[256,1024]{1,0:T(8,128)(2,1)}, u32[]{:S(2)}, u32[]{:S(2)}) collective-permute-start(bf16[256,1024]{1,0:T(8,128)(2,1)S(1)} %maximum_select_fusion.refs_5_), channel_id=1, source_target_pairs={{0,1},{1,2},{2,3},{3,0},{4,5},{5,6},{6,7},{7,4},{8,9},{9,10},{10,1... | collective-permute-start | bytes 1572872 | tf_op jit(solution)/shard_map/ppermute | solution.py:815
  32.7 16.7 %all-to-all-start = ((f32[32,1,1088]{2,1,0:T(1,128)}), f32[32,1,1088]{2,1,0:T(1,128)S(1)}, u32[]{:S(2)}, u32[]{:S(2)}) async-start(f32[32,1,1088]{2,1,0:T(1,128)} %reshape.224), calls=%async_computation | async-start | bytes 294912 | tf_op jit(solution)/shard_map/all_to_all | solution.py:914
  39.1 27.0 %collective-permute-start.9 = (bf16[256,1024]{1,0:T(8,128)(2,1)}, bf16[256,1024]{1,0:T(8,128)(2,1)}, u32[]{:S(2)}, u32[]{:S(2)}) collective-permute-start(bf16[256,1024]{1,0:T(8,128)(2,1)} %collective-permute-done.4.refs_4_.refs_9_), channel_id=1, source_target_pairs={{0,1},{1,2},{2,3},{3,0},{4,5},{5,6},{6,7},{7,4},{8,9},{9,10},{10,1... | collective-permute-start | bytes 1572872 | tf_op jit(solution)/shard_map/ppermute | solution.py:815
  44.4 24.1 %collective-permute-start.8 = (bf16[256,1024]{1,0:T(8,128)(2,1)}, bf16[256,1024]{1,0:T(8,128)(2,1)S(1)}, u32[]{:S(2)}, u32[]{:S(2)}) collective-permute-start(bf16[256,1024]{1,0:T(8,128)(2,1)} %collective-permute-done.4.refs_4_.refs_9_), channel_id=1, source_target_pairs={{0,16},{8,24},{16,0},{24,8},{1,17},{9,25},{17,1},{25,9},{2,18},{10... | collective-permute-start | bytes 1572872 | tf_op jit(solution)/shard_map/ppermute | solution.py:815
  44.4 25.2 %collective-permute-start.7 = (bf16[256,1024]{1,0:T(8,128)(2,1)}, bf16[256,1024]{1,0:T(8,128)(2,1)}, u32[]{:S(2)}, u32[]{:S(2)}) collective-permute-start(bf16[256,1024]{1,0:T(8,128)(2,1)} %collective-permute-done.4.refs_4_.refs_9_), channel_id=1, source_target_pairs={{0,8},{8,0},{16,24},{24,16},{1,9},{9,1},{17,25},{25,17},{2,10},{10... | collective-permute-start | bytes 1572872 | tf_op jit(solution)/shard_map/ppermute | solution.py:815
  44.4 31.0 %collective-permute-start.6 = (bf16[256,1024]{1,0:T(8,128)(2,1)}, bf16[256,1024]{1,0:T(8,128)(2,1)}, u32[]{:S(2)}, u32[]{:S(2)}) collective-permute-start(bf16[256,1024]{1,0:T(8,128)(2,1)} %collective-permute-done.2.refs_2_.refs_6_), channel_id=1, source_target_pairs={{0,16},{8,24},{16,0},{24,8},{1,17},{9,25},{17,1},{25,9},{2,18},{10... | collective-permute-start | bytes 1572872 | tf_op jit(solution)/shard_map/ppermute | solution.py:815
  66.1 15.9 %collective-permute-start.10 = (bf16[256,1024]{1,0:T(8,128)(2,1)}, bf16[256,1024]{1,0:T(8,128)(2,1)}, u32[]{:S(2)}, u32[]{:S(2)}) collective-permute-start(bf16[256,1024]{1,0:T(8,128)(2,1)} %collective-permute-done.9.refs_13_), channel_id=1, source_target_pairs={{0,1},{1,2},{2,3},{3,0},{4,5},{5,6},{6,7},{7,4},{8,9},{9,10},{10,1... | collective-permute-start | bytes 1572872 | tf_op jit(solution)/shard_map/ppermute | solution.py:815
  66.1 17.1 %collective-permute-start.19 = (bf16[256,1024]{1,0:T(8,128)(2,1)}, bf16[256,1024]{1,0:T(8,128)(2,1)S(1)}, u32[]{:S(2)}, u32[]{:S(2)}) collective-permute-start(bf16[256,1024]{1,0:T(8,128)(2,1)} %collective-permute-done.9.refs_13_), channel_id=1, source_target_pairs={{0,8},{8,0},{16,24},{24,16},{1,9},{9,1},{17,25},{25,17},{2,10},{10... | collective-permute-start | bytes 1572872 | tf_op jit(solution)/shard_map/ppermute | solution.py:815
  68.5 24.7 %collective-permute-start.11 = (bf16[2,256,512]{2,1,0:T(8,128)(2,1)S(1)}, bf16[2,256,512]{2,1,0:T(8,128)(2,1)S(1)}, u32[]{:S(2)}, u32[]{:S(2)}) collective-permute-start(bf16[2,256,512]{2,1,0:T(8,128)(2,1)S(1)} %get-tuple-element.205.refs_5_.refs_2_.refs_9_), channel_id=1, source_target_pairs={{0,8},{8,0},{16,24},{24,16},{1,9},{9,1},{17,25},{25,17},{2,10},{10... | collective-permute-start | bytes 1572872 | tf_op jit(solution)/shard_map/ppermute | solution.py:815
  69.6 24.1 %collective-permute-start.12 = (bf16[2,256,512]{2,1,0:T(8,128)(2,1)S(1)}, bf16[2,256,512]{2,1,0:T(8,128)(2,1)S(1)}, u32[]{:S(2)}, u32[]{:S(2)}) collective-permute-start(bf16[2,256,512]{2,1,0:T(8,128)(2,1)S(1)} %get-tuple-element.205.refs_5_.refs_2_.refs_9_), channel_id=1, source_target_pairs={{0,16},{8,24},{16,0},{24,8},{1,17},{9,25},{17,1},{25,9},{2,18},{10... | collective-permute-start | bytes 1572872 | tf_op jit(solution)/shard_map/ppermute | solution.py:815
  70.7 23.4 %all-to-all-start.1 = ((bf16[8,16,512]{2,1,0:T(8,128)(2,1)}), bf16[8,16,512]{2,1,0:T(8,128)(2,1)S(1)}, u32[]{:S(2)}, u32[]{:S(2)}) async-start(bf16[8,16,512]{2,1,0:T(8,128)(2,1)} %broadcast_in_dim.11), calls=%async_computation.1 | async-start | bytes 262144 | tf_op jit(solution)/shard_map/all_to_all | solution.py:914
  75.2 202.0 %all-gather.8.cloned.1.call-start = ((), (), s32[]{:S(2)}) async-start(), calls=%async_computation.6 | async-start | bytes 2621440 | tf_op jit(solution)/shard_map/all_gather | solution.py:1080
  75.5 25.6 %collective-permute-start.20 = (bf16[256,1024]{1,0:T(8,128)(2,1)}, bf16[256,1024]{1,0:T(8,128)(2,1)}, u32[]{:S(2)}, u32[]{:S(2)}) collective-permute-start(bf16[256,1024]{1,0:T(8,128)(2,1)} %collective-permute-done.9.refs_13_), channel_id=1, source_target_pairs={{0,16},{8,24},{16,0},{24,8},{1,17},{9,25},{17,1},{25,9},{2,18},{10... | collective-permute-start | bytes 1572872 | tf_op jit(solution)/shard_map/ppermute | solution.py:815
  82.0 23.2 %collective-permute-start.18 = (bf16[256,1024]{1,0:T(8,128)(2,1)}, bf16[256,1024]{1,0:T(8,128)(2,1)}, u32[]{:S(2)}, u32[]{:S(2)}) collective-permute-start(bf16[256,1024]{1,0:T(8,128)(2,1)} %copy-done.67), channel_id=1, source_target_pairs={{0,8},{8,0},{16,24},{24,16},{1,9},{9,1},{17,25},{25,17},{2,10},{10... | collective-permute-start | bytes 1572872 | tf_op jit(solution)/shard_map/ppermute | solution.py:815
  84.1 24.2 %collective-permute-start.16 = (bf16[2,256,512]{2,1,0:T(8,128)(2,1)S(1)}, bf16[2,256,512]{2,1,0:T(8,128)(2,1)S(1)}, u32[]{:S(2)}, u32[]{:S(2)}) collective-permute-start(bf16[2,256,512]{2,1,0:T(8,128)(2,1)S(1)} %get-tuple-element.204.refs_9_.refs_6_.refs_13_), channel_id=1, source_target_pairs={{0,16},{8,24},{16,0},{24,8},{1,17},{9,25},{17,1},{25,9},{2,18},{10... | collective-permute-start | bytes 1572872 | tf_op jit(solution)/shard_map/ppermute | solution.py:815
  93.2 23.2 %collective-permute-start.15 = (bf16[2,256,512]{2,1,0:T(8,128)(2,1)S(1)}, bf16[2,256,512]{2,1,0:T(8,128)(2,1)S(1)}, u32[]{:S(2)}, u32[]{:S(2)}) collective-permute-start(bf16[2,256,512]{2,1,0:T(8,128)(2,1)S(1)} %get-tuple-element.204.refs_9_.refs_6_.refs_13_), channel_id=1, source_target_pairs={{0,8},{8,0},{16,24},{24,16},{1,9},{9,1},{17,25},{25,17},{2,10},{10... | collective-permute-start | bytes 1572872 | tf_op jit(solution)/shard_map/ppermute | solution.py:815
  93.6 26.0 %collective-permute-start.21 = (bf16[256,1024]{1,0:T(8,128)(2,1)}, bf16[256,1024]{1,0:T(8,128)(2,1)}, u32[]{:S(2)}, u32[]{:S(2)}) collective-permute-start(bf16[256,1024]{1,0:T(8,128)(2,1)} %copy-done.50), channel_id=1, source_target_pairs={{0,16},{8,24},{16,0},{24,8},{1,17},{9,25},{17,1},{25,9},{2,18},{10... | collective-permute-start | bytes 1572872 | tf_op jit(solution)/shard_map/ppermute | solution.py:815
  101.0 20.7 %collective-permute-start.13 = (bf16[512,512]{1,0:T(8,128)(2,1)}, bf16[512,512]{1,0:T(8,128)(2,1)S(1)}, u32[]{:S(2)}, u32[]{:S(2)}) collective-permute-start(bf16[512,512]{1,0:T(8,128)(2,1)} %shard_map.367.refs_3_), channel_id=1, source_target_pairs={{0,4},{4,0},{1,5},{5,1},{2,6},{6,2},{3,7},{7,3},{8,12},{12,8},{9,1... | collective-permute-start | bytes 1572872 | tf_op jit(solution)/shard_map/ppermute | solution.py:815
  105.2 25.5 %collective-permute-start.14 = (bf16[2,256,512]{2,1,0:T(8,128)(2,1)}, bf16[2,256,512]{2,1,0:T(8,128)(2,1)S(1)}, u32[]{:S(2)}, u32[]{:S(2)}) collective-permute-start(bf16[2,256,512]{2,1,0:T(8,128)(2,1)} %copy-done.15), channel_id=1, source_target_pairs={{0,16},{8,24},{16,0},{24,8},{1,17},{9,25},{17,1},{25,9},{2,18},{10... | collective-permute-start | bytes 1572872 | tf_op jit(solution)/shard_map/ppermute | solution.py:815
  108.3 22.5 %collective-permute-start.17 = (bf16[2,256,512]{2,1,0:T(8,128)(2,1)S(1)}, bf16[2,256,512]{2,1,0:T(8,128)(2,1)S(1)}, u32[]{:S(2)}, u32[]{:S(2)}) collective-permute-start(bf16[2,256,512]{2,1,0:T(8,128)(2,1)S(1)} %collective-permute-done.16.refs_11_.refs_8_.refs_15_), channel_id=1, source_target_pairs={{0,8},{8,0},{16,24},{24,16},{1,9},{9,1},{17,25},{25,17},{2,10},{10... | collective-permute-start | bytes 1572872 | tf_op jit(solution)/shard_map/ppermute | solution.py:815
  116.3 24.5 %collective-permute-start.23 = (bf16[256,1024]{1,0:T(8,128)(2,1)}, bf16[256,1024]{1,0:T(8,128)(2,1)S(1)}, u32[]{:S(2)}, u32[]{:S(2)}) collective-permute-start(bf16[256,1024]{1,0:T(8,128)(2,1)} %collective-permute-done.10.refs_9_.refs_17_), channel_id=1, source_target_pairs={{0,16},{8,24},{16,0},{24,8},{1,17},{9,25},{17,1},{25,9},{2,18},{10... | collective-permute-start | bytes 1572872 | tf_op jit(solution)/shard_map/ppermute | solution.py:815
  119.6 21.2 %collective-permute-start.22 = (bf16[256,1024]{1,0:T(8,128)(2,1)}, bf16[256,1024]{1,0:T(8,128)(2,1)S(1)}, u32[]{:S(2)}, u32[]{:S(2)}) collective-permute-start(bf16[256,1024]{1,0:T(8,128)(2,1)} %collective-permute-done.10.refs_9_.refs_17_), channel_id=1, source_target_pairs={{0,8},{8,0},{16,24},{24,16},{1,9},{9,1},{17,25},{25,17},{2,10},{10... | collective-permute-start | bytes 1572872 | tf_op jit(solution)/shard_map/ppermute | solution.py:815
  148.1 14.6 %collective-permute-start.25 = (bf16[256,1024]{1,0:T(8,128)(2,1)}, bf16[256,1024]{1,0:T(8,128)(2,1)S(1)}, u32[]{:S(2)}, u32[]{:S(2)}) collective-permute-start(bf16[256,1024]{1,0:T(8,128)(2,1)} %copy-done.53), channel_id=1, source_target_pairs={{0,8},{8,0},{16,24},{24,16},{1,9},{9,1},{17,25},{25,17},{2,10},{10... | collective-permute-start | bytes 1572872 | tf_op jit(solution)/shard_map/ppermute | solution.py:815
  190.4 25.9 %collective-permute-start.30 = (bf16[2,2,256,512]{3,2,1,0:T(8,128)(2,1)}, bf16[2,2,256,512]{3,2,1,0:T(8,128)(2,1)S(1)}, u32[]{:S(2)}, u32[]{:S(2)}) collective-permute-start(bf16[2,2,256,512]{3,2,1,0:T(8,128)(2,1)} %get-tuple-element.133), channel_id=1, source_target_pairs={{0,16},{8,24},{16,0},{24,8},{1,17},{9,25},{17,1},{25,9},{2,18},{10... | collective-permute-start | bytes 3145736 | tf_op jit(solution)/shard_map/ppermute | solution.py:815
  190.9 25.4 %collective-permute-start.31 = (bf16[2,2,256,512]{3,2,1,0:T(8,128)(2,1)}, bf16[2,2,256,512]{3,2,1,0:T(8,128)(2,1)S(1)}, u32[]{:S(2)}, u32[]{:S(2)}) collective-permute-start(bf16[2,2,256,512]{3,2,1,0:T(8,128)(2,1)} %get-tuple-element.134), channel_id=1, source_target_pairs={{0,8},{8,0},{16,24},{24,16},{1,9},{9,1},{17,25},{25,17},{2,10},{10... | collective-permute-start | bytes 3145736 | tf_op jit(solution)/shard_map/ppermute | solution.py:815
  225.8 12.6 %all-to-all-start.2 = ((bf16[8,2,16,512]{3,2,1,0:T(8,128)(2,1)}), bf16[8,2,16,512]{3,2,1,0:T(8,128)(2,1)S(1)}, u32[]{:S(2)}, u32[]{:S(2)}) async-start(bf16[8,2,16,512]{3,2,1,0:T(8,128)(2,1)} %broadcast_in_dim.12), calls=%async_computation.2 | async-start | bytes 524288 | tf_op jit(solution)/shard_map/all_to_all | solution.py:914
  229.3 148.9 %all-gather.10.cloned.1.call-start = ((), (), s32[]{:S(2)}) async-start(), calls=%async_computation.7 | async-start | bytes 2621440 | tf_op jit(solution)/shard_map/all_gather | solution.py:1183
  239.1 47.1 %collective-permute-start.38 = (bf16[2,2,256,512]{3,2,1,0:T(8,128)(2,1)}, bf16[2,2,256,512]{3,2,1,0:T(8,128)(2,1)}, u32[]{:S(2)}, u32[]{:S(2)}) collective-permute-start(bf16[2,2,256,512]{3,2,1,0:T(8,128)(2,1)} %get-tuple-element.155.refs_11_), channel_id=1, source_target_pairs={{0,8},{8,0},{16,24},{24,16},{1,9},{9,1},{17,25},{25,17},{2,10},{10... | collective-permute-start | bytes 3145736 | tf_op jit(solution)/shard_map/ppermute | solution.py:815
  240.8 49.4 %collective-permute-start.36 = (bf16[2,2,256,512]{3,2,1,0:T(8,128)(2,1)}, bf16[2,2,256,512]{3,2,1,0:T(8,128)(2,1)}, u32[]{:S(2)}, u32[]{:S(2)}) collective-permute-start(bf16[2,2,256,512]{3,2,1,0:T(8,128)(2,1)} %get-tuple-element.154.refs_10_), channel_id=1, source_target_pairs={{0,16},{8,24},{16,0},{24,8},{1,17},{9,25},{17,1},{25,9},{2,18},{10... | collective-permute-start | bytes 3145736 | tf_op jit(solution)/shard_map/ppermute | solution.py:815
  254.6 20.9 %collective-permute-start.33 = (bf16[1,2,256,512]{3,2,1,0:T(8,128)(2,1)S(1)}, bf16[1,2,256,512]{3,2,1,0:T(8,128)(2,1)S(1)}, u32[]{:S(2)}, u32[]{:S(2)}) collective-permute-start(bf16[1,2,256,512]{3,2,1,0:T(8,128)(2,1)S(1)} %copy-done.3), channel_id=1, source_target_pairs={{0,8},{8,0},{16,24},{24,16},{1,9},{9,1},{17,25},{25,17},{2,10},{10... | collective-permute-start | bytes 1572872 | tf_op jit(solution)/shard_map/ppermute | solution.py:815
  256.2 21.0 %collective-permute-start.34 = (bf16[1,2,256,512]{3,2,1,0:T(8,128)(2,1)S(1)}, bf16[1,2,256,512]{3,2,1,0:T(8,128)(2,1)S(1)}, u32[]{:S(2)}, u32[]{:S(2)}) collective-permute-start(bf16[1,2,256,512]{3,2,1,0:T(8,128)(2,1)S(1)} %copy-done.2), channel_id=1, source_target_pairs={{0,16},{8,24},{16,0},{24,8},{1,17},{9,25},{17,1},{25,9},{2,18},{10... | collective-permute-start | bytes 1572872 | tf_op jit(solution)/shard_map/ppermute | solution.py:815
  281.5 42.2 %collective-permute-start.41 = (bf16[2,2,256,512]{3,2,1,0:T(8,128)(2,1)}, bf16[2,2,256,512]{3,2,1,0:T(8,128)(2,1)S(1)}, u32[]{:S(2)}, u32[]{:S(2)}) collective-permute-start(bf16[2,2,256,512]{3,2,1,0:T(8,128)(2,1)} %get-tuple-element.166), channel_id=1, source_target_pairs={{0,8},{8,0},{16,24},{24,16},{1,9},{9,1},{17,25},{25,17},{2,10},{10... | collective-permute-start | bytes 3145736 | tf_op jit(solution)/shard_map/ppermute | solution.py:815
  284.5 40.7 %collective-permute-start.40 = (bf16[2,2,256,512]{3,2,1,0:T(8,128)(2,1)}, bf16[2,2,256,512]{3,2,1,0:T(8,128)(2,1)S(1)}, u32[]{:S(2)}, u32[]{:S(2)}) collective-permute-start(bf16[2,2,256,512]{3,2,1,0:T(8,128)(2,1)} %get-tuple-element.164), channel_id=1, source_target_pairs={{0,16},{8,24},{16,0},{24,8},{1,17},{9,25},{17,1},{25,9},{2,18},{10... | collective-permute-start | bytes 3145736 | tf_op jit(solution)/shard_map/ppermute | solution.py:815
  286.1 47.4 %collective-permute-start.27 = (bf16[2,256,1024]{2,1,0:T(8,128)(2,1)}, bf16[2,256,1024]{2,1,0:T(8,128)(2,1)}, u32[]{:S(2)}, u32[]{:S(2)}) collective-permute-start(bf16[2,256,1024]{2,1,0:T(8,128)(2,1)} %dynamic-slice_bitcast_fusion.1), channel_id=1, source_target_pairs={{0,4},{4,0},{1,5},{5,1},{2,6},{6,2},{3,7},{7,3},{8,12},{12,8},{9,1... | collective-permute-start | bytes 3145736 | tf_op jit(solution)/shard_map/ppermute | solution.py:815
  288.7 30.8 %collective-permute-start.39 = (bf16[1,2,256,512]{3,2,1,0:T(8,128)(2,1)S(1)}, bf16[1,2,256,512]{3,2,1,0:T(8,128)(2,1)S(1)}, u32[]{:S(2)}, u32[]{:S(2)}) collective-permute-start(bf16[1,2,256,512]{3,2,1,0:T(8,128)(2,1)S(1)} %add_convert_fusion.5), channel_id=1, source_target_pairs={{0,16},{8,24},{16,0},{24,8},{1,17},{9,25},{17,1},{25,9},{2,18},{10... | collective-permute-start | bytes 1572872 | tf_op jit(solution)/shard_map/ppermute | solution.py:815
  292.0 29.6 %collective-permute-start.37 = (bf16[1,2,256,512]{3,2,1,0:T(8,128)(2,1)S(1)}, bf16[1,2,256,512]{3,2,1,0:T(8,128)(2,1)S(1)}, u32[]{:S(2)}, u32[]{:S(2)}) collective-permute-start(bf16[1,2,256,512]{3,2,1,0:T(8,128)(2,1)S(1)} %add_convert_fusion.7), channel_id=1, source_target_pairs={{0,8},{8,0},{16,24},{24,16},{1,9},{9,1},{17,25},{25,17},{2,10},{10... | collective-permute-start | bytes 1572872 | tf_op jit(solution)/shard_map/ppermute | solution.py:815
  324.5 23.1 %collective-permute-start.51 = (bf16[1,2,256,512]{3,2,1,0:T(8,128)(2,1)S(1)}, bf16[1,2,256,512]{3,2,1,0:T(8,128)(2,1)}, u32[]{:S(2)}, u32[]{:S(2)}) collective-permute-start(bf16[1,2,256,512]{3,2,1,0:T(8,128)(2,1)S(1)} %add_convert_fusion.2.refs_3_), channel_id=1, source_target_pairs={{0,16},{8,24},{16,0},{24,8},{1,17},{9,25},{17,1},{25,9},{2,18},{10... | collective-permute-start | bytes 1572872 | tf_op jit(solution)/shard_map/ppermute | solution.py:815
  327.0 32.6 %collective-permute-start.50 = (bf16[1,2,256,512]{3,2,1,0:T(8,128)(2,1)S(1)}, bf16[1,2,256,512]{3,2,1,0:T(8,128)(2,1)}, u32[]{:S(2)}, u32[]{:S(2)}) collective-permute-start(bf16[1,2,256,512]{3,2,1,0:T(8,128)(2,1)S(1)} %add_convert_fusion.3.refs_2_), channel_id=1, source_target_pairs={{0,8},{8,0},{16,24},{24,16},{1,9},{9,1},{17,25},{25,17},{2,10},{10... | collective-permute-start | bytes 1572872 | tf_op jit(solution)/shard_map/ppermute | solution.py:815
  331.9 11.8 %collective-permute-start.42 = (bf16[256,512]{1,0:T(8,128)(2,1)S(1)}, bf16[256,512]{1,0:T(8,128)(2,1)S(1)}, u32[]{:S(2)}, u32[]{:S(2)}) collective-permute-start(bf16[256,512]{1,0:T(8,128)(2,1)S(1)} %slice_bitcast_fusion.5), channel_id=1, source_target_pairs={{0,3},{1,0},{2,1},{3,2},{4,7},{5,4},{6,5},{7,6},{8,11},{9,8},{10,9... | collective-permute-start | bytes 786440 | tf_op jit(solution)/shard_map/ppermute | solution.py:815
  349.7 17.3 %collective-permute-start.52 = (bf16[256,512]{1,0:T(8,128)(2,1)}, bf16[256,512]{1,0:T(8,128)(2,1)}, u32[]{:S(2)}, u32[]{:S(2)}) collective-permute-start(bf16[256,512]{1,0:T(8,128)(2,1)} %slice_bitcast_fusion), channel_id=1, source_target_pairs={{0,3},{1,0},{2,1},{3,2},{4,7},{5,4},{6,5},{7,6},{8,11},{9,8},{10,9... | collective-permute-start | bytes 786440 | tf_op jit(solution)/shard_map/ppermute | solution.py:815
  350.6 21.1 %collective-permute-start.48 = (bf16[256,512]{1,0:T(8,128)(2,1)}, bf16[256,512]{1,0:T(8,128)(2,1)}, u32[]{:S(2)}, u32[]{:S(2)}) collective-permute-start(bf16[256,512]{1,0:T(8,128)(2,1)} %fusion.10), channel_id=1, source_target_pairs={{0,3},{1,0},{2,1},{3,2},{4,7},{5,4},{6,5},{7,6},{8,11},{9,8},{10,9... | collective-permute-start | bytes 786440 | tf_op jit(solution)/shard_map/ppermute | solution.py:815
  355.7 17.2 %collective-permute-start.44 = (bf16[256,512]{1,0:T(8,128)(2,1)}, bf16[256,512]{1,0:T(8,128)(2,1)S(1)}, u32[]{:S(2)}, u32[]{:S(2)}) collective-permute-start(bf16[256,512]{1,0:T(8,128)(2,1)} %fusion.13), channel_id=1, source_target_pairs={{0,3},{1,0},{2,1},{3,2},{4,7},{5,4},{6,5},{7,6},{8,11},{9,8},{10,9... | collective-permute-start | bytes 786440 | tf_op jit(solution)/shard_map/ppermute | solution.py:815
  368.0 13.2 %collective-permute-start.53 = (bf16[256,512]{1,0:T(8,128)(2,1)S(1)}, bf16[256,512]{1,0:T(8,128)(2,1)S(1)}, u32[]{:S(2)}, u32[]{:S(2)}) collective-permute-start(bf16[256,512]{1,0:T(8,128)(2,1)S(1)} %fusion.6), channel_id=1, source_target_pairs={{0,3},{1,0},{2,1},{3,2},{4,7},{5,4},{6,5},{7,6},{8,11},{9,8},{10,9... | collective-permute-start | bytes 786440 | tf_op jit(solution)/shard_map/ppermute | solution.py:815
  (89 other events, 682.8 us)
Sparse Core Ops, SparseCore 0:
  21.8 45.3 all-gather.5
  190.3 45.1 all-gather.7
  281.6 45.1 all-gather.9
